TPU v7x, 32 devices: a whole 2x2x4 slice. The times are simulated.
32 devices in a mesh: section: 4 (over y, x), row: 8 (over z, core).
Axes of the slice: x: 2, y: 2, z: 4, core: 2. Of those that a mesh axis runs over, the one named last changes fastest.
Arguments:
- states: bfloat16 [4, 96, 768, 128], P('section', 'row'), may hold values from -6 to 6
- cotangent: bfloat16 [96, 768, 128], P('row'), may hold values from -6 to 6
- spec_weights: bfloat16 [64, 128, 2, 128, 128], P(None, 'row'), may hold values from -0.375 to 0.375
- local_weight: bfloat16 [128, 128], replicated, may hold values from -0.5 to 0.5
- bias: float32 [128], replicated, may hold values from -4 to 4
Outputs:
- grad_states: bfloat16 [4, 96, 768, 128], P('section', 'row')
- d_spectral: bfloat16 [64, 128, 2, 128, 128], P('section', 'row')
- d_local: float32 [128, 128], replicated
All inputs are finite; a program needn't handle non-finite values.
Results may differ from a plain program's by a relative error of at most 0.017.
Values may be sent and summed in bfloat16 or wider, within the bound.
No kernel may reach another device: no remote copies, remote signals or barrier semaphores. Data moves between devices by JAX's collectives and lax.ppermute only.
A program may use at most 384 MiB of HBM per device.

v0:
```python
import math

import jax
import jax.numpy as jnp
from jax import lax
from jax.sharding import PartitionSpec as P

GELU_SLOPE = math.sqrt(2.0 / math.pi)
GELU_CUBIC = 0.044715


def shifted(block, axis, distance):
    devices = range(lax.axis_size(axis))
    route = [(i - distance, i) for i in devices if i - distance in devices]
    return lax.ppermute(block, axis, route)


def gelu_derivative(values):
    inner_arg = GELU_SLOPE * (values + GELU_CUBIC * values * values * values)
    tangent = jnp.tanh(inner_arg)
    return 0.5 * (1.0 + tangent) + 0.5 * values * (1.0 - tangent * tangent) * GELU_SLOPE * (
        1.0 + 3.0 * GELU_CUBIC * values * values
    )


def lon_tables(mode_list, lon_cells):
    cell_ids = lax.iota(jnp.int32, lon_cells)
    phases = cell_ids[:, None] * mode_list[None, :] % lon_cells
    angles = phases.astype(jnp.float32) * (2.0 * math.pi / lon_cells)
    factor = 1.0 / math.sqrt(lon_cells)
    forward = jnp.stack([jnp.cos(angles), -jnp.sin(angles)], 2) * factor
    doubling = jnp.where(mode_list == 0, 1.0, 2.0).astype(jnp.float32)
    backward = jnp.transpose(forward, (1, 2, 0)) * doubling[:, None, None]
    return (
        forward.reshape(lon_cells, -1).astype(jnp.bfloat16),
        backward.reshape(-1, lon_cells).astype(jnp.bfloat16),
    )


def lat_tables(row_list, freq_count, lat_cells):
    freq_index = lax.iota(jnp.int32, freq_count)
    signed = jnp.where(freq_index < freq_count // 2, freq_index, freq_index - freq_count)
    phases = (signed % lat_cells)[:, None] * row_list[None, :] % lat_cells
    angles = phases.astype(jnp.float32) * (2.0 * math.pi / lat_cells)
    factor = 1.0 / math.sqrt(lat_cells)
    return (jnp.stack([jnp.cos(angles), jnp.sin(angles)], 0) * factor).astype(jnp.bfloat16)


def lat_forward(values, tables):
    lat_cells, mode_count, pair_width = values.shape
    channels = pair_width // 2
    freq_count = tables.shape[1]
    paired = jnp.dot(
        tables.reshape(2 * freq_count, lat_cells),
        values.reshape(lat_cells, mode_count * pair_width),
        preferred_element_type=jnp.float32,
    )
    paired = paired.reshape(2, freq_count, mode_count, 2, channels)
    real_part = paired[0, :, :, 0] + paired[1, :, :, 1]
    imag_part = paired[0, :, :, 1] - paired[1, :, :, 0]
    return jnp.stack([real_part, imag_part], 2).astype(jnp.bfloat16)


def lat_inverse(spectrum, tables):
    freq_count, mode_count, _, channels = spectrum.shape
    lat_cells = tables.shape[2]
    paired = jnp.einsum(
        "tjh,jx->thx", tables, spectrum.reshape(freq_count, -1), preferred_element_type=jnp.float32
    )
    paired = paired.reshape(2, lat_cells, mode_count, 2, channels)
    real_part = paired[0, :, :, 0] - paired[1, :, :, 1]
    imag_part = paired[0, :, :, 1] + paired[1, :, :, 0]
    return (
        jnp.stack([real_part, imag_part], 2)
        .reshape(lat_cells, mode_count, 2 * channels)
        .astype(jnp.bfloat16)
    )


def spectral(spectrum, weights):
    product = jnp.einsum("jkpi,jkqio->jkpqo", spectrum, weights, preferred_element_type=jnp.float32)
    real_part = product[:, :, 0, 0] - product[:, :, 1, 1]
    imag_part = product[:, :, 0, 1] + product[:, :, 1, 0]
    return jnp.stack([real_part, imag_part], 2).astype(jnp.bfloat16)


def spectral_adjoint(cotan_spec, weights):
    product = jnp.einsum(
        "jkqio,jkpo->jkqpi", weights, cotan_spec, preferred_element_type=jnp.float32
    )
    real_part = product[:, :, 0, 0] + product[:, :, 1, 1]
    imag_part = product[:, :, 0, 1] - product[:, :, 1, 0]
    return jnp.stack([real_part, imag_part], 2).astype(jnp.bfloat16)


def weight_gradient(coeff_steps, cotan_steps):
    product = jnp.einsum(
        "sjkpi,sjkqo->jkpqio", coeff_steps, cotan_steps, preferred_element_type=jnp.float32
    )
    real_part = product[:, :, 0, 0] + product[:, :, 1, 1]
    imag_part = product[:, :, 0, 1] - product[:, :, 1, 0]
    return jnp.stack([real_part, imag_part], 2).astype(jnp.bfloat16)


def forward_step(
    fields, weights, local_weight, bias, lon_basis, lon_synth, lat_basis, to_modes, to_rows
):
    row_count, lon_cells, channels = fields.shape
    mode_count = lon_basis.shape[1] // 2
    spectra = jnp.einsum(
        "hwc,wm->hmc", fields, lon_basis, preferred_element_type=jnp.float32
    ).astype(jnp.bfloat16)
    gathered = to_modes(spectra.reshape(row_count, mode_count, 2 * channels))
    coefficients = lat_forward(gathered, lat_basis)
    mixed = spectral(coefficients, weights)
    returned = to_rows(lat_inverse(mixed, lat_basis))
    smooth = jnp.einsum(
        "hmc,mw->hwc",
        returned.reshape(row_count, 2 * mode_count, channels),
        lon_synth,
        preferred_element_type=jnp.float32,
    )
    linear = jnp.dot(
        fields.reshape(-1, channels), local_weight, preferred_element_type=jnp.float32
    ).reshape(row_count, lon_cells, channels)
    return (smooth + linear + bias, coefficients)


def backward_step(
    fields,
    pre_act,
    carried,
    weights,
    local_weight,
    lon_basis,
    lon_synth,
    lat_basis,
    to_modes,
    to_rows,
):
    row_count, lon_cells, channels = fields.shape
    mode_count = lon_basis.shape[1] // 2
    slopes = carried.astype(jnp.float32) * gelu_derivative(pre_act)
    slopes_low = slopes.astype(jnp.bfloat16)
    spectra = jnp.einsum(
        "hwc,mw->hmc", slopes_low, lon_synth, preferred_element_type=jnp.float32
    ).astype(jnp.bfloat16)
    gathered = to_modes(spectra.reshape(row_count, mode_count, 2 * channels))
    coeff_cotan = lat_forward(gathered, lat_basis)
    inner_cotan = spectral_adjoint(coeff_cotan, weights)
    returned = to_rows(lat_inverse(inner_cotan, lat_basis))
    spread = jnp.einsum(
        "hmc,wm->hwc",
        returned.reshape(row_count, 2 * mode_count, channels),
        lon_basis,
        preferred_element_type=jnp.float32,
    )
    flat_slopes = slopes_low.reshape(-1, channels)
    linear = lax.dot_general(
        flat_slopes, local_weight, (((1,), (1,)), ((), ())), preferred_element_type=jnp.float32
    )
    gradient = (
        carried.astype(jnp.float32) + linear.reshape(row_count, lon_cells, channels) + spread
    ).astype(jnp.bfloat16)
    step_term = lax.dot_general(
        fields.reshape(-1, channels),
        flat_slopes,
        (((0,), (0,)), ((), ())),
        preferred_element_type=jnp.float32,
    )
    return (gradient, coeff_cotan, step_term)


def local(states, cotangent, spec_weights, local_weight, bias):
    sections = lax.axis_size("section")
    row_devs = lax.axis_size("row")
    section_id = lax.axis_index("section")
    channels = local_weight.shape[0]
    lon_cells = states.shape[2]
    rows_here = states.shape[1]
    freq_count = spec_weights.shape[0]
    row_modes = spec_weights.shape[1]
    mode_total = row_modes * row_devs
    lat_cells = rows_here * row_devs
    lon_basis, lon_synth = lon_tables(lax.iota(jnp.int32, mode_total), lon_cells)
    lat_basis = lat_tables(lax.iota(jnp.int32, lat_cells), freq_count, lat_cells)

    def to_modes(payload):
        return lax.all_to_all(payload, "row", split_axis=1, concat_axis=0, tiled=True)

    def to_rows(payload):
        return lax.all_to_all(payload, "row", split_axis=0, concat_axis=1, tiled=True)

    fields = states[0]
    pre_act, coefficients = forward_step(
        fields, spec_weights, local_weight, bias, lon_basis, lon_synth, lat_basis, to_modes, to_rows
    )
    carried = cotangent
    own_grad = jnp.zeros_like(cotangent)
    own_spec = jnp.zeros_like(coefficients)
    own_term = jnp.zeros((channels, channels), jnp.float32)
    for turn_no in range(sections):
        active = section_id == sections - 1 - turn_no
        gradient, coeff_cotan, step_term = backward_step(
            fields,
            pre_act,
            carried,
            spec_weights,
            local_weight,
            lon_basis,
            lon_synth,
            lat_basis,
            to_modes,
            to_rows,
        )
        own_grad = jnp.where(active, gradient, own_grad)
        own_spec = jnp.where(active, coeff_cotan, own_spec)
        own_term = jnp.where(active, step_term, own_term)
        if turn_no + 1 < sections:
            carried = shifted(gradient, "section", -1)
    grad_states = own_grad[None]
    step_coeffs, step_cotans = (
        lax.all_to_all(coefficients[None], "section", split_axis=1, concat_axis=0, tiled=True),
        lax.all_to_all(own_spec[None], "section", split_axis=1, concat_axis=0, tiled=True),
    )
    local_total = lax.psum(own_term, ("section", "row"))
    d_local = local_total * lax.rsqrt(jnp.float32(sections * lat_cells * lon_cells))
    d_spectral = weight_gradient(step_coeffs, step_cotans)
    return (grad_states, d_spectral, d_local)


def solution(mesh):
    return jax.shard_map(
        local,
        mesh=mesh,
        in_specs=(
            P("section", "row", None, None),
            P("row", None, None),
            P(None, "row", None, None, None),
            P(),
            P(),
        ),
        out_specs=(P("section", "row", None, None), P("section", "row", None, None, None), P()),
        check_vma=False,
    )
```

profile of v0, /device:TPU:0, one launch (start us, length us, event | category | flops | bytes accessed | tf_op | source)
XLA Modules:
  0.0 956.4 jit_solution(1411919714667423178)
XLA Ops:
  14.7 6.7 all-to-all-start
  21.7 26.3 %all-to-all-done = bf16[12,128,256]{2,0,1:T(8,128)(2,1)S(1)} async-done(((bf16[12,128,256]{2,0,1:T(8,128)(2,1)}), bf16[12,128,256]{2,0,1:T(8,128)(2,1)S(1)}, u32[]{:S(2)}, u32[]{:S(2)}) %all-to-all-start) | async-done | bytes 786464 | tf_op jit(solution)/shard_map/all_to_all | solution.py:189
  51.9 24.9 %fusion.111 = f32[64,16,2,2,128]{4,2,3,1,0:T(2,128)} fusion(bf16[64,16,2,128,128]{4,3,2,1,0:T(8,128)(2,1)} %param.7, bf16[64,16,2,128,1]{3,0,1,2,4:T(8,128)(2,1)S(1)} %maximum_bitcast_fusion), kind=kOutput, calls=%fused_computation.195 | convolution fusion | flops 134217728 | bytes 69730304 | tf_op jit(solution)/shard_map/jkpi,jkqio->jkpqo/dot_general | solution.py:81
  76.8 3.6 fusion.92
  84.9 16.1 %all-to-all-start.1 = ((bf16[96,16,256]{2,1,0:T(8,128)(2,1)}), bf16[96,16,256]{2,1,0:T(8,128)(2,1)}, u32[]{:S(2)}, u32[]{:S(2)}) async-start(bf16[96,16,256]{2,1,0:T(8,128)(2,1)} %convert_element_type.248), calls=%async_computation.1 | async-start | bytes 1572864 | tf_op jit(solution)/shard_map/all_to_all | solution.py:192
  104.2 17.5 %all-to-all-done.1 = bf16[96,16,256]{2,1,0:T(8,128)(2,1)} async-done(((bf16[96,16,256]{2,1,0:T(8,128)(2,1)}), bf16[96,16,256]{2,1,0:T(8,128)(2,1)}, u32[]{:S(2)}, u32[]{:S(2)}) %all-to-all-start.1) | async-done | bytes 786464 | tf_op jit(solution)/shard_map/all_to_all | solution.py:192
  121.7 2.1 copy.423
  127.2 5.2 fusion.5
  137.3 29.0 %all_to_all.174 = bf16[12,128,256]{2,0,1:T(8,128)(2,1)S(1)} all-to-all(bf16[12,128,256]{2,0,1:T(8,128)(2,1)S(1)} %copy.425), channel_id=1, replica_groups=mesh['section'=4,'row'=8] {'row'}, dimensions={1} | all-to-all | bytes 1572864 | tf_op jit(solution)/shard_map/all_to_all | solution.py:189
  170.3 26.7 %convolution_bitcast_fusion.4 = f32[64,16,2,2,128]{4,3,2,1,0:T(2,128)} fusion(bf16[64,16,2,128,128]{4,3,2,1,0:T(8,128)(2,1)} %param.7, bf16[64,16,2,128,1]{3,0,1,2,4:T(8,128)(2,1)S(1)} %maximum_bitcast_fusion.1), kind=kOutput, calls=%fused_computation.48 | convolution fusion | flops 134217728 | bytes 69730304 | tf_op jit(solution)/shard_map/jkqio,jkpo->jkqpi/dot_general | solution.py:88
  197.0 3.6 fusion.88
  204.6 3.1 convert_element_type.253
  207.8 4.2 all-to-all-start.3
  212.2 4.6 fusion.151
  216.8 16.2 %all-to-all-done.3 = bf16[96,16,256]{2,1,0:T(8,128)(2,1)} async-done(((bf16[96,16,256]{2,1,0:T(8,128)(2,1)}), bf16[96,16,256]{2,1,0:T(8,128)(2,1)}, u32[]{:S(2)}, u32[]{:S(2)}) %all-to-all-start.3) | async-done | bytes 786464 | tf_op jit(solution)/shard_map/all_to_all | solution.py:192
  233.0 2.1 copy.435
  235.1 2.2 reshape.1076
  237.3 4.3 fusion.7
  243.3 53.0 %collective-permute-done = bf16[12,768,128]{2,1,0:T(8,128)(2,1)S(1)} collective-permute-done((bf16[12,768,128]{2,1,0:T(8,128)(2,1)S(1)}, bf16[12,768,128]{2,1,0:T(8,128)(2,1)S(1)}, u32[]{:S(2)}, u32[]{:S(2)}) %collective-permute-start) | collective-permute-done | bytes 2359328 | tf_op jit(solution)/shard_map/ppermute | solution.py:15
  300.7 2.1 reshape.1077
  304.4 29.3 %all_to_all.175 = bf16[12,128,256]{2,0,1:T(8,128)(2,1)S(1)} all-to-all(bf16[12,128,256]{2,0,1:T(8,128)(2,1)S(1)} %copy.437), channel_id=1, replica_groups=mesh['section'=4,'row'=8] {'row'}, dimensions={1} | all-to-all | bytes 1572864 | tf_op jit(solution)/shard_map/all_to_all | solution.py:189
  335.2 3.2 dot_general.168
  341.6 26.6 %convolution_bitcast_fusion.3 = f32[64,16,2,2,128]{4,3,2,1,0:T(2,128)} fusion(bf16[64,16,2,128,128]{4,3,2,1,0:T(8,128)(2,1)} %param.7, bf16[64,16,2,128,1]{3,0,1,2,4:T(8,128)(2,1)S(1)} %maximum_bitcast_fusion.2), kind=kOutput, calls=%fused_computation.47 | convolution fusion | flops 134217728 | bytes 69730304 | tf_op jit(solution)/shard_map/jkqio,jkpo->jkqpi/dot_general | solution.py:88
  368.2 3.5 fusion.83
  377.6 3.1 convert_element_type.260
  380.7 24.6 %all_to_all.176 = bf16[96,16,256]{2,1,0:T(8,128)(2,1)S(1)} all-to-all(bf16[96,16,256]{2,1,0:T(8,128)(2,1)} %convert_element_type.260), channel_id=1, replica_groups=mesh['section'=4,'row'=8] {'row'}, dimensions={0} | all-to-all | bytes 1572864 | tf_op jit(solution)/shard_map/all_to_all | solution.py:192
  406.3 2.1 reshape.1079
  410.5 2.6 fusion.10
  414.6 53.9 %collective-permute-done.1 = bf16[12,768,128]{2,1,0:T(8,128)(2,1)S(1)} collective-permute-done((bf16[12,768,128]{2,1,0:T(8,128)(2,1)S(1)}, bf16[12,768,128]{2,1,0:T(8,128)(2,1)S(1)}, u32[]{:S(2)}, u32[]{:S(2)}) %collective-permute-start.1) | collective-permute-done | bytes 2359328 | tf_op jit(solution)/shard_map/ppermute | solution.py:15
  473.0 2.1 reshape.1080
  476.6 29.5 %all_to_all.177 = bf16[12,128,256]{2,0,1:T(8,128)(2,1)S(1)} all-to-all(bf16[12,128,256]{2,0,1:T(8,128)(2,1)S(1)} %copy.451), channel_id=1, replica_groups=mesh['section'=4,'row'=8] {'row'}, dimensions={1} | all-to-all | bytes 1572864 | tf_op jit(solution)/shard_map/all_to_all | solution.py:189
  507.6 3.2 dot_general.178
  513.9 26.6 %convolution_bitcast_fusion.2 = f32[64,16,2,2,128]{4,3,2,1,0:T(2,128)} fusion(bf16[64,16,2,128,128]{4,3,2,1,0:T(8,128)(2,1)} %param.7, bf16[64,16,2,128,1]{3,0,1,2,4:T(8,128)(2,1)S(1)} %maximum_bitcast_fusion.3), kind=kOutput, calls=%fused_computation.46 | convolution fusion | flops 134217728 | bytes 69730304 | tf_op jit(solution)/shard_map/jkqio,jkpo->jkqpi/dot_general | solution.py:88
  540.5 3.6 fusion.78
  550.0 3.1 convert_element_type.267
  553.1 24.6 %all_to_all.178 = bf16[96,16,256]{2,1,0:T(8,128)(2,1)S(1)} all-to-all(bf16[96,16,256]{2,1,0:T(8,128)(2,1)} %convert_element_type.267), channel_id=1, replica_groups=mesh['section'=4,'row'=8] {'row'}, dimensions={0} | all-to-all | bytes 1572864 | tf_op jit(solution)/shard_map/all_to_all | solution.py:192
  578.8 2.1 reshape.1082
  583.5 2.1 fusion.13
  589.5 2.6 convolution_select_fusion
  595.3 46.1 %collective-permute-done.2 = bf16[12,768,128]{2,1,0:T(8,128)(2,1)} collective-permute-done((bf16[12,768,128]{2,1,0:T(8,128)(2,1)}, bf16[12,768,128]{2,1,0:T(8,128)(2,1)}, u32[]{:S(2)}, u32[]{:S(2)}) %collective-permute-start.2) | collective-permute-done | bytes 2359328 | tf_op jit(solution)/shard_map/ppermute | solution.py:15
  641.3 2.3 fusion.14
  646.7 2.2 reshape.1083
  648.8 2.6 copy.465
  651.4 4.3 all-to-all-start.8
  655.7 2.6 convolution_select_fusion.2
  662.6 124.3 %all-reduce.2.cloned.1.call-done = f32[128,128]{0,1:T(8,128)} async-done(((f32[128,128]{0,1:T(8,128)}), f32[128,128]{0,1:T(8,128)}) %all-reduce.2.cloned.1.call-update) | async-done | bytes 65552 | tf_op jit(solution)/shard_map/psum | solution.py:226
  788.5 4.0 all-to-all-start.11
  795.1 3.3 dot_general.188
  803.7 26.8 %convolution_bitcast_fusion.1 = f32[64,16,2,2,128]{4,3,2,1,0:T(2,128)} fusion(bf16[64,16,2,128,128]{4,3,2,1,0:T(8,128)(2,1)} %param.7, bf16[64,16,2,128,1]{3,0,1,2,4:T(8,128)(2,1)} %maximum_bitcast_fusion.4), kind=kOutput, calls=%fused_computation.45 | convolution fusion | flops 134217728 | bytes 69730304 | tf_op jit(solution)/shard_map/jkqio,jkpo->jkqpi/dot_general | solution.py:88
  830.5 3.6 fusion.73
  835.6 2.2 convert_element_type.273
  837.8 2.2 dot_general.192
  840.1 3.3 fusion.97
  843.4 4.2 all-to-all-start.10
  852.2 3.1 convert_element_type.274
  856.7 4.4 all-to-all-start.9
  861.1 24.2 %convolution_bitcast_fusion = f32[16,16,2,2,128,128]{4,5,2,3,1,0:T(8,128)} fusion(bf16[4,16,16,2,128,1]{4,3,2,1,0,5:T(2,128)(2,1)S(1)} %bitcast.519, bf16[4,16,16,2,128,1]{4,3,2,1,0,5:T(2,128)(2,1)} %bitcast.100), kind=kOutput, calls=%fused_computation | convolution fusion | flops 134217728 | bytes 68157440 | tf_op jit(solution)/shard_map/sjkpi,sjkqo->jkpqio/dot_general | solution.py:97
  885.4 11.8 %fusion.4 = bf16[16,16,1,128,128]{3,4,1,0,2:T(8,128)(2,1)S(1)} fusion(f32[16,16,2,2,128,128]{4,5,2,3,1,0:T(8,128)} %convolution_bitcast_fusion), kind=kLoop, calls=%fused_computation.9 | loop fusion | flops 8388608 | bytes 41943040 | tf_op jit(solution)/shard_map/sub | solution.py:101
  897.2 11.8 %fusion.3 = bf16[16,16,1,128,128]{3,4,1,0,2:T(8,128)(2,1)S(1)} fusion(f32[16,16,2,2,128,128]{4,5,2,3,1,0:T(8,128)} %convolution_bitcast_fusion), kind=kLoop, calls=%fused_computation.8 | loop fusion | flops 8388608 | bytes 41943040 | tf_op jit(solution)/shard_map/add | solution.py:100
  909.0 6.7 pad_maximum_fusion
  915.7 21.6 %copy.490 = bf16[16,16,2,128,128]{4,3,2,1,0:T(8,128)(2,1)} copy(bf16[16,16,2,128,128]{3,4,1,0,2:T(8,128)(2,1)} %pad_maximum_fusion) | data formatting | bytes 33554432
  937.3 2.1 copy.477
  939.5 2.1 reshape.1085
  944.9 4.4 fusion.24
  (233 shorter events, 112.7 us)
Async XLA Ops:
  7.2 3.1 copy-start
  10.1 1.8 copy-start.21
  14.7 33.3 %all-to-all-start = ((bf16[12,128,256]{2,0,1:T(8,128)(2,1)}), bf16[12,128,256]{2,0,1:T(8,128)(2,1)S(1)}, u32[]{:S(2)}, u32[]{:S(2)}) async-start(bf16[12,128,256]{2,0,1:T(8,128)(2,1)} %copy.413), calls=%async_computation | async-start | bytes 2097152 | tf_op jit(solution)/shard_map/all_to_all | solution.py:189
  51.8 25.0 %copy-start.27 = (bf16[1,64,16,1,128]{4,1,3,2,0:T(8,128)(2,1)}, bf16[1,64,16,1,128]{4,1,3,2,0:T(8,128)(2,1)S(1)}, u32[]{:S(2)}) copy-start(bf16[1,64,16,1,128]{4,1,3,2,0:T(8,128)(2,1)S(1)} %get-tuple-element.36) | copy-start | bytes 786436
  51.8 25.0 %copy-start.28 = (bf16[1,64,16,1,128]{4,1,3,2,0:T(8,128)(2,1)}, bf16[1,64,16,1,128]{4,1,3,2,0:T(8,128)(2,1)S(1)}, u32[]{:S(2)}) copy-start(bf16[1,64,16,1,128]{4,1,3,2,0:T(8,128)(2,1)S(1)} %get-tuple-element.37) | copy-start | bytes 786436
  84.9 36.8 %all-to-all-start.1 = ((bf16[96,16,256]{2,1,0:T(8,128)(2,1)}), bf16[96,16,256]{2,1,0:T(8,128)(2,1)}, u32[]{:S(2)}, u32[]{:S(2)}) async-start(bf16[96,16,256]{2,1,0:T(8,128)(2,1)} %convert_element_type.248), calls=%async_computation.1 | async-start | bytes 1572864 | tf_op jit(solution)/shard_map/all_to_all | solution.py:192
  125.1 2.0 copy-start.29
  125.2 2.0 copy-start.34
  125.2 2.0 copy-start.39
  127.2 6.6 copy-start.35
  132.4 1.4 copy-start.17
  170.2 26.8 %copy-start.23 = (bf16[1,64,16,1,128]{4,1,3,2,0:T(8,128)(2,1)}, bf16[1,64,16,1,128]{4,1,3,2,0:T(8,128)(2,1)S(1)}, u32[]{:S(2)}) copy-start(bf16[1,64,16,1,128]{4,1,3,2,0:T(8,128)(2,1)S(1)} %get-tuple-element.32) | copy-start | bytes 786436
  170.2 26.8 %copy-start.25 = (bf16[1,64,16,1,128]{4,1,3,2,0:T(8,128)(2,1)}, bf16[1,64,16,1,128]{4,1,3,2,0:T(8,128)(2,1)S(1)}, u32[]{:S(2)}) copy-start(bf16[1,64,16,1,128]{4,1,3,2,0:T(8,128)(2,1)S(1)} %get-tuple-element.33) | copy-start | bytes 786436
  202.9 9.1 copy-start.22
  207.8 25.2 %all-to-all-start.3 = ((bf16[96,16,256]{2,1,0:T(8,128)(2,1)}), bf16[96,16,256]{2,1,0:T(8,128)(2,1)}, u32[]{:S(2)}, u32[]{:S(2)}) async-start(bf16[96,16,256]{2,1,0:T(8,128)(2,1)} %convert_element_type.253), calls=%async_computation.3 | async-start | bytes 1572864 | tf_op jit(solution)/shard_map/all_to_all | solution.py:192
  235.1 61.2 %slice-start = ((s8[4718592]{0:T(1024)(128)(4,1)}), s8[524288]{0:T(1024)(128)(4,1)S(1)}, s32[]{:S(2)}) async-start(s8[4718592]{0:T(1024)(128)(4,1)} %bitcast.493), calls=%async_computation.13 | async-start | bytes 1048576
  237.3 59.0 %slice-start.1 = ((s8[4718592]{0:T(1024)(128)(4,1)}), s8[4194304]{0:T(1024)(128)(4,1)S(1)}, s32[]{:S(2)}) async-start(s8[4718592]{0:T(1024)(128)(4,1)} %bitcast.493), calls=%async_computation.14 | async-start | bytes 8388608
  241.6 54.7 %copy-start.13 = (bf16[12,768,128]{2,1,0:T(8,128)(2,1)}, bf16[12,768,128]{2,1,0:T(8,128)(2,1)S(1)}, u32[]{:S(2)}) copy-start(bf16[12,768,128]{2,1,0:T(8,128)(2,1)S(1)} %fusion.7) | copy-start | bytes 7077892
  241.6 54.7 %collective-permute-start = (bf16[12,768,128]{2,1,0:T(8,128)(2,1)S(1)}, bf16[12,768,128]{2,1,0:T(8,128)(2,1)S(1)}, u32[]{:S(2)}, u32[]{:S(2)}) collective-permute-start(bf16[12,768,128]{2,1,0:T(8,128)(2,1)S(1)} %fusion.7), channel_id=1, source_target_pairs={{8,0},{16,8},{24,16},{9,1},{17,9},{25,17},{10,2},{18,10},{26,18},{... | collective-permute-start | bytes 7077896 | tf_op jit(solution)/shard_map/ppermute | solution.py:15
  296.3 1.4 copy-start.18
  296.3 2.8 copy-start.36
  297.7 1.4 copy-start.4
  340.1 1.4 copy-start.9
  408.4 2.1 copy-start.5
  408.4 60.0 %slice-start.2 = ((s8[4718592]{0:T(1024)(128)(4,1)}), s8[4194304]{0:T(1024)(128)(4,1)S(1)}, s32[]{:S(2)}) async-start(s8[4718592]{0:T(1024)(128)(4,1)} %bitcast.495), calls=%async_computation.15 | async-start | bytes 8388608
  410.5 57.9 %slice-start.3 = ((s8[4718592]{0:T(1024)(128)(4,1)}), s8[524288]{0:T(1024)(128)(4,1)S(1)}, s32[]{:S(2)}) async-start(s8[4718592]{0:T(1024)(128)(4,1)} %bitcast.495), calls=%async_computation.16 | async-start | bytes 1048576
  413.1 55.9 %copy-start.15 = (bf16[12,768,128]{2,1,0:T(8,128)(2,1)}, bf16[12,768,128]{2,1,0:T(8,128)(2,1)S(1)}, u32[]{:S(2)}) copy-start(bf16[12,768,128]{2,1,0:T(8,128)(2,1)S(1)} %fusion.10) | copy-start | bytes 7077892
  413.1 58.1 %copy-start.37 = (bf16[256,768,1]{1,0,2:T(8,128)(2,1)S(1)}, bf16[256,768,1]{1,0,2:T(8,128)(2,1)}, u32[]{:S(2)}) copy-start(bf16[256,768,1]{1,0,2:T(8,128)(2,1)} %reshape.1097) | copy-start | bytes 1179652
  413.2 55.3 %collective-permute-start.1 = (bf16[12,768,128]{2,1,0:T(8,128)(2,1)S(1)}, bf16[12,768,128]{2,1,0:T(8,128)(2,1)S(1)}, u32[]{:S(2)}, u32[]{:S(2)}) collective-permute-start(bf16[12,768,128]{2,1,0:T(8,128)(2,1)S(1)} %fusion.10), channel_id=1, source_target_pairs={{8,0},{16,8},{24,16},{9,1},{17,9},{25,17},{10,2},{18,10},{26,18},{... | collective-permute-start | bytes 7077896 | tf_op jit(solution)/shard_map/ppermute | solution.py:15
  468.5 1.4 copy-start.19
  469.9 1.4 copy-start.7
  512.4 1.3 copy-start.11
  580.9 2.1 copy-start.8
  580.9 2.6 copy-start.20
  583.5 57.9 %slice-start.4 = ((s8[4718592]{0:T(1024)(128)(4,1)}), s8[524288]{0:T(1024)(128)(4,1)S(1)}, s32[]{:S(2)}) async-start(s8[4718592]{0:T(1024)(128)(4,1)} %bitcast.497), calls=%async_computation.17 | async-start | bytes 1048576
  585.6 55.7 %collective-permute-start.2 = (bf16[12,768,128]{2,1,0:T(8,128)(2,1)}, bf16[12,768,128]{2,1,0:T(8,128)(2,1)}, u32[]{:S(2)}, u32[]{:S(2)}) collective-permute-start(bf16[12,768,128]{2,1,0:T(8,128)(2,1)} %fusion.13), channel_id=1, source_target_pairs={{8,0},{16,8},{24,16},{9,1},{17,9},{25,17},{10,2},{18,10},{26,18},{... | collective-permute-start | bytes 7077896 | tf_op jit(solution)/shard_map/ppermute | solution.py:15
  586.9 5.2 copy-start.6
  588.2 53.2 %slice-start.5 = ((s8[4718592]{0:T(1024)(128)(4,1)}), s8[4194304]{0:T(1024)(128)(4,1)S(1)}, s32[]{:S(2)}) async-start(s8[4718592]{0:T(1024)(128)(4,1)} %bitcast.497), calls=%async_computation.18 | async-start | bytes 8388608
  592.1 1.6 copy-start.10
  595.3 49.7 %copy-start.38 = (bf16[256,768,1]{1,0,2:T(8,128)(2,1)S(1)}, bf16[256,768,1]{1,0,2:T(8,128)(2,1)}, u32[]{:S(2)}) copy-start(bf16[256,768,1]{1,0,2:T(8,128)(2,1)} %reshape.1097) | copy-start | bytes 1179652
  643.6 1.4 copy-start.1
  651.4 137.1 %all-to-all-start.8 = ((bf16[12,128,256]{2,0,1:T(8,128)(2,1)}), bf16[12,128,256]{2,0,1:T(8,128)(2,1)}, u32[]{:S(2)}, u32[]{:S(2)}) async-start(bf16[12,128,256]{2,0,1:T(8,128)(2,1)} %copy.465), calls=%async_computation.8 | async-start | bytes 2097152 | tf_op jit(solution)/shard_map/all_to_all | solution.py:189
  655.6 131.3 %all-reduce.2.cloned.1.call-start = ((), (), s32[]{:S(2)}) async-start(), calls=%async_computation.12 | async-start | bytes 131072 | tf_op jit(solution)/shard_map/psum | solution.py:226
  655.7 2.7 copy-start.12
  655.7 3.4 copy-start.2
  788.5 54.9 %all-to-all-start.11 = ((bf16[1,64,16,2,128]{4,3,2,0,1:T(2,128)(2,1)}), bf16[1,64,16,2,128]{4,3,2,0,1:T(2,128)(2,1)S(1)}, u32[]{:S(2)}, u32[]{:S(2)}) async-start(bf16[1,64,16,2,128]{4,3,2,0,1:T(2,128)(2,1)} %copy.484), calls=%async_computation.11 | async-start | bytes 1048576 | tf_op jit(solution)/shard_map/all_to_all | solution.py:223
  800.0 1.0 copy-start.24
  800.0 1.0 copy-start.26
  800.0 1.1 copy-start.30
  800.0 1.2 copy-start.31
  800.0 1.2 copy-start.32
  800.0 1.3 copy-start.33
  843.4 13.4 %all-to-all-start.10 = ((bf16[1,64,16,2,128]{4,3,2,0,1:T(2,128)(2,1)}), bf16[1,64,16,2,128]{4,3,2,0,1:T(2,128)(2,1)}, u32[]{:S(2)}, u32[]{:S(2)}) async-start(bf16[1,64,16,2,128]{4,3,2,0,1:T(2,128)(2,1)} %copy.482), calls=%async_computation.10 | async-start | bytes 1048576 | tf_op jit(solution)/shard_map/all_to_all | solution.py:224
  856.7 80.6 %all-to-all-start.9 = ((bf16[96,16,256]{2,1,0:T(8,128)(2,1)}), bf16[96,16,256]{2,1,0:T(8,128)(2,1)}, u32[]{:S(2)}, u32[]{:S(2)}) async-start(bf16[96,16,256]{2,1,0:T(8,128)(2,1)} %convert_element_type.274), calls=%async_computation.9 | async-start | bytes 1572864 | tf_op jit(solution)/shard_map/all_to_all | solution.py:192
  941.6 2.1 copy-start.3
  941.6 2.6 copy-start.14
  941.6 3.3 copy-start.16
Sparse Core Ops, SparseCore 0:
  662.6 124.2 all-reduce.1
where the time goes:
time: 957 us; the launch traced here: 956 us
  waiting for transfers between devices  339 us (35%)
  matrix products  217 us (23%)
  blocking collectives  137 us (14%)
  local copies, waits for them, and re-layouts  133 us (14%)
  other arithmetic  67.3 us (7%)
  starting transfers between devices  48.3 us (5%)
  between operations  15.4 us (2%)
    ppermute x3, waiting for transfers between devices, shifted(): return lax.ppermute(block, axis, route)  153 us
    psum x1, waiting for transfers between devices, local(): local_total = lax.psum(own_term, ('section', 'row'))  124 us
    dot_general x4, matrix products, spectral_adjoint(): jnp.einsum('jkqio,jkpo->jkqpi', weights, cotan_spec, preferred_element_ty...  107 us
    all_to_all x3, blocking collectives, to_modes(): lax.all_to_all(payload, 'row', split_axis=1, concat_axis=0, tiled=True)  87.9 us
    all_to_all x2, blocking collectives, to_rows(): lax.all_to_all(payload, 'row', split_axis=0, concat_axis=1, tiled=True)  49.2 us
    unnamed x109, local copies, waits for them, and re-layouts  40.1 us
    all_to_all x3, waiting for transfers between devices, to_rows(): lax.all_to_all(payload, 'row', split_axis=0, concat_axis=1, tiled=True)  33.7 us
    all_to_all x2, waiting for transfers between devices, to_modes(): lax.all_to_all(payload, 'row', split_axis=1, concat_axis=0, tiled=True)  26.3 us
  transfers between devices with their start and end apart: 11, of which 8 were waited for; matrix products, arithmetic and copies ran while one was open for 17% of the time, Pallas kernels for 0%

commit v1 on v0

v1 whole, which is shorter than its diff:
```python
import functools
import math

import jax
import jax.numpy as jnp
import numpy as np
from jax import lax
from jax.experimental import pallas as pl
from jax.experimental.pallas import tpu as pltpu
from jax.sharding import PartitionSpec as P

GELU_SLOPE = math.sqrt(2.0 / math.pi)
GELU_CUBIC = 0.044715
BF16 = jnp.bfloat16
F32 = jnp.float32
ALL = ("section", "row")
VMEM_LIMIT = 56 * 1024 * 1024


def gelu_derivative(values):
    square = values * values
    inner_arg = GELU_SLOPE * values * (1.0 + GELU_CUBIC * square)
    tangent = jnp.tanh(inner_arg)
    return 0.5 * (1.0 + tangent) + (0.5 * GELU_SLOPE) * values * (1.0 - tangent * tangent) * (
        1.0 + 3.0 * GELU_CUBIC * square
    )


def lon_tables(mode_list, lon_cells):
    phases = np.arange(lon_cells)[:, None] * mode_list[None, :] % lon_cells
    angles = phases * (2.0 * math.pi / lon_cells)
    factor = 1.0 / math.sqrt(lon_cells)
    forward = np.stack([np.cos(angles), -np.sin(angles)], 2) * factor
    doubling = np.where(mode_list == 0, 1.0, 2.0)
    backward = np.transpose(forward, (1, 2, 0)) * doubling[:, None, None]
    return (
        forward.reshape(lon_cells, -1).astype(np.float32),
        backward.reshape(-1, lon_cells).astype(np.float32),
    )


def lat_matrices(row_list, freq_count, lat_cells, modes):
    freq = np.arange(freq_count)
    signed = np.where(freq < freq_count // 2, freq, freq - freq_count)
    angles = ((signed % lat_cells)[:, None] * row_list[None, :] % lat_cells) * (
        2.0 * math.pi / lat_cells
    )
    factor = 1.0 / math.sqrt(lat_cells)
    cos, sin = np.cos(angles) * factor, np.sin(angles) * factor
    same = np.eye(modes)
    rot = np.array([[[1.0, 0.0], [0.0, 1.0]], [[0.0, 1.0], [-1.0, 0.0]]])
    block = cos[:, None, None, :, None, None] * same[None, :, None, None, :, None] * rot[0][
        None, None, :, None, None, :
    ] + sin[:, None, None, :, None, None] * same[None, :, None, None, :, None] * rot[1][
        None, None, :, None, None, :
    ]
    return block.reshape(freq_count * modes * 2, row_list.size * modes * 2).astype(np.float32)


def dot(a, b, contract=((1,), (0,))):
    return lax.dot_general(a, b, (contract, ((), ())), preferred_element_type=F32)


def unpack_rows(values, rows, packed):
    channels = values.shape[-1]
    if packed:
        devices, per_dev, _ = values.shape
        wide = values.astype(F32).reshape(devices, per_dev // 8, 8, channels)
        parts = [wide[:, r].reshape(devices * 8, channels) for r in rows]
    else:
        parts = [values[r].astype(F32) for r in rows]
    return jnp.concatenate(parts, axis=1).astype(BF16)


def pack_rows(spec, row_count, packed, devices):
    channels = spec.shape[1] // row_count
    parts = [spec[:, r * channels : (r + 1) * channels] for r in range(row_count)]
    if packed:
        parts = [p.reshape(devices, 8, channels) for p in parts]
        return jnp.concatenate(parts, axis=1).astype(BF16)
    return jnp.stack(parts, 0).astype(BF16)


def outer_pack(spec, devices):
    rows, total, channels = spec.shape
    per = total // devices
    return spec.reshape(rows, devices, per, channels).transpose(1, 0, 2, 3).reshape(
        devices, rows * per, channels
    )


def outer_unpack(received, row_count):
    devices, total, channels = received.shape
    per = total // row_count
    return received.reshape(devices, row_count, per, channels).transpose(1, 0, 2, 3).reshape(
        row_count, devices * per, channels
    )


def spectra_kernel(rows_at_once, packed, devices, fields_ref, basis_ref, out_ref):
    basis = basis_ref[...]
    row_count = fields_ref.shape[0]
    for first in range(0, row_count, rows_at_once):
        field = jnp.concatenate([fields_ref[first + r] for r in range(rows_at_once)], axis=1)
        spec = pack_rows(dot(basis, field), rows_at_once, packed, devices)
        if packed:
            out_ref[:, first * 8 : (first + rows_at_once) * 8, :] = spec
        else:
            out_ref[first : first + rows_at_once] = spec


def spread_pairs(values, per_group, sign):
    rows, _ = values.shape
    ids = lax.broadcasted_iota(jnp.int32, values.shape, 0)
    after = pltpu.roll(values, rows - 1, 0)
    before = pltpu.roll(values, 1, 0)
    turned = jnp.where(ids % 2 == 0, sign * after, -sign * before)
    pair = (ids // 2) % per_group
    parts = []
    for t in range(per_group):
        parts.append(jnp.where(pair == t, values, 0.0).astype(BF16))
        parts.append(jnp.where(pair == t, turned, 0.0).astype(BF16))
    return parts


def mix_kernel(steps, sec_ref, x_ref, lat_ref, inv_ref, w_ref, coeff_ref, out_ref, lhs_ref, z_ref):
    turn = pl.program_id(0)
    channels = x_ref.shape[-1]
    span = x_ref.shape[0] // steps
    total = lat_ref.shape[0]
    groups = total // 8

    @pl.when(turn == 0)
    def _():
        lat = lat_ref[...]
        found = []
        for s in range(steps):
            value = dot(lat, x_ref[s * span : (s + 1) * span, :]).astype(BF16)
            coeff_ref[s] = value
            found.append(value.astype(F32).reshape(groups, 8, channels))
        tall = jnp.concatenate(found, axis=1).reshape(groups * steps * 8, channels)
        for n, part in enumerate(spread_pairs_steps(tall, steps)):
            lhs_ref[:, n * channels : (n + 1) * channels] = part

    pairs = w_ref.shape[0] * w_ref.shape[1]
    here = pairs // 4
    weights = w_ref[...].reshape(here, 8 * channels, channels)
    for g in range(here):
        at = pl.multiple_of((turn * here + g) * (8 * steps), 8 * steps)
        mixed = dot(lhs_ref[pl.ds(at, 8 * steps), :], weights[g])
        to = pl.multiple_of((turn * here + g) * 8, 8)
        for s in range(steps):
            z_ref[s, pl.ds(to, 8), :] = mixed[s * 8 : (s + 1) * 8]

    @pl.when(turn == pl.num_programs(0) - 1)
    def _():
        inv = inv_ref[...]
        for s in range(steps):
            out_ref[s] = dot(inv, z_ref[s].astype(BF16)).astype(BF16)


def spread_pairs_steps(values, steps):
    return spread_pairs(values, 4, -1.0)


def adjoint_kernel(sec_ref, x_ref, lat_ref, inv_ref, w_ref, coeff_ref, out_ref, lhs_ref, z_ref):
    turn = pl.program_id(0)
    channels = x_ref.shape[-1]

    @pl.when(turn == 0)
    def _():
        value = dot(lat_ref[...], x_ref[...]).astype(BF16)
        coeff_ref[...] = value
        for n, part in enumerate(spread_pairs(value.astype(F32), 8, 1.0)):
            lhs_ref[:, n * channels : (n + 1) * channels] = part

    pairs = w_ref.shape[0] * w_ref.shape[1]
    here = pairs // 8
    weights = w_ref[...].reshape(here, 8, 2, channels, channels)
    for g in range(here):
        at = pl.multiple_of((turn * here + g) * 16, 16)
        mixed = jnp.zeros((16, channels), F32)
        for t in range(8):
            left = lhs_ref[pl.ds(at, 16), 2 * t * channels : (2 * t + 2) * channels]
            right = jnp.concatenate([weights[g, t, 0], weights[g, t, 1]], axis=1)
            mixed = mixed + dot(left, right, ((1,), (1,)))
        z_ref[pl.ds(at, 16), :] = mixed

    @pl.when(turn == pl.num_programs(0) - 1)
    def _():
        out_ref[...] = dot(inv_ref[...], z_ref[...].astype(BF16)).astype(BF16)


def slope_kernel(
    step, rows, packed, sec_ref, recv_ref, state_ref, synth_ref, mix_ref, bias_ref, out_ref
):
    channels = mix_ref.shape[0]
    cells = state_ref.shape[2]
    modes = unpack_rows(recv_ref[...], range(step * rows, (step + 1) * rows), packed)
    mixing = mix_ref[...]
    bias = bias_ref[...]
    tile = 256
    for w in range(0, cells, tile):
        smooth = dot(synth_ref[w : w + tile, :], modes)
        for r in range(rows):
            linear = dot(state_ref[0, r, w : w + tile, :], mixing)
            pre = smooth[:, r * channels : (r + 1) * channels] + linear + bias
            out_ref[r, w : w + tile, :] = gelu_derivative(pre)


def finish_tile(
    r, w, tile, carried, slope_ref, state_ref, low_ref
):
    low = (carried.astype(F32) * slope_ref[r, w : w + tile, :]).astype(BF16)
    low_ref[r, w : w + tile, :] = low
    term = dot(state_ref[0, r, w : w + tile, :], low, ((0,), (0,)))
    return low, term


def start_kernel(
    packed, devices, sec_ref, cot_ref, slope_ref, state_ref, synth_ref, low_ref, send_ref, acc_ref
):
    rows, cells, channels = cot_ref.shape
    tile = 256
    spec, acc = None, None
    for w in range(0, cells, tile):
        lows = []
        for r in range(rows):
            low, term = finish_tile(
                r, w, tile, cot_ref[r, w : w + tile, :], slope_ref, state_ref, low_ref
            )
            lows.append(low)
            acc = term if acc is None else acc + term
        part = dot(synth_ref[:, w : w + tile], jnp.concatenate(lows, axis=1))
        spec = part if spec is None else spec + part
    acc_ref[...] = acc
    send_ref[...] = pack_rows(spec, rows, packed, devices)


def gradient_tile(r, w, tile, spread, carried_ref, low_ref, mixing):
    channels = mixing.shape[0]
    linear = dot(low_ref[r, w : w + tile, :], mixing, ((1,), (1,)))
    total = (
        carried_ref[r, w : w + tile, :].astype(F32)
        + linear
        + spread[:, r * channels : (r + 1) * channels]
    )
    return total.astype(BF16)


def turn_kernel(
    packed,
    devices,
    sec_ref,
    recv_ref,
    carried_ref,
    prev_ref,
    slope_ref,
    state_ref,
    basis_ref,
    synth_ref,
    mix_ref,
    acc_in_ref,
    grad_ref,
    low_ref,
    send_ref,
    acc_ref,
):
    rows, cells, channels = carried_ref.shape
    modes = unpack_rows(recv_ref[...], range(rows), packed)
    mixing = mix_ref[...]
    tile = 256
    spec, acc = None, acc_in_ref[...]
    for w in range(0, cells, tile):
        spread = dot(basis_ref[w : w + tile, :], modes)
        lows = []
        for r in range(rows):
            grad = gradient_tile(r, w, tile, spread, carried_ref, prev_ref, mixing)
            grad_ref[r, w : w + tile, :] = grad
            low, term = finish_tile(r, w, tile, grad, slope_ref, state_ref, low_ref)
            lows.append(low)
            acc = acc + term
        part = dot(synth_ref[:, w : w + tile], jnp.concatenate(lows, axis=1))
        spec = part if spec is None else spec + part
    acc_ref[...] = acc
    send_ref[...] = pack_rows(spec, rows, packed, devices)


def last_kernel(packed, recv_ref, carried_ref, prev_ref, basis_ref, mix_ref, grad_ref):
    rows, cells, channels = carried_ref.shape
    modes = unpack_rows(recv_ref[...], range(rows), packed)
    mixing = mix_ref[...]
    tile = 256
    for w in range(0, cells, tile):
        spread = dot(basis_ref[w : w + tile, :], modes)
        for r in range(rows):
            grad_ref[r, w : w + tile, :] = gradient_tile(
                r, w, tile, spread, carried_ref, prev_ref, mixing
            )


def weight_kernel(steps, *refs):
    coeff_ref, cot_refs, out_ref = refs[0], refs[1 : 1 + steps], refs[1 + steps]
    channels = out_ref.shape[-1]
    tall = coeff_ref.shape[2]
    groups = tall // 8
    left = jnp.concatenate(
        [coeff_ref[s, 0].astype(F32).reshape(groups, 8, channels) for s in range(steps)], axis=1
    )
    right = jnp.concatenate(
        [ref[0].astype(F32).reshape(groups, 8, channels) for ref in cot_refs], axis=1
    )
    span = steps * 8
    left = left.reshape(groups * span, channels)
    right = right.reshape(groups * span, channels)
    ids = lax.broadcasted_iota(jnp.int32, right.shape, 0)
    turned = jnp.where(
        ids % 2 == 0,
        pltpu.roll(right, groups * span - 1, 0),
        -pltpu.roll(right, 1, 0),
    )
    right = jnp.concatenate([right, turned], axis=1).astype(BF16)
    pair = (ids // 2) % 4
    lefts = [jnp.where(pair == t, left, 0.0).astype(BF16) for t in range(4)]
    per_j = out_ref.shape[1]
    for g in range(groups):
        rhs = right[g * span : (g + 1) * span]
        for t in range(4):
            product = dot(lefts[t][g * span : (g + 1) * span], rhs, ((0,), (0,))).astype(BF16)
            j, k = divmod(g * 4 + t, per_j)
            out_ref[j, k, 0] = product[:, :channels]
            out_ref[j, k, 1] = product[:, channels:]


def whole(shape):
    return pl.BlockSpec(shape, lambda *_: (0,) * len(shape))


def call(kernel, outs, in_specs, operands, grid=(1,), out_specs=None, scratch=(), prefetch=None,
         flops=0, moved=0):
    if out_specs is None:
        out_specs = [whole(o.shape) for o in outs]
    count = 0 if prefetch is None else 1
    lead = () if prefetch is None else (prefetch,)
    return pl.pallas_call(
        kernel,
        out_shape=outs,
        grid_spec=pltpu.PrefetchScalarGridSpec(
            num_scalar_prefetch=count,
            grid=grid,
            in_specs=in_specs,
            out_specs=out_specs,
            scratch_shapes=list(scratch),
        ),
        compiler_params=pltpu.CompilerParams(
            vmem_limit_bytes=VMEM_LIMIT, dimension_semantics=("arbitrary",) * len(grid)
        ),
        cost_estimate=pl.CostEstimate(flops=flops, bytes_accessed=moved, transcendentals=0),
    )(*lead, *operands)


def local(states, cotangent, spec_weights, local_weight, bias):
    sections = lax.axis_size("section")
    row_devs = lax.axis_size("row")
    section = lax.axis_index("section")
    devices = sections * row_devs
    channels = local_weight.shape[0]
    cells = states.shape[2]
    rows_here = states.shape[1]
    rows = rows_here // sections
    freqs = spec_weights.shape[0]
    row_modes = spec_weights.shape[1]
    modes = row_modes // sections
    parts = 2 * modes
    lat_cells = rows_here * row_devs
    packed = parts == 8
    sec = section.astype(jnp.int32).reshape(1)

    order = (
        np.arange(row_devs)[None, :, None] * row_modes
        + np.arange(sections)[:, None, None] * modes
        + np.arange(modes)[None, None, :]
    ).reshape(-1)
    basis_np, synth_np = lon_tables(order, cells)
    basis = jnp.asarray(basis_np, BF16)
    basis_t = jnp.asarray(basis_np.T, BF16)
    synth = jnp.asarray(synth_np, BF16)
    synth_t = jnp.asarray(synth_np.T, BF16)
    row_order = (
        np.arange(row_devs)[None, :, None] * rows_here
        + np.arange(sections)[:, None, None] * rows
        + np.arange(rows)[None, None, :]
    ).reshape(-1)
    lat_plain = jnp.asarray(lat_matrices(np.arange(lat_cells), freqs, lat_cells, modes), BF16)
    shared_np = lat_matrices(row_order, freqs, lat_cells, modes)
    lat_shared = jnp.asarray(shared_np, BF16)
    inv_shared = jnp.asarray(shared_np.T, BF16)
    mode_rows = lat_plain.shape[0]
    grid_rows = lat_plain.shape[1]

    def exchange(values):
        return lax.all_to_all(values, ALL, 0, 0, tiled=True)

    own = states[0].reshape(sections, rows, cells, channels)
    pieces = [lax.dynamic_index_in_dim(own, section, 0, False)]
    for d in range(1, sections):
        piece = lax.dynamic_index_in_dim(own, section ^ d, 0, False)
        pieces.append(lax.ppermute(piece, "section", [(i, i ^ d) for i in range(sections)]))
    all_states = jnp.stack(pieces, 0)

    total = basis_t.shape[0]
    out_shape = (devices, rows_here * 8, channels) if packed else (rows_here, total, channels)
    (spectra,) = call(
        functools.partial(spectra_kernel, 2, packed, devices),
        [jax.ShapeDtypeStruct(out_shape, BF16)],
        [whole(states.shape[1:]), whole(basis_t.shape)],
        (states[0], basis_t),
        flops=2 * total * cells * rows_here * channels,
        moved=4 * rows_here * cells * channels,
    )
    if not packed:
        spectra = outer_pack(spectra, devices)
    gathered = exchange(spectra).reshape(sections * grid_rows, channels)

    block_j = max(1, min(freqs, 32 // modes))
    weight_block = (block_j, modes, 2, channels, channels)
    weight_spec = pl.BlockSpec(weight_block, lambda b, s: (b, s[0], 0, 0, 0))
    weight_bytes = 4 * freqs * modes * channels * channels
    coeffs, mixed = call(
        functools.partial(mix_kernel, sections),
        [
            jax.ShapeDtypeStruct((sections, mode_rows, channels), BF16),
            jax.ShapeDtypeStruct((sections, grid_rows, channels), BF16),
        ],
        [whole(gathered.shape), whole(lat_plain.shape), whole(inv_shared.shape), weight_spec],
        (gathered, lat_plain, inv_shared, spec_weights),
        grid=(freqs // block_j,),
        scratch=[
            pltpu.VMEM((sections * mode_rows, 8 * channels), BF16),
            pltpu.VMEM((sections, mode_rows, channels), F32),
        ],
        prefetch=sec,
        flops=4 * weight_bytes,
        moved=weight_bytes,
    )
    mixed = mixed.reshape(sections, devices, rows * parts, channels).transpose(1, 0, 2, 3)
    back = exchange(mixed.reshape(devices, sections * rows * parts, channels))
    if not packed:
        back = outer_unpack(back, sections * rows)

    field_block = (1, rows, cells, channels)
    shape3 = (rows, cells, channels)
    bias2 = bias.reshape(1, channels)
    slopes = [None] * sections
    for s in range(sections - 1, -1, -1):
        (slopes[s],) = call(
            functools.partial(slope_kernel, s, rows, packed),
            [jax.ShapeDtypeStruct(shape3, F32)],
            [
                whole(back.shape),
                pl.BlockSpec(field_block, functools.partial(lambda s, b, i: (i[0] ^ s, 0, 0, 0), s)),
                whole(synth_t.shape),
                whole(local_weight.shape),
                whole(bias2.shape),
            ],
            (back, all_states, synth_t, local_weight, bias2),
            prefetch=sec,
            flops=2 * total * cells * rows * channels,
            moved=10 * rows * cells * channels,
        )

    send_shape = (devices, rows * 8, channels) if packed else (rows, total, channels)
    turn_outs = [
        jax.ShapeDtypeStruct(shape3, BF16),
        jax.ShapeDtypeStruct(send_shape, BF16),
        jax.ShapeDtypeStruct((channels, channels), F32),
    ]

    def state_spec(s):
        return pl.BlockSpec(field_block, lambda b, i: (i[0] ^ s, 0, 0, 0))

    s = sections - 1
    carried = lax.dynamic_slice_in_dim(cotangent, section * rows, rows, 0)
    low, send, acc = call(
        functools.partial(start_kernel, packed, devices),
        turn_outs,
        [whole(shape3), whole(shape3), state_spec(s), whole(synth.shape)],
        (carried, slopes[s], all_states, synth),
        prefetch=sec,
        flops=2 * total * cells * rows * channels,
        moved=10 * rows * cells * channels,
    )
    grads = [None] * sections
    cots = [None] * sections
    slot = -(-channels // devices)
    for s in range(sections - 1, -1, -1):
        if not packed:
            send = outer_pack(send, devices)
        if s == 0:
            terms = jnp.pad(acc, ((0, slot * devices - channels), (0, 0)))
            terms = terms.reshape(devices, slot, channels)
            high = terms.astype(BF16)
            rest = (terms - high.astype(F32)).astype(BF16)
            send = jnp.concatenate([send, high, rest], axis=1)
        got = exchange(send)
        if s == 0:
            sums = jnp.sum(got[:, rows * parts :].astype(F32), 0)
            sums = sums[:slot] + sums[slot:]
            got = got[:, : rows * parts]
        cots[s], inner = call(
            adjoint_kernel,
            [
                jax.ShapeDtypeStruct((mode_rows, channels), BF16),
                jax.ShapeDtypeStruct((grid_rows, channels), BF16),
            ],
            [
                whole((grid_rows, channels)),
                whole(lat_shared.shape),
                whole(inv_shared.shape),
                weight_spec,
            ],
            (got.reshape(grid_rows, channels), lat_shared, inv_shared, spec_weights),
            grid=(freqs // block_j,),
            scratch=[
                pltpu.VMEM((mode_rows, 16 * channels), BF16),
                pltpu.VMEM((mode_rows, channels), F32),
            ],
            prefetch=sec,
            flops=2 * weight_bytes,
            moved=weight_bytes,
        )
        inner = inner.reshape(devices, rows * parts, channels)
        if s == 0:
            high = sums.astype(BF16)
            rest = (sums - high.astype(F32)).astype(BF16)
            both = jnp.concatenate([high, rest], 0)
            both = jnp.broadcast_to(both[None], (devices,) + both.shape)
            inner = jnp.concatenate([inner, both], axis=1)
        got = exchange(inner)
        if s == 0:
            both = got[:, rows * parts :].astype(F32)
            got = got[:, : rows * parts]
            local_total = (both[:, :slot] + both[:, slot:]).reshape(-1, channels)[:channels]
        if not packed:
            got = outer_unpack(got, rows)
        if s > 0:
            grads[s], low, send, acc = call(
                functools.partial(turn_kernel, packed, devices),
                [jax.ShapeDtypeStruct(shape3, BF16)] + turn_outs,
                [
                    whole(got.shape),
                    whole(shape3),
                    whole(shape3),
                    whole(shape3),
                    state_spec(s - 1),
                    whole(basis.shape),
                    whole(synth.shape),
                    whole(local_weight.shape),
                    whole(acc.shape),
                ],
                (got, carried, low, slopes[s - 1], all_states, basis, synth, local_weight, acc),
                prefetch=sec,
                flops=4 * total * cells * rows * channels,
                moved=16 * rows * cells * channels,
            )
            carried = grads[s]
        else:
            (grads[0],) = call(
                functools.partial(last_kernel, packed),
                [jax.ShapeDtypeStruct(shape3, BF16)],
                [
                    whole(got.shape),
                    whole(shape3),
                    whole(shape3),
                    whole(basis.shape),
                    whole(local_weight.shape),
                ],
                (got, carried, low, basis, local_weight),
                flops=2 * total * cells * rows * channels,
                moved=8 * rows * cells * channels,
            )

    d_local = local_total * lax.rsqrt(jnp.float32(sections * lat_cells * cells))

    part = mode_rows // sections

    def to_sections(values, axis):
        return lax.all_to_all(values, "section", axis, axis, tiled=True)

    step_coeffs = to_sections(coeffs.reshape(sections, sections, part, channels), 1)
    step_cots = [to_sections(c.reshape(sections, part, channels), 0) for c in cots]
    own_freqs = freqs // sections
    own_j = max(1, min(own_freqs, 32 // modes))
    tall = own_j * parts
    (d_spectral,) = call(
        functools.partial(weight_kernel, sections),
        [jax.ShapeDtypeStruct((own_freqs, row_modes, 2, channels, channels), BF16)],
        [pl.BlockSpec((sections, 1, tall, channels), lambda a, b: (0, a, b, 0))]
        + [pl.BlockSpec((1, tall, channels), lambda a, b: (a, b, 0))] * sections,
        (step_coeffs, *step_cots),
        grid=(sections, own_freqs // own_j),
        out_specs=[
            pl.BlockSpec((own_j, modes, 2, channels, channels), lambda a, b: (b, a, 0, 0, 0))
        ],
        flops=8 * weight_bytes,
        moved=weight_bytes,
    )

    grad_states = lax.all_to_all(jnp.stack(grads, 0), "section", 0, 0, tiled=True)
    grad_states = grad_states.reshape(1, rows_here, cells, channels)
    return (grad_states, d_spectral, d_local)


def solution(mesh):
    return jax.shard_map(
        local,
        mesh=mesh,
        in_specs=(
            P("section", "row", None, None),
            P("row", None, None),
            P(None, "row", None, None, None),
            P(),
            P(),
        ),
        out_specs=(P("section", "row", None, None), P("section", "row", None, None, None), P()),
        check_vma=False,
    )
```

time: 957 us -> 344 us (0.36)
  waiting for transfers between devices: 339 us -> 103 us
  matrix products: 217 us -> 0 us
  local copies, waits for them, and re-layouts: 133 us -> 18.1 us
  Pallas kernels: 0 us -> 109 us
  blocking collectives: 137 us -> 50.2 us
  other arithmetic: 67.3 us -> 12.1 us
  between operations: 15.4 us -> 0.84 us
    dot_general x35 -> x0, matrix products: 217 us -> none  [the longest x4 107 us: spectral_adjoint(): jnp.einsum('jkqio,jkpo->jkqpi', weights, cotan_spec, preferred_element_ty...]
    psum x1 -> x0, waiting for transfers between devices: 124 us -> none  [local(): local_total = lax.psum(own_term, ('section', 'row'))]
    ppermute x3, waiting for transfers between devices: 153 us -> 30.9 us  [local(): lax.ppermute(piece, 'section', [(i, i ^ d) for i in range(sections)])]
    pallas_call x0 -> x16, Pallas kernels: none -> 109 us  [call(): pl.pallas_call(kernel, out_shape=outs, grid_spec=pltpu.PrefetchScalarGrid...]
    all_to_all x5 -> x4, blocking collectives: 137 us -> 50.2 us  [exchange(): return lax.all_to_all(values, ALL, 0, 0, tiled=True)]
    unnamed x109 -> x21, local copies, waits for them, and re-layouts: 40.1 us -> 7.04 us
    another operation x30 -> x2, other arithmetic: 32.4 us -> 6.24 us  [the longest x1 3.3 us: local(): all_states = jnp.stack(pieces, 0)]
    convert_element_type x16 -> x0, local copies, waits for them, and re-layouts: 23.2 us -> none  [the longest x5 13.9 us: lat_inverse(): return jnp.stack([real_part, imag_part], 2).reshape(lat_cells, mode_count...]
  transfers between devices with their start and end apart: 11 -> 15, of which waited for: 8 -> 13; matrix products, arithmetic and copies ran while one was open for 17% -> 5% of each run, Pallas kernels for 0% -> 10%
where the time goes in v1:
time: 344 us; the launch traced here: 341 us
  Pallas kernels  109 us (32%)
  waiting for transfers between devices  103 us (30%)
  blocking collectives  50.2 us (15%)
  starting transfers between devices  48.2 us (14%)
  local copies, waits for them, and re-layouts  18.1 us (5%)
  other arithmetic  12.1 us (4%)
    pallas_call x16, Pallas kernels, call(): pl.pallas_call(kernel, out_shape=outs, grid_spec=pltpu.PrefetchScalarGrid...  109 us
    all_to_all x4, blocking collectives, exchange(): return lax.all_to_all(values, ALL, 0, 0, tiled=True)  50.2 us
    all_to_all x6, waiting for transfers between devices, exchange(): return lax.all_to_all(values, ALL, 0, 0, tiled=True)  46.4 us
    ppermute x3, waiting for transfers between devices, local(): lax.ppermute(piece, 'section', [(i, i ^ d) for i in range(sections)])  30.9 us
    all_to_all x6, starting transfers between devices, exchange(): return lax.all_to_all(values, ALL, 0, 0, tiled=True)  20.8 us
    all_to_all x5, starting transfers between devices, to_sections(): return lax.all_to_all(values, 'section', axis, axis, tiled=True)  19.5 us
    all_to_all x1, waiting for transfers between devices, local(): lax.all_to_all(jnp.stack(grads, 0), 'section', 0, 0, tiled=True)  14 us
    all_to_all x5, waiting for transfers between devices, to_sections(): return lax.all_to_all(values, 'section', axis, axis, tiled=True)  11.4 us
  transfers between devices with their start and end apart: 15, of which 13 were waited for; matrix products, arithmetic and copies ran while one was open for 5% of the time, Pallas kernels for 10%

profile of v1, /device:TPU:0, one launch (start us, length us, event | category | flops | bytes accessed | tf_op | source)
XLA Modules:
  0.0 341.4 jit_solution(6077677862472499309)
XLA Ops:
  0.6 3.5 %shard_map.139 = bf16[32,96,128]{2,1,0:T(8,128)(2,1)} custom-call(bf16[12,768,128]{2,1,0:T(8,128)(2,1)} %bitcast.38, bf16[256,768]{1,0:T(8,128)(2,1)} %constant.45.clone.basis_ref), custom_call_target="tpu_custom_call" | custom-call | flops 603979776 | bytes 4718592 | tf_op jit(solution)/shard_map/pallas_call | solution.py:345
  4.2 7.3 %all-to-all-start = ((bf16[32,96,128]{2,1,0:T(8,128)(2,1)}), bf16[32,96,128]{2,1,0:T(8,128)(2,1)S(1)}, u32[]{:S(2)}, u32[]{:S(2)}) async-start(bf16[32,96,128]{2,1,0:T(8,128)(2,1)} %shard_map.139), calls=%async_computation | async-start | bytes 1572864 | tf_op jit(solution)/shard_map/all_to_all | solution.py:402
  11.5 22.0 %all-to-all-done = bf16[32,96,128]{2,1,0:T(8,128)(2,1)S(1)} async-done(((bf16[32,96,128]{2,1,0:T(8,128)(2,1)}), bf16[32,96,128]{2,1,0:T(8,128)(2,1)S(1)}, u32[]{:S(2)}, u32[]{:S(2)}) %all-to-all-start) | async-done | bytes 786464 | tf_op jit(solution)/shard_map/all_to_all | solution.py:402
  33.4 0.9 copy-done.2
  34.3 13.9 %shard_map.140 = (bf16[4,512,128]{2,1,0:T(8,128)(2,1)}, bf16[4,768,128]{2,1,0:T(8,128)(2,1)}) custom-call(s32[1]{0:T(128)} %bitcast.sec_ref, bf16[3072,128]{1,0:T(8,128)(2,1)} %bitcast.41, bf16[512,768]{1,0:T(8,128)(2,1)} %constant.48.clone.lat_ref, bf16[768,512]{1,0:T(8,128)(2,1)} %constant.50.clone.inv_ref, bf16[64,16,2,128,128]{4,3,2,1,0:T(8,128)(2,1)} %w_ref.9), custom_call_target="tpu_custom_call" | custom-call | flops 67108864 | bytes 16777216 | tf_op jit(solution)/shard_map/pallas_call | solution.py:345
  48.2 2.1 copy.16
  50.3 2.6 all-to-all-start.1
  52.9 3.0 constant_dynamic-slice_fusion
  56.0 2.6 collective-permute-start.2
  59.5 0.9 constant_dynamic-slice_fusion.1.cot_ref.carried_ref
  60.3 19.0 %collective-permute-done.2 = bf16[3,768,128]{2,1,0:T(8,128)(2,1)} collective-permute-done((bf16[3,768,128]{2,1,0:T(8,128)(2,1)}, bf16[3,768,128]{2,1,0:T(8,128)(2,1)}, u32[]{:S(2)}, u32[]{:S(2)}) %collective-permute-start.2) | collective-permute-done | bytes 589856 | tf_op jit(solution)/shard_map/ppermute | solution.py:408
  79.3 10.9 %collective-permute-done.1 = bf16[3,768,128]{2,1,0:T(8,128)(2,1)} collective-permute-done((bf16[3,768,128]{2,1,0:T(8,128)(2,1)}, bf16[3,768,128]{2,1,0:T(8,128)(2,1)}, u32[]{:S(2)}, u32[]{:S(2)}) %collective-permute-start.1) | collective-permute-done | bytes 589856 | tf_op jit(solution)/shard_map/ppermute | solution.py:408
  90.2 1.0 collective-permute-done
  91.2 3.3 pad_maximum_fusion.state_ref
  94.5 0.9 copy-done.1
  95.4 3.4 shard_map.141.slope_ref
  98.8 3.0 shard_map.142
  101.8 12.5 %all_to_all.80 = bf16[32,24,128]{2,1,0:T(8,128)(2,1)} all-to-all(bf16[32,24,128]{2,1,0:T(8,128)(2,1)} %get-tuple-element.29), channel_id=1, replica_groups=mesh['section'=4,'row'=8] {'section','row'}, dimensions={0} | all-to-all | bytes 393216 | tf_op jit(solution)/shard_map/all_to_all | solution.py:402
  114.3 12.5 %shard_map.143 = (bf16[512,128]{1,0:T(8,128)(2,1)}, bf16[768,128]{1,0:T(8,128)(2,1)}) custom-call(s32[1]{0:T(128)} %bitcast.sec_ref, bf16[768,128]{1,0:T(8,128)(2,1)} %bitcast.48, bf16[512,768]{1,0:T(8,128)(2,1)} %constant.49.clone.lat_ref, bf16[768,512]{1,0:T(8,128)(2,1)} %constant.50.clone.inv_ref, bf16[64,16,2,128,128]{4,3,2,1,0:T(8,128)(2,1)} %w_ref.9), custom_call_target="tpu_custom_call" | custom-call | flops 33554432 | bytes 16777216 | tf_op jit(solution)/shard_map/pallas_call | solution.py:345
  126.8 2.7 all-to-all-start.3
  129.5 3.4 shard_map.144.slope_ref
  132.9 5.4 %all-to-all-done.3.recv_ref = bf16[32,24,128]{2,1,0:T(8,128)(2,1)S(1)} async-done(((bf16[32,24,128]{2,1,0:T(8,128)(2,1)}), bf16[32,24,128]{2,1,0:T(8,128)(2,1)S(1)}, u32[]{:S(2)}, u32[]{:S(2)}) %all-to-all-start.3) | async-done | bytes 196640 | tf_op jit(solution)/shard_map/all_to_all | solution.py:402
  138.2 0.7 copy-done.8
  138.9 4.1 %shard_map.145 = (bf16[3,768,128]{2,1,0:T(8,128)(2,1)}, bf16[3,768,128]{2,1,0:T(8,128)(2,1)}, bf16[32,24,128]{2,1,0:T(8,128)(2,1)}, f32[128,128]{1,0:T(8,128)}) custom-call(s32[1]{0:T(128)} %bitcast.sec_ref, bf16[32,24,128]{2,1,0:T(8,128)(2,1)} %copy-done.8, bf16[3,768,128]{2,1,0:T(8,128)(2,1)} %constant_dynamic-slice_fusion.1.cot_ref.carried_ref, ...), custom_call_target="tpu_custom_call" | custom-call | flops 301989888 | bytes 4718592 | tf_op jit(solution)/shard_map/pallas_call | solution.py:345
  143.0 12.0 %all_to_all.81 = bf16[32,24,128]{2,1,0:T(8,128)(2,1)} all-to-all(bf16[32,24,128]{2,1,0:T(8,128)(2,1)} %get-tuple-element.33), channel_id=1, replica_groups=mesh['section'=4,'row'=8] {'section','row'}, dimensions={0} | all-to-all | bytes 393216 | tf_op jit(solution)/shard_map/all_to_all | solution.py:402
  155.0 12.5 %shard_map.146 = (bf16[512,128]{1,0:T(8,128)(2,1)}, bf16[768,128]{1,0:T(8,128)(2,1)}) custom-call(s32[1]{0:T(128)} %bitcast.sec_ref, bf16[768,128]{1,0:T(8,128)(2,1)} %bitcast.49, bf16[512,768]{1,0:T(8,128)(2,1)} %constant.49.clone.lat_ref, bf16[768,512]{1,0:T(8,128)(2,1)} %constant.50.clone.inv_ref, bf16[64,16,2,128,128]{4,3,2,1,0:T(8,128)(2,1)} %w_ref.9), custom_call_target="tpu_custom_call" | custom-call | flops 33554432 | bytes 16777216 | tf_op jit(solution)/shard_map/pallas_call | solution.py:345
  167.5 2.8 all-to-all-start.5
  170.3 3.4 shard_map.147.slope_ref
  173.7 5.2 %all-to-all-done.5.recv_ref = bf16[32,24,128]{2,1,0:T(8,128)(2,1)S(1)} async-done(((bf16[32,24,128]{2,1,0:T(8,128)(2,1)}), bf16[32,24,128]{2,1,0:T(8,128)(2,1)S(1)}, u32[]{:S(2)}, u32[]{:S(2)}) %all-to-all-start.5) | async-done | bytes 196640 | tf_op jit(solution)/shard_map/all_to_all | solution.py:402
  179.5 4.1 %shard_map.148 = (bf16[3,768,128]{2,1,0:T(8,128)(2,1)}, bf16[3,768,128]{2,1,0:T(8,128)(2,1)}, bf16[32,24,128]{2,1,0:T(8,128)(2,1)}, f32[128,128]{1,0:T(8,128)}) custom-call(s32[1]{0:T(128)} %bitcast.sec_ref, bf16[32,24,128]{2,1,0:T(8,128)(2,1)} %copy-done.9, bf16[3,768,128]{2,1,0:T(8,128)(2,1)} %get-tuple-element.35.carried_ref, ...), custom_call_target="tpu_custom_call" | custom-call | flops 301989888 | bytes 4718592 | tf_op jit(solution)/shard_map/pallas_call | solution.py:345
  183.6 12.0 %all_to_all.82 = bf16[32,24,128]{2,1,0:T(8,128)(2,1)} all-to-all(bf16[32,24,128]{2,1,0:T(8,128)(2,1)} %get-tuple-element.38), channel_id=1, replica_groups=mesh['section'=4,'row'=8] {'section','row'}, dimensions={0} | all-to-all | bytes 393216 | tf_op jit(solution)/shard_map/all_to_all | solution.py:402
  195.7 12.5 %shard_map.149 = (bf16[512,128]{1,0:T(8,128)(2,1)}, bf16[768,128]{1,0:T(8,128)(2,1)}) custom-call(s32[1]{0:T(128)} %bitcast.sec_ref, bf16[768,128]{1,0:T(8,128)(2,1)} %bitcast.50, bf16[512,768]{1,0:T(8,128)(2,1)} %constant.49.clone.lat_ref, bf16[768,512]{1,0:T(8,128)(2,1)} %constant.50.clone.inv_ref, bf16[64,16,2,128,128]{4,3,2,1,0:T(8,128)(2,1)} %w_ref.9), custom_call_target="tpu_custom_call" | custom-call | flops 33554432 | bytes 16777216 | tf_op jit(solution)/shard_map/pallas_call | solution.py:345
  208.2 2.6 all-to-all-start.7
  210.8 3.4 shard_map.150.slope_ref
  214.2 5.4 %all-to-all-done.7.recv_ref = bf16[32,24,128]{2,1,0:T(8,128)(2,1)S(1)} async-done(((bf16[32,24,128]{2,1,0:T(8,128)(2,1)}), bf16[32,24,128]{2,1,0:T(8,128)(2,1)S(1)}, u32[]{:S(2)}, u32[]{:S(2)}) %all-to-all-start.7) | async-done | bytes 196640 | tf_op jit(solution)/shard_map/all_to_all | solution.py:402
  219.5 0.7 copy-done.7
  220.2 4.1 %shard_map.151 = (bf16[3,768,128]{2,1,0:T(8,128)(2,1)}, bf16[3,768,128]{2,1,0:T(8,128)(2,1)}, bf16[32,24,128]{2,1,0:T(8,128)(2,1)}, f32[128,128]{1,0:T(8,128)}) custom-call(s32[1]{0:T(128)} %bitcast.sec_ref, bf16[32,24,128]{2,1,0:T(8,128)(2,1)} %copy-done.7, bf16[3,768,128]{2,1,0:T(8,128)(2,1)} %get-tuple-element.40.carried_ref, ...), custom_call_target="tpu_custom_call" | custom-call | flops 301989888 | bytes 4718592 | tf_op jit(solution)/shard_map/pallas_call | solution.py:345
  224.3 0.9 subtract_convert_fusion
  225.3 1.7 pad_maximum_fusion.2
  227.0 2.7 all-to-all-start.8
  229.7 1.9 copy.17
  231.6 8.5 %all-to-all-done.8 = bf16[32,32,128]{2,1,0:T(8,128)(2,1)S(1)} async-done(((bf16[32,32,128]{2,1,0:T(8,128)(2,1)}), bf16[32,32,128]{2,1,0:T(8,128)(2,1)S(1)}, u32[]{:S(2)}, u32[]{:S(2)}) %all-to-all-start.8) | async-done | bytes 262176 | tf_op jit(solution)/shard_map/all_to_all | solution.py:402
  240.1 3.5 %all-to-all-start.11 = ((bf16[4,4,128,128]{3,2,0,1:T(8,128)(2,1)}), bf16[4,4,128,128]{3,2,0,1:T(8,128)(2,1)S(1)}, u32[]{:S(2)}, u32[]{:S(2)}) async-start(bf16[4,4,128,128]{3,2,0,1:T(8,128)(2,1)} %copy.17), calls=%async_computation.11 | async-start | bytes 1048576 | tf_op jit(solution)/shard_map/all_to_all | solution.py:588
  243.6 0.7 slice.32
  244.3 12.5 %shard_map.152 = (bf16[512,128]{1,0:T(8,128)(2,1)}, bf16[768,128]{1,0:T(8,128)(2,1)}) custom-call(s32[1]{0:T(128)} %bitcast.sec_ref, bf16[768,128]{1,0:T(8,128)(2,1)} %bitcast.47, bf16[512,768]{1,0:T(8,128)(2,1)} %constant.49.clone.lat_ref, bf16[768,512]{1,0:T(8,128)(2,1)} %constant.50.clone.inv_ref, bf16[64,16,2,128,128]{4,3,2,1,0:T(8,128)(2,1)} %w_ref.9), custom_call_target="tpu_custom_call" | custom-call | flops 33554432 | bytes 16777216 | tf_op jit(solution)/shard_map/pallas_call | solution.py:345
  256.8 4.2 %all-to-all-start.15 = ((bf16[4,128,128]{2,1,0:T(8,128)(2,1)}), bf16[4,128,128]{2,1,0:T(8,128)(2,1)}, u32[]{:S(2)}, u32[]{:S(2)}) async-start(bf16[4,128,128]{2,1,0:T(8,128)(2,1)} %bitcast.32), calls=%async_computation.15 | async-start | bytes 262144 | tf_op jit(solution)/shard_map/all_to_all | solution.py:588
  261.0 5.1 %all-to-all-done.15.refs_4_ = bf16[4,128,128]{2,1,0:T(8,128)(2,1)} async-done(((bf16[4,128,128]{2,1,0:T(8,128)(2,1)}), bf16[4,128,128]{2,1,0:T(8,128)(2,1)}, u32[]{:S(2)}, u32[]{:S(2)}) %all-to-all-start.15) | async-done | bytes 131104 | tf_op jit(solution)/shard_map/all_to_all | solution.py:588
  266.1 3.9 %all-to-all-start.14 = ((bf16[4,128,128]{2,1,0:T(8,128)(2,1)}), bf16[4,128,128]{2,1,0:T(8,128)(2,1)}, u32[]{:S(2)}, u32[]{:S(2)}) async-start(bf16[4,128,128]{2,1,0:T(8,128)(2,1)} %bitcast.56), calls=%async_computation.14 | async-start | bytes 262144 | tf_op jit(solution)/shard_map/all_to_all | solution.py:588
  270.1 1.7 pad_maximum_fusion.3
  271.8 3.4 all-to-all-done.14.refs_3_
  275.2 13.7 %all_to_all.83 = bf16[32,32,128]{2,1,0:T(8,128)(2,1)} all-to-all(bf16[32,32,128]{2,1,0:T(8,128)(2,1)} %pad_maximum_fusion.3), channel_id=1, replica_groups=mesh['section'=4,'row'=8] {'section','row'}, dimensions={0} | all-to-all | bytes 524288 | tf_op jit(solution)/shard_map/all_to_all | solution.py:402
  288.8 3.9 %all-to-all-start.13 = ((bf16[4,128,128]{2,1,0:T(8,128)(2,1)}), bf16[4,128,128]{2,1,0:T(8,128)(2,1)}, u32[]{:S(2)}, u32[]{:S(2)}) async-start(bf16[4,128,128]{2,1,0:T(8,128)(2,1)} %bitcast.57), calls=%async_computation.13 | async-start | bytes 262144 | tf_op jit(solution)/shard_map/all_to_all | solution.py:588
  292.8 1.6 slice.34.recv_ref
  294.4 2.7 shard_map.153
  297.2 0.8 all-to-all-done.13.refs_2_
  298.0 3.9 %all-to-all-start.12 = ((bf16[4,128,128]{2,1,0:T(8,128)(2,1)}), bf16[4,128,128]{2,1,0:T(8,128)(2,1)}, u32[]{:S(2)}, u32[]{:S(2)}) async-start(bf16[4,128,128]{2,1,0:T(8,128)(2,1)} %bitcast.58), calls=%async_computation.12 | async-start | bytes 262144 | tf_op jit(solution)/shard_map/all_to_all | solution.py:588
  302.0 2.9 pad_maximum_fusion.1
  304.9 2.1 all-to-all-done.12.refs_1_
  307.0 4.5 %all-to-all-start.10 = ((bf16[4,3,768,128]{3,2,1,0:T(8,128)(2,1)}), bf16[4,3,768,128]{3,2,1,0:T(8,128)(2,1)}, u32[]{:S(2)}, u32[]{:S(2)}) async-start(bf16[4,3,768,128]{3,2,1,0:T(8,128)(2,1)} %pad_maximum_fusion.1), calls=%async_computation.10 | async-start | bytes 4718592 | tf_op jit(solution)/shard_map/all_to_all | solution.py:609
  311.5 0.8 copy.18.refs_0_
  312.4 10.2 %shard_map.154 = bf16[16,16,2,128,128]{4,3,2,1,0:T(8,128)(2,1)} custom-call(bf16[4,4,128,128]{3,2,1,0:T(8,128)(2,1)} %copy.18.refs_0_, bf16[4,128,128]{2,1,0:T(8,128)(2,1)} %all-to-all-done.12.refs_1_, bf16[4,128,128]{2,1,0:T(8,128)(2,1)} %all-to-all-done.13.refs_2_, bf16[4,128,128]{2,1,0:T(8,128)(2,1)} %all-to-all-done.14.refs_3_, ...), custom_call_target="tpu_custom_call" | custom-call | flops 134217728 | bytes 16777216 | tf_op jit(solution)/shard_map/pallas_call | solution.py:345
  322.6 0.8 slice_convert_fusion
  324.1 14.0 %all-to-all-done.10 = bf16[4,3,768,128]{3,2,1,0:T(8,128)(2,1)} async-done(((bf16[4,3,768,128]{3,2,1,0:T(8,128)(2,1)}), bf16[4,3,768,128]{3,2,1,0:T(8,128)(2,1)}, u32[]{:S(2)}, u32[]{:S(2)}) %all-to-all-start.10) | async-done | bytes 2359328 | tf_op jit(solution)/shard_map/all_to_all | solution.py:609
  338.1 3.2 copy.20
  (25 shorter events, 2.3 us)
Async XLA Ops:
  0.6 58.9 %copy-start = (bf16[12,768,128]{2,1,0:T(8,128)(2,1)S(1)}, bf16[12,768,128]{2,1,0:T(8,128)(2,1)}, u32[]{:S(2)}) copy-start(bf16[12,768,128]{2,1,0:T(8,128)(2,1)} %param.13) | copy-start | bytes 7077892
  4.2 29.3 %all-to-all-start = ((bf16[32,96,128]{2,1,0:T(8,128)(2,1)}), bf16[32,96,128]{2,1,0:T(8,128)(2,1)S(1)}, u32[]{:S(2)}, u32[]{:S(2)}) async-start(bf16[32,96,128]{2,1,0:T(8,128)(2,1)} %shard_map.139), calls=%async_computation | async-start | bytes 1572864 | tf_op jit(solution)/shard_map/all_to_all | solution.py:402
  33.4 0.9 copy-start.2
  50.3 44.2 %all-to-all-start.1 = ((bf16[32,96,128]{2,1,0:T(8,128)(2,1)}), bf16[32,96,128]{2,1,0:T(8,128)(2,1)S(1)}, u32[]{:S(2)}, u32[]{:S(2)}) async-start(bf16[32,96,128]{2,1,0:T(8,128)(2,1)} %bitcast.40), calls=%async_computation.1 | async-start | bytes 1572864 | tf_op jit(solution)/shard_map/all_to_all | solution.py:402
  56.0 23.3 %collective-permute-start.2 = (bf16[3,768,128]{2,1,0:T(8,128)(2,1)}, bf16[3,768,128]{2,1,0:T(8,128)(2,1)}, u32[]{:S(2)}, u32[]{:S(2)}) collective-permute-start(bf16[3,768,128]{2,1,0:T(8,128)(2,1)} %get-tuple-element.58), channel_id=1, source_target_pairs={{0,24},{8,16},{16,8},{24,0},{1,25},{9,17},{17,9},{25,1},{2,26},{10... | collective-permute-start | bytes 1769480 | tf_op jit(solution)/shard_map/ppermute | solution.py:408
  58.6 31.7 %collective-permute-start.1 = (bf16[3,768,128]{2,1,0:T(8,128)(2,1)}, bf16[3,768,128]{2,1,0:T(8,128)(2,1)}, u32[]{:S(2)}, u32[]{:S(2)}) collective-permute-start(bf16[3,768,128]{2,1,0:T(8,128)(2,1)} %get-tuple-element.59), channel_id=1, source_target_pairs={{0,16},{8,24},{16,0},{24,8},{1,17},{9,25},{17,1},{25,9},{2,18},{10... | collective-permute-start | bytes 1769480 | tf_op jit(solution)/shard_map/ppermute | solution.py:408
  59.1 32.1 %collective-permute-start = (bf16[3,768,128]{2,1,0:T(8,128)(2,1)}, bf16[3,768,128]{2,1,0:T(8,128)(2,1)}, u32[]{:S(2)}, u32[]{:S(2)}) collective-permute-start(bf16[3,768,128]{2,1,0:T(8,128)(2,1)} %get-tuple-element.60), channel_id=1, source_target_pairs={{0,8},{8,0},{16,24},{24,16},{1,9},{9,1},{17,25},{25,17},{2,10},{10... | collective-permute-start | bytes 1769480 | tf_op jit(solution)/shard_map/ppermute | solution.py:408
  94.5 0.9 copy-start.1
  126.8 11.5 %all-to-all-start.3 = ((bf16[32,24,128]{2,1,0:T(8,128)(2,1)}), bf16[32,24,128]{2,1,0:T(8,128)(2,1)S(1)}, u32[]{:S(2)}, u32[]{:S(2)}) async-start(bf16[32,24,128]{2,1,0:T(8,128)(2,1)} %bitcast.53), calls=%async_computation.3 | async-start | bytes 393216 | tf_op jit(solution)/shard_map/all_to_all | solution.py:402
  138.2 0.7 copy-start.8
  167.5 11.4 %all-to-all-start.5 = ((bf16[32,24,128]{2,1,0:T(8,128)(2,1)}), bf16[32,24,128]{2,1,0:T(8,128)(2,1)S(1)}, u32[]{:S(2)}, u32[]{:S(2)}) async-start(bf16[32,24,128]{2,1,0:T(8,128)(2,1)} %bitcast.54), calls=%async_computation.5 | async-start | bytes 393216 | tf_op jit(solution)/shard_map/all_to_all | solution.py:402
  178.9 0.7 copy-start.9
  208.2 11.4 %all-to-all-start.7 = ((bf16[32,24,128]{2,1,0:T(8,128)(2,1)}), bf16[32,24,128]{2,1,0:T(8,128)(2,1)S(1)}, u32[]{:S(2)}, u32[]{:S(2)}) async-start(bf16[32,24,128]{2,1,0:T(8,128)(2,1)} %bitcast.52), calls=%async_computation.7 | async-start | bytes 393216 | tf_op jit(solution)/shard_map/all_to_all | solution.py:402
  219.5 0.7 copy-start.7
  227.0 13.1 %all-to-all-start.8 = ((bf16[32,32,128]{2,1,0:T(8,128)(2,1)}), bf16[32,32,128]{2,1,0:T(8,128)(2,1)S(1)}, u32[]{:S(2)}, u32[]{:S(2)}) async-start(bf16[32,32,128]{2,1,0:T(8,128)(2,1)} %pad_maximum_fusion.2), calls=%async_computation.8 | async-start | bytes 524288 | tf_op jit(solution)/shard_map/all_to_all | solution.py:402
  240.1 16.7 %all-to-all-start.11 = ((bf16[4,4,128,128]{3,2,0,1:T(8,128)(2,1)}), bf16[4,4,128,128]{3,2,0,1:T(8,128)(2,1)S(1)}, u32[]{:S(2)}, u32[]{:S(2)}) async-start(bf16[4,4,128,128]{3,2,0,1:T(8,128)(2,1)} %copy.17), calls=%async_computation.11 | async-start | bytes 1048576 | tf_op jit(solution)/shard_map/all_to_all | solution.py:588
  256.8 4.2 %copy-start.5 = (bf16[4,4,128,128]{3,2,0,1:T(8,128)(2,1)}, bf16[4,4,128,128]{3,2,0,1:T(8,128)(2,1)S(1)}, u32[]{:S(2)}) copy-start(bf16[4,4,128,128]{3,2,0,1:T(8,128)(2,1)S(1)} %all-to-all-done.11) | copy-start | bytes 1572868
  256.8 9.3 %all-to-all-start.15 = ((bf16[4,128,128]{2,1,0:T(8,128)(2,1)}), bf16[4,128,128]{2,1,0:T(8,128)(2,1)}, u32[]{:S(2)}, u32[]{:S(2)}) async-start(bf16[4,128,128]{2,1,0:T(8,128)(2,1)} %bitcast.32), calls=%async_computation.15 | async-start | bytes 262144 | tf_op jit(solution)/shard_map/all_to_all | solution.py:588
  261.0 40.9 %copy-start.3 = (bf16[3,768,128]{2,1,0:T(8,128)(2,1)S(1)}, bf16[3,768,128]{2,1,0:T(8,128)(2,1)}, u32[]{:S(2)}) copy-start(bf16[3,768,128]{2,1,0:T(8,128)(2,1)} %get-tuple-element.35.carried_ref) | copy-start | bytes 1769476
  261.0 40.9 %copy-start.4 = (bf16[3,768,128]{2,1,0:T(8,128)(2,1)S(1)}, bf16[3,768,128]{2,1,0:T(8,128)(2,1)}, u32[]{:S(2)}) copy-start(bf16[3,768,128]{2,1,0:T(8,128)(2,1)} %get-tuple-element.40.carried_ref) | copy-start | bytes 1769476
  266.1 9.0 %all-to-all-start.14 = ((bf16[4,128,128]{2,1,0:T(8,128)(2,1)}), bf16[4,128,128]{2,1,0:T(8,128)(2,1)}, u32[]{:S(2)}, u32[]{:S(2)}) async-start(bf16[4,128,128]{2,1,0:T(8,128)(2,1)} %bitcast.56), calls=%async_computation.14 | async-start | bytes 262144 | tf_op jit(solution)/shard_map/all_to_all | solution.py:588
  288.8 9.2 %all-to-all-start.13 = ((bf16[4,128,128]{2,1,0:T(8,128)(2,1)}), bf16[4,128,128]{2,1,0:T(8,128)(2,1)}, u32[]{:S(2)}, u32[]{:S(2)}) async-start(bf16[4,128,128]{2,1,0:T(8,128)(2,1)} %bitcast.57), calls=%async_computation.13 | async-start | bytes 262144 | tf_op jit(solution)/shard_map/all_to_all | solution.py:588
  298.0 9.0 %all-to-all-start.12 = ((bf16[4,128,128]{2,1,0:T(8,128)(2,1)}), bf16[4,128,128]{2,1,0:T(8,128)(2,1)}, u32[]{:S(2)}, u32[]{:S(2)}) async-start(bf16[4,128,128]{2,1,0:T(8,128)(2,1)} %bitcast.58), calls=%async_computation.12 | async-start | bytes 262144 | tf_op jit(solution)/shard_map/all_to_all | solution.py:588
  304.9 6.6 %copy-start.6 = (bf16[4,4,128,128]{3,2,0,1:T(8,128)(2,1)S(1)}, bf16[4,4,128,128]{3,2,0,1:T(8,128)(2,1)}, u32[]{:S(2)}) copy-start(bf16[4,4,128,128]{3,2,0,1:T(8,128)(2,1)} %copy-done.5) | copy-start | bytes 1572868
  307.0 31.1 %all-to-all-start.10 = ((bf16[4,3,768,128]{3,2,1,0:T(8,128)(2,1)}), bf16[4,3,768,128]{3,2,1,0:T(8,128)(2,1)}, u32[]{:S(2)}, u32[]{:S(2)}) async-start(bf16[4,3,768,128]{3,2,1,0:T(8,128)(2,1)} %pad_maximum_fusion.1), calls=%async_computation.10 | async-start | bytes 4718592 | tf_op jit(solution)/shard_map/all_to_all | solution.py:609

commit v2 on v1

--- a/solution.py
+++ b/solution.py
@@ -15,6 +15,7 @@
 F32 = jnp.float32
 ALL = ("section", "row")
 VMEM_LIMIT = 56 * 1024 * 1024
+CHUNK = 16
 
 
 def gelu_derivative(values):
@@ -123,72 +124,108 @@
     return parts
 
 
-def mix_kernel(steps, sec_ref, x_ref, lat_ref, inv_ref, w_ref, coeff_ref, out_ref, lhs_ref, z_ref):
-    turn = pl.program_id(0)
+def weight_copies(sec_ref, all_ref, weights_ref, sems):
+    span = weights_ref.shape[0] // sems.shape[0]
+    modes = weights_ref.shape[1]
+    first = sec_ref[0] * modes
+
+    def chunk(n):
+        return pltpu.make_async_copy(
+            all_ref.at[pl.ds(n * span, span), pl.ds(first, modes)],
+            weights_ref.at[pl.ds(n * span, span)],
+            sems.at[n],
+        )
+
+    for n in range(sems.shape[0]):
+        chunk(n).start()
+    return chunk
+
+
+def mix_kernel(
+    steps, packed, sec_ref, x_ref, lat_ref, inv_ref, all_ref, coeff_ref, out_ref, weights_ref,
+    lhs_ref, z_ref, sems
+):
+    chunk = weight_copies(sec_ref, all_ref, weights_ref, sems)
     channels = x_ref.shape[-1]
     span = x_ref.shape[0] // steps
-    total = lat_ref.shape[0]
-    groups = total // 8
-
-    @pl.when(turn == 0)
-    def _():
-        lat = lat_ref[...]
-        found = []
+    groups = lat_ref.shape[0] // 8
+    lat = lat_ref[...]
+    found = []
+    for s in range(steps):
+        value = dot(lat, x_ref[s * span : (s + 1) * span, :]).astype(BF16)
+        coeff_ref[s] = value
+        found.append(value.astype(F32).reshape(groups, 8, channels))
+    tall = jnp.concatenate(found, axis=1).reshape(groups * steps * 8, channels)
+    for n, part in enumerate(spread_pairs(tall, 4, -1.0)):
+        lhs_ref[:, n * channels : (n + 1) * channels] = part
+
+    block = weights_ref.shape[0] // sems.shape[0]
+    per_chunk = groups // sems.shape[0]
+
+    @pl.loop(0, sems.shape[0])
+    def _(n):
+        chunk(n).wait()
+        here = weights_ref[pl.ds(n * block, block)].reshape(per_chunk, 8 * channels, channels)
+        for g in range(per_chunk):
+            at = pl.multiple_of((n * per_chunk + g) * (8 * steps), 8 * steps)
+            mixed = dot(lhs_ref[pl.ds(at, 8 * steps), :], here[g])
+            to = pl.multiple_of((n * per_chunk + g) * 8, 8)
+            for s in range(steps):
+                z_ref[s, pl.ds(to, 8), :] = mixed[s * 8 : (s + 1) * 8]
+
+    inv = inv_ref[...]
+    results = [dot(inv, z_ref[s].astype(BF16)) for s in range(steps)]
+    if packed:
+        devices = out_ref.shape[0]
+        results = [r.reshape(devices, span // devices, channels) for r in results]
+        out_ref[...] = jnp.concatenate(results, axis=1).astype(BF16)
+    else:
         for s in range(steps):
-            value = dot(lat, x_ref[s * span : (s + 1) * span, :]).astype(BF16)
-            coeff_ref[s] = value
-            found.append(value.astype(F32).reshape(groups, 8, channels))
-        tall = jnp.concatenate(found, axis=1).reshape(groups * steps * 8, channels)
-        for n, part in enumerate(spread_pairs_steps(tall, steps)):
-            lhs_ref[:, n * channels : (n + 1) * channels] = part
-
-    pairs = w_ref.shape[0] * w_ref.shape[1]
-    here = pairs // 4
-    weights = w_ref[...].reshape(here, 8 * channels, channels)
-    for g in range(here):
-        at = pl.multiple_of((turn * here + g) * (8 * steps), 8 * steps)
-        mixed = dot(lhs_ref[pl.ds(at, 8 * steps), :], weights[g])
-        to = pl.multiple_of((turn * here + g) * 8, 8)
-        for s in range(steps):
-            z_ref[s, pl.ds(to, 8), :] = mixed[s * 8 : (s + 1) * 8]
-
-    @pl.when(turn == pl.num_programs(0) - 1)
-    def _():
-        inv = inv_ref[...]
-        for s in range(steps):
-            out_ref[s] = dot(inv, z_ref[s].astype(BF16)).astype(BF16)
-
-
-def spread_pairs_steps(values, steps):
-    return spread_pairs(values, 4, -1.0)
-
-
-def adjoint_kernel(sec_ref, x_ref, lat_ref, inv_ref, w_ref, coeff_ref, out_ref, lhs_ref, z_ref):
-    turn = pl.program_id(0)
+            out_ref[s] = results[s].astype(BF16)
+
+
+def adjoint_kernel(
+    extra, sec_ref, x_ref, lat_ref, inv_ref, all_ref, coeff_ref, out_ref, weights_ref,
+    lhs_ref, z_ref, sems
+):
+    chunk = weight_copies(sec_ref, all_ref, weights_ref, sems)
     channels = x_ref.shape[-1]
-
-    @pl.when(turn == 0)
-    def _():
-        value = dot(lat_ref[...], x_ref[...]).astype(BF16)
-        coeff_ref[...] = value
-        for n, part in enumerate(spread_pairs(value.astype(F32), 8, 1.0)):
-            lhs_ref[:, n * channels : (n + 1) * channels] = part
-
-    pairs = w_ref.shape[0] * w_ref.shape[1]
-    here = pairs // 8
-    weights = w_ref[...].reshape(here, 8, 2, channels, channels)
-    for g in range(here):
-        at = pl.multiple_of((turn * here + g) * 16, 16)
-        mixed = jnp.zeros((16, channels), F32)
-        for t in range(8):
-            left = lhs_ref[pl.ds(at, 16), 2 * t * channels : (2 * t + 2) * channels]
-            right = jnp.concatenate([weights[g, t, 0], weights[g, t, 1]], axis=1)
-            mixed = mixed + dot(left, right, ((1,), (1,)))
-        z_ref[pl.ds(at, 16), :] = mixed
-
-    @pl.when(turn == pl.num_programs(0) - 1)
-    def _():
-        out_ref[...] = dot(inv_ref[...], z_ref[...].astype(BF16)).astype(BF16)
+    groups = lat_ref.shape[0] // 16
+    if extra:
+        wide = x_ref[...].astype(F32)
+        size = wide.shape[1] - extra
+        sums = jnp.sum(wide[:, size:], axis=0)
+        x = wide[:, :size].reshape(-1, channels).astype(BF16)
+    else:
+        x = x_ref[...]
+    value = dot(lat_ref[...], x).astype(BF16)
+    coeff_ref[...] = value
+    for n, part in enumerate(spread_pairs(value.astype(F32), 8, 1.0)):
+        lhs_ref[:, n * channels : (n + 1) * channels] = part
+
+    block = weights_ref.shape[0] // sems.shape[0]
+    per_chunk = groups // sems.shape[0]
+
+    @pl.loop(0, sems.shape[0])
+    def _(n):
+        chunk(n).wait()
+        here = weights_ref[pl.ds(n * block, block)].reshape(per_chunk, 8, 2, channels, channels)
+        for g in range(per_chunk):
+            at = pl.multiple_of((n * per_chunk + g) * 16, 16)
+            mixed = jnp.zeros((16, channels), F32)
+            for t in range(8):
+                left = lhs_ref[pl.ds(at, 16), 2 * t * channels : (2 * t + 2) * channels]
+                right = jnp.concatenate([here[g, t, 0], here[g, t, 1]], axis=1)
+                mixed = mixed + dot(left, right, ((1,), (1,)))
+            z_ref[pl.ds(at, 16), :] = mixed
+
+    result = dot(inv_ref[...], z_ref[...].astype(BF16))
+    if extra:
+        count = out_ref.shape[0]
+        result = result.reshape(count, -1, channels)
+        sums = jnp.broadcast_to(sums[None], (count, extra, channels))
+        result = jnp.concatenate([result, sums], axis=1)
+    out_ref[...] = result.astype(BF16)
 
 
 def slope_kernel(
@@ -251,6 +288,8 @@
 def turn_kernel(
     packed,
     devices,
+    row_devs,
+    last,
     sec_ref,
     recv_ref,
     carried_ref,
@@ -266,7 +305,9 @@
     send_ref,
     acc_ref,
 ):
-    rows, cells, channels = carried_ref.shape
+    rows, cells, channels = prev_ref.shape
+    carried_ref = carried_ref.at[0]
+    here = grad_ref.at[1 if last else 0]
     modes = unpack_rows(recv_ref[...], range(rows), packed)
     mixing = mix_ref[...]
     tile = 256
@@ -276,43 +317,82 @@
         lows = []
         for r in range(rows):
             grad = gradient_tile(r, w, tile, spread, carried_ref, prev_ref, mixing)
-            grad_ref[r, w : w + tile, :] = grad
+            here[r, w : w + tile, :] = grad
             low, term = finish_tile(r, w, tile, grad, slope_ref, state_ref, low_ref)
+            if last:
+                base = grad.astype(F32) + dot(low, mixing, ((1,), (1,)))
+                grad_ref[0, r, w : w + tile, :] = base.astype(BF16)
             lows.append(low)
             acc = acc + term
         part = dot(synth_ref[:, w : w + tile], jnp.concatenate(lows, axis=1))
         spec = part if spec is None else spec + part
     acc_ref[...] = acc
-    send_ref[...] = pack_rows(spec, rows, packed, devices)
-
-
-def last_kernel(packed, recv_ref, carried_ref, prev_ref, basis_ref, mix_ref, grad_ref):
-    rows, cells, channels = carried_ref.shape
-    modes = unpack_rows(recv_ref[...], range(rows), packed)
-    mixing = mix_ref[...]
+    if last and packed:
+        parts = [
+            spec[:, r * channels : (r + 1) * channels].reshape(devices, 8, channels)
+            for r in range(rows)
+        ]
+        terms = acc.reshape(row_devs, channels // row_devs, channels)
+        parts.append(jnp.concatenate([terms] * (devices // row_devs), axis=0))
+        send_ref[...] = jnp.concatenate(parts, axis=1).astype(BF16)
+    else:
+        send_ref[...] = pack_rows(spec, rows, packed, devices)
+
+
+def close_kernel(
+    packed, sec_ref, *refs
+):
+    count = (len(refs) - 2) // 2
+    piece_refs, mode_refs = refs[:count], refs[count : 2 * count]
+    basis_ref, out_ref = refs[2 * count :]
+    turn = pl.program_id(0)
+    rows, cells, channels = out_ref.shape
     tile = 256
-    for w in range(0, cells, tile):
-        spread = dot(basis_ref[w : w + tile, :], modes)
-        for r in range(rows):
-            grad_ref[r, w : w + tile, :] = gradient_tile(
-                r, w, tile, spread, carried_ref, prev_ref, mixing
-            )
-
-
-def weight_kernel(steps, *refs):
-    coeff_ref, cot_refs, out_ref = refs[0], refs[1 : 1 + steps], refs[1 + steps]
+
+    for d in range(count):
+
+        @pl.when((turn == d) & (sec_ref[0] != 0))
+        def _():
+            out_ref[...] = piece_refs[d][...]
+
+        @pl.when((turn == d) & (sec_ref[0] == 0))
+        def _():
+            if packed:
+                wides = [ref[...].astype(F32) for ref in mode_refs]
+                modes = []
+                for r in range(rows):
+                    at = (d * rows + r) * 8
+                    parts = [wide[:, at : at + 8].reshape(-1, channels) for wide in wides]
+                    modes.append(jnp.concatenate(parts, axis=0))
+                modes = jnp.concatenate(modes, axis=1).astype(BF16)
+            else:
+                modes = []
+                for r in range(rows):
+                    parts = [ref[d * rows + r].astype(F32) for ref in mode_refs]
+                    modes.append(jnp.concatenate(parts, axis=0))
+                modes = jnp.concatenate(modes, axis=1).astype(BF16)
+            for w in range(0, cells, tile):
+                spread = dot(basis_ref[w : w + tile, :], modes)
+                for r in range(rows):
+                    base = piece_refs[d][r, w : w + tile, :].astype(F32)
+                    total = base + spread[:, r * channels : (r + 1) * channels]
+                    out_ref[r, w : w + tile, :] = total.astype(BF16)
+
+
+def weight_kernel(steps, sec_ref, early_ref, late_ref, out_ref):
     channels = out_ref.shape[-1]
-    tall = coeff_ref.shape[2]
+    tall = early_ref.shape[2]
     groups = tall // 8
-    left = jnp.concatenate(
-        [coeff_ref[s, 0].astype(F32).reshape(groups, 8, channels) for s in range(steps)], axis=1
-    )
-    right = jnp.concatenate(
-        [ref[0].astype(F32).reshape(groups, 8, channels) for ref in cot_refs], axis=1
-    )
+    lefts = [early_ref[0, s] for s in range(steps)]
+    rights = [early_ref[0, steps + s] for s in range(steps - 1)] + [late_ref[0]]
+    rights = [rights[-1]] + rights[:-1]
+
+    def tallied(values):
+        wide = [v.astype(F32).reshape(groups, 8, channels) for v in values]
+        return jnp.concatenate(wide, axis=1).reshape(groups * steps * 8, channels)
+
     span = steps * 8
-    left = left.reshape(groups * span, channels)
-    right = right.reshape(groups * span, channels)
+    left, right = tallied(lefts), tallied(rights)
     ids = lax.broadcasted_iota(jnp.int32, right.shape, 0)
     turned = jnp.where(
         ids % 2 == 0,
@@ -337,7 +417,7 @@
 
 
 def call(kernel, outs, in_specs, operands, grid=(1,), out_specs=None, scratch=(), prefetch=None,
-         flops=0, moved=0):
+         flops=0, moved=0, aliases=None):
     if out_specs is None:
         out_specs = [whole(o.shape) for o in outs]
     count = 0 if prefetch is None else 1
@@ -352,6 +432,7 @@
             out_specs=out_specs,
             scratch_shapes=list(scratch),
         ),
+        input_output_aliases=aliases or {},
         compiler_params=pltpu.CompilerParams(
             vmem_limit_bytes=VMEM_LIMIT, dimension_semantics=("arbitrary",) * len(grid)
         ),
@@ -395,18 +476,20 @@
     shared_np = lat_matrices(row_order, freqs, lat_cells, modes)
     lat_shared = jnp.asarray(shared_np, BF16)
     inv_shared = jnp.asarray(shared_np.T, BF16)
+    inv_plain = jnp.asarray(lat_matrices(np.arange(lat_cells), freqs, lat_cells, modes).T, BF16)
     mode_rows = lat_plain.shape[0]
     grid_rows = lat_plain.shape[1]
 
     def exchange(values):
         return lax.all_to_all(values, ALL, 0, 0, tiled=True)
+
+    def share(piece, d):
+        return lax.ppermute(piece, "section", [(i, i ^ d) for i in range(sections)])
 
     own = states[0].reshape(sections, rows, cells, channels)
     pieces = [lax.dynamic_index_in_dim(own, section, 0, False)]
     for d in range(1, sections):
-        piece = lax.dynamic_index_in_dim(own, section ^ d, 0, False)
-        pieces.append(lax.ppermute(piece, "section", [(i, i ^ d) for i in range(sections)]))
-    all_states = jnp.stack(pieces, 0)
+        pieces.append(share(lax.dynamic_index_in_dim(own, section ^ d, 0, False), d))
 
     total = basis_t.shape[0]
     out_shape = (devices, rows_here * 8, channels) if packed else (rows_here, total, channels)
@@ -420,31 +503,43 @@
     )
     if not packed:
         spectra = outer_pack(spectra, devices)
-    gathered = exchange(spectra).reshape(sections * grid_rows, channels)
-
-    block_j = max(1, min(freqs, 32 // modes))
-    weight_block = (block_j, modes, 2, channels, channels)
-    weight_spec = pl.BlockSpec(weight_block, lambda b, s: (b, s[0], 0, 0, 0))
+    gathered = exchange(spectra)
+    gathered, *pieces = lax.optimization_barrier((gathered, *pieces))
+    gathered = gathered.reshape(sections * grid_rows, channels)
+    all_states = jnp.stack(pieces, 0)
+
+    chunk_j = max(1, min(freqs, CHUNK // modes))
+    weight_scratch = [pltpu.VMEM((freqs, modes, 2, channels, channels), BF16)]
+    weight_sems = [pltpu.SemaphoreType.DMA((freqs // chunk_j,))]
+    weight_spec = pl.BlockSpec(memory_space=pl.ANY)
     weight_bytes = 4 * freqs * modes * channels * channels
+    mixed_shape = (
+        (devices, sections * rows * parts, channels)
+        if packed
+        else (sections, grid_rows, channels)
+    )
     coeffs, mixed = call(
-        functools.partial(mix_kernel, sections),
+        functools.partial(mix_kernel, sections, packed),
         [
             jax.ShapeDtypeStruct((sections, mode_rows, channels), BF16),
-            jax.ShapeDtypeStruct((sections, grid_rows, channels), BF16),
+            jax.ShapeDtypeStruct(mixed_shape, BF16),
         ],
         [whole(gathered.shape), whole(lat_plain.shape), whole(inv_shared.shape), weight_spec],
         (gathered, lat_plain, inv_shared, spec_weights),
-        grid=(freqs // block_j,),
-        scratch=[
+        scratch=weight_scratch
+        + [
             pltpu.VMEM((sections * mode_rows, 8 * channels), BF16),
             pltpu.VMEM((sections, mode_rows, channels), F32),
-        ],
+        ]
+        + weight_sems,
         prefetch=sec,
         flops=4 * weight_bytes,
         moved=weight_bytes,
     )
-    mixed = mixed.reshape(sections, devices, rows * parts, channels).transpose(1, 0, 2, 3)
-    back = exchange(mixed.reshape(devices, sections * rows * parts, channels))
+    if not packed:
+        mixed = mixed.reshape(sections, devices, rows * parts, channels).transpose(1, 0, 2, 3)
+        mixed = mixed.reshape(devices, sections * rows * parts, channels)
+    back = exchange(mixed)
     if not packed:
         back = outer_unpack(back, sections * rows)
 
@@ -490,125 +585,151 @@
         flops=2 * total * cells * rows * channels,
         moved=10 * rows * cells * channels,
     )
-    grads = [None] * sections
     cots = [None] * sections
-    slot = -(-channels // devices)
+    slot = channels // row_devs
+    store = carried[None]
+    store_shape = (sections,) + shape3
     for s in range(sections - 1, -1, -1):
-        if not packed:
+        extra = 0
+        if s == 0:
+            extra = slot
+            if not packed:
+                terms = acc.reshape(row_devs, slot, channels).astype(BF16)
+                terms = jnp.concatenate([terms] * sections, axis=0)
+                send = jnp.concatenate([outer_pack(send, devices), terms], axis=1)
+        elif not packed:
             send = outer_pack(send, devices)
-        if s == 0:
-            terms = jnp.pad(acc, ((0, slot * devices - channels), (0, 0)))
-            terms = terms.reshape(devices, slot, channels)
-            high = terms.astype(BF16)
-            rest = (terms - high.astype(F32)).astype(BF16)
-            send = jnp.concatenate([send, high, rest], axis=1)
         got = exchange(send)
-        if s == 0:
+        if extra and not packed:
             sums = jnp.sum(got[:, rows * parts :].astype(F32), 0)
-            sums = sums[:slot] + sums[slot:]
             got = got[:, : rows * parts]
+        inside = extra if packed else 0
+        if not inside:
+            got = got.reshape(grid_rows, channels)
+        inner_shape = (grid_rows, channels)
+        if inside:
+            inner_shape = (row_devs, grid_rows // row_devs + extra, channels)
+        inverse = inv_shared if s > 0 else inv_plain
         cots[s], inner = call(
-            adjoint_kernel,
+            functools.partial(adjoint_kernel, inside),
             [
                 jax.ShapeDtypeStruct((mode_rows, channels), BF16),
-                jax.ShapeDtypeStruct((grid_rows, channels), BF16),
+                jax.ShapeDtypeStruct(inner_shape, BF16),
             ],
-            [
-                whole((grid_rows, channels)),
-                whole(lat_shared.shape),
-                whole(inv_shared.shape),
-                weight_spec,
-            ],
-            (got.reshape(grid_rows, channels), lat_shared, inv_shared, spec_weights),
-            grid=(freqs // block_j,),
-            scratch=[
+            [whole(got.shape), whole(lat_shared.shape), whole(inverse.shape), weight_spec],
+            (got, lat_shared, inverse, spec_weights),
+            scratch=weight_scratch
+            + [
                 pltpu.VMEM((mode_rows, 16 * channels), BF16),
                 pltpu.VMEM((mode_rows, channels), F32),
-            ],
+            ]
+            + weight_sems,
             prefetch=sec,
             flops=2 * weight_bytes,
             moved=weight_bytes,
         )
-        inner = inner.reshape(devices, rows * parts, channels)
         if s == 0:
-            high = sums.astype(BF16)
-            rest = (sums - high.astype(F32)).astype(BF16)
-            both = jnp.concatenate([high, rest], 0)
-            both = jnp.broadcast_to(both[None], (devices,) + both.shape)
-            inner = jnp.concatenate([inner, both], axis=1)
-        got = exchange(inner)
-        if s == 0:
-            both = got[:, rows * parts :].astype(F32)
-            got = got[:, : rows * parts]
-            local_total = (both[:, :slot] + both[:, slot:]).reshape(-1, channels)[:channels]
+            break
+        got = exchange(inner.reshape(devices, rows * parts, channels))
         if not packed:
             got = outer_unpack(got, rows)
-        if s > 0:
-            grads[s], low, send, acc = call(
-                functools.partial(turn_kernel, packed, devices),
-                [jax.ShapeDtypeStruct(shape3, BF16)] + turn_outs,
-                [
-                    whole(got.shape),
-                    whole(shape3),
-                    whole(shape3),
-                    whole(shape3),
-                    state_spec(s - 1),
-                    whole(basis.shape),
-                    whole(synth.shape),
-                    whole(local_weight.shape),
-                    whole(acc.shape),
-                ],
-                (got, carried, low, slopes[s - 1], all_states, basis, synth, local_weight, acc),
-                prefetch=sec,
-                flops=4 * total * cells * rows * channels,
-                moved=16 * rows * cells * channels,
-            )
-            carried = grads[s]
-        else:
-            (grads[0],) = call(
-                functools.partial(last_kernel, packed),
-                [jax.ShapeDtypeStruct(shape3, BF16)],
-                [
-                    whole(got.shape),
-                    whole(shape3),
-                    whole(shape3),
-                    whole(basis.shape),
-                    whole(local_weight.shape),
-                ],
-                (got, carried, low, basis, local_weight),
-                flops=2 * total * cells * rows * channels,
-                moved=8 * rows * cells * channels,
-            )
-
+        last = s == 1
+        first = s == sections - 1
+        if last and packed:
+            turn_outs[1] = jax.ShapeDtypeStruct((devices, rows * 8 + slot, channels), BF16)
+        carried_at = 0 if first else s + 1
+        span = 2 if last else 1
+        grad_at = 0 if last else s
+        store, low, send, acc = call(
+            functools.partial(turn_kernel, packed, devices, row_devs, last),
+            [jax.ShapeDtypeStruct(store_shape, BF16)] + turn_outs,
+            [
+                whole(got.shape),
+                pl.BlockSpec(field_block, functools.partial(lambda n, *_: (n, 0, 0, 0), carried_at)),
+                whole(shape3),
+                whole(shape3),
+                state_spec(s - 1),
+                whole(basis.shape),
+                whole(synth.shape),
+                whole(local_weight.shape),
+                whole(acc.shape),
+            ],
+            (got, store, low, slopes[s - 1], all_states, basis, synth, local_weight, acc),
+            out_specs=[
+                pl.BlockSpec(
+                    (span,) + shape3, functools.partial(lambda n, *_: (n, 0, 0, 0), grad_at)
+                )
+            ]
+            + [whole(o.shape) for o in turn_outs],
+            prefetch=sec,
+            aliases={} if first else {2: 0},
+            flops=4 * total * cells * rows * channels,
+            moved=16 * rows * cells * channels,
+        )
+
+    parts_of = [lax.dynamic_index_in_dim(store, section, 0, False)]
+    for d in range(1, sections):
+        parts_of.append(share(lax.dynamic_index_in_dim(store, section ^ d, 0, False), d))
+
+    part = mode_rows // sections
+
+    def gather_modes(values):
+        mine = [lax.dynamic_index_in_dim(values, section ^ d, 0, False) for d in range(sections)]
+        return jnp.stack([mine[0]] + [share(mine[d], d) for d in range(1, sections)], 0)
+
+    early = jnp.concatenate([coeffs, jnp.stack(cots[1:], 0)], 0)
+    early = early.reshape(-1, sections, part, channels).swapaxes(0, 1)
+    early = gather_modes(early)
+
+    if not packed:
+        inner = inner.reshape(row_devs, grid_rows // row_devs, channels)
+        both = jnp.broadcast_to(sums.astype(BF16)[None], (row_devs, slot, channels))
+        inner = jnp.concatenate([inner, both], axis=1)
+    got = lax.all_to_all(inner, "row", 0, 0, tiled=True)
+    size = grid_rows // row_devs
+    local_total = got[:, size:].reshape(channels, channels).astype(F32)
     d_local = local_total * lax.rsqrt(jnp.float32(sections * lat_cells * cells))
-
-    part = mode_rows // sections
-
-    def to_sections(values, axis):
-        return lax.all_to_all(values, "section", axis, axis, tiled=True)
-
-    step_coeffs = to_sections(coeffs.reshape(sections, sections, part, channels), 1)
-    step_cots = [to_sections(c.reshape(sections, part, channels), 0) for c in cots]
+    if not packed:
+        got = outer_unpack(got[:, :size], rows_here)
+    mode_parts = [got] + [
+        lax.ppermute(got, "section", [(d, 0)]) for d in range(1, sections)
+    ]
+
+    late = gather_modes(cots[0].reshape(sections, part, channels))
     own_freqs = freqs // sections
     own_j = max(1, min(own_freqs, 32 // modes))
     tall = own_j * parts
     (d_spectral,) = call(
         functools.partial(weight_kernel, sections),
         [jax.ShapeDtypeStruct((own_freqs, row_modes, 2, channels, channels), BF16)],
-        [pl.BlockSpec((sections, 1, tall, channels), lambda a, b: (0, a, b, 0))]
-        + [pl.BlockSpec((1, tall, channels), lambda a, b: (a, b, 0))] * sections,
-        (step_coeffs, *step_cots),
+        [
+            pl.BlockSpec((1, 2 * sections - 1, tall, channels), lambda a, b, i: (a, 0, b, 0)),
+            pl.BlockSpec((1, tall, channels), lambda a, b, i: (a, b, 0)),
+        ],
+        (early, late),
         grid=(sections, own_freqs // own_j),
         out_specs=[
-            pl.BlockSpec((own_j, modes, 2, channels, channels), lambda a, b: (b, a, 0, 0, 0))
+            pl.BlockSpec(
+                (own_j, modes, 2, channels, channels), lambda a, b, i: (b, i[0] ^ a, 0, 0, 0)
+            )
         ],
+        prefetch=sec,
         flops=8 * weight_bytes,
         moved=weight_bytes,
     )
 
-    grad_states = lax.all_to_all(jnp.stack(grads, 0), "section", 0, 0, tiled=True)
-    grad_states = grad_states.reshape(1, rows_here, cells, channels)
-    return (grad_states, d_spectral, d_local)
+    (grad_states,) = call(
+        functools.partial(close_kernel, packed),
+        [jax.ShapeDtypeStruct((rows_here, cells, channels), BF16)],
+        [whole(shape3)] * sections + [whole(got.shape)] * sections + [whole(basis.shape)],
+        (*parts_of, *mode_parts, basis),
+        grid=(sections,),
+        out_specs=[pl.BlockSpec(shape3, lambda d, i: (i[0] ^ d, 0, 0))],
+        prefetch=sec,
+        flops=2 * total * cells * rows_here * channels,
+        moved=8 * rows_here * cells * channels,
+    )
+    return (grad_states[None], d_spectral, d_local)
 
 
 def solution(mesh):

time: 344 us -> 284 us (0.83)
  waiting for transfers between devices: 103 us -> 80.2 us
  blocking collectives: 50.2 us -> 36.1 us
  Pallas kernels: 109 us -> 99.4 us
  starting transfers between devices: 48.2 us -> 44 us
  local copies, waits for them, and re-layouts: 18.1 us -> 13.9 us
  other arithmetic: 12.1 us -> 8.06 us
    all_to_all x6 -> x1, waiting for transfers between devices: 25.5 us -> 0.01 us  [local(): got = lax.all_to_all(inner, 'row', 0, 0, tiled=True)]
    all_to_all x6 -> x1, starting transfers between devices: 24 us -> 3.41 us  [local(): got = lax.all_to_all(inner, 'row', 0, 0, tiled=True)]
    ppermute x3 -> x15, starting transfers between devices: 3.49 us -> 18.3 us  [the longest x12 14.4 us: share(): return lax.ppermute(piece, 'section', [(i, i ^ d) for i in range(sections)])]
    all_to_all x4 -> x3, blocking collectives: 50.2 us -> 36.1 us  [exchange(): return lax.all_to_all(values, ALL, 0, 0, tiled=True)]
    ppermute x3 -> x15, waiting for transfers between devices: 30.9 us -> 45 us  [the longest x12 45 us: share(): return lax.ppermute(piece, 'section', [(i, i ^ d) for i in range(sections)])]
    all_to_all x6, waiting for transfers between devices: 46.4 us -> 35.2 us  [exchange(): return lax.all_to_all(values, ALL, 0, 0, tiled=True)]
    pallas_call x16, Pallas kernels: 109 us -> 99.4 us  [call(): pl.pallas_call(kernel, out_shape=outs, grid_spec=pltpu.PrefetchScalarGrid...]
    squeeze x0 -> x2, local copies, waits for them, and re-layouts: none -> 4.04 us  [the longest x1 2.57 us: local(): lax.dynamic_index_in_dim(own, section ^ d, 0, False)]
  transfers between devices with their start and end apart: 15 -> 22, of which waited for: 13 -> 10; matrix products, arithmetic and copies ran while one was open for 5% -> 6% of each run, Pallas kernels for 10% -> 11%
where the time goes in v2:
time: 284 us; the launch traced here: 283 us
  Pallas kernels  99.4 us (35%)
  waiting for transfers between devices  80.2 us (28%)
  starting transfers between devices  44 us (15%)
  blocking collectives  36.1 us (13%)
  local copies, waits for them, and re-layouts  13.9 us (5%)
  other arithmetic  8.06 us (3%)
    pallas_call x16, Pallas kernels, call(): pl.pallas_call(kernel, out_shape=outs, grid_spec=pltpu.PrefetchScalarGrid...  99.4 us
    ppermute x12, waiting for transfers between devices, share(): return lax.ppermute(piece, 'section', [(i, i ^ d) for i in range(sections)])  45 us
    all_to_all x3, blocking collectives, exchange(): return lax.all_to_all(values, ALL, 0, 0, tiled=True)  36.1 us
    all_to_all x6, waiting for transfers between devices, exchange(): return lax.all_to_all(values, ALL, 0, 0, tiled=True)  35.2 us
    all_to_all x6, starting transfers between devices, exchange(): return lax.all_to_all(values, ALL, 0, 0, tiled=True)  22.3 us
    ppermute x12, starting transfers between devices, share(): return lax.ppermute(piece, 'section', [(i, i ^ d) for i in range(sections)])  14.4 us
    unnamed x36, local copies, waits for them, and re-layouts  6.38 us
  transfers between devices with their start and end apart: 22, of which 10 were waited for; matrix products, arithmetic and copies ran while one was open for 6% of the time, Pallas kernels for 11%

profile of v2, /device:TPU:0, one launch (start us, length us, event | category | flops | bytes accessed | tf_op | source)
XLA Modules:
  0.0 282.5 jit_solution(16295463222204571243)
XLA Ops:
  0.6 3.5 %shard_map.148 = bf16[32,96,128]{2,1,0:T(8,128)(2,1)} custom-call(bf16[12,768,128]{2,1,0:T(8,128)(2,1)} %bitcast.66, bf16[256,768]{1,0:T(8,128)(2,1)} %constant.73.clone.basis_ref), custom_call_target="tpu_custom_call" | custom-call | flops 603979776 | bytes 4718592 | tf_op jit(solution)/shard_map/pallas_call | solution.py:425
  4.2 7.3 %all-to-all-start = ((bf16[32,96,128]{2,1,0:T(8,128)(2,1)}), bf16[32,96,128]{2,1,0:T(8,128)(2,1)S(1)}, u32[]{:S(2)}, u32[]{:S(2)}) async-start(bf16[32,96,128]{2,1,0:T(8,128)(2,1)} %shard_map.148), calls=%async_computation | async-start | bytes 1572864 | tf_op jit(solution)/shard_map/all_to_all | solution.py:484
  11.5 2.6 dynamic-slice_bitcast_fusion.4
  14.1 2.7 collective-permute-start.2
  17.6 19.9 %collective-permute-done.2 = bf16[3,768,128]{2,1,0:T(8,128)(2,1)S(1)} collective-permute-done((bf16[3,768,128]{2,1,0:T(8,128)(2,1)S(1)}, bf16[3,768,128]{2,1,0:T(8,128)(2,1)S(1)}, u32[]{:S(2)}, u32[]{:S(2)}) %collective-permute-start.2) | collective-permute-done | bytes 589856 | tf_op jit(solution)/shard_map/ppermute | solution.py:487
  37.4 11.2 %collective-permute-done.1 = bf16[3,768,128]{2,1,0:T(8,128)(2,1)S(1)} collective-permute-done((bf16[3,768,128]{2,1,0:T(8,128)(2,1)S(1)}, bf16[3,768,128]{2,1,0:T(8,128)(2,1)S(1)}, u32[]{:S(2)}, u32[]{:S(2)}) %collective-permute-start.1) | collective-permute-done | bytes 589856 | tf_op jit(solution)/shard_map/ppermute | solution.py:487
  48.6 0.8 copy-done.11
  49.5 0.9 copy-done.3
  50.3 10.0 %shard_map.149 = (bf16[4,512,128]{2,1,0:T(8,128)(2,1)}, bf16[32,96,128]{2,1,0:T(8,128)(2,1)}) custom-call(s32[1]{0:T(128)} %bitcast.sec_ref, bf16[3072,128]{1,0:T(8,128)(2,1)} %bitcast.68, bf16[512,768]{1,0:T(8,128)(2,1)} %constant.76.clone.lat_ref, bf16[768,512]{1,0:T(8,128)(2,1)} %constant.78.clone.inv_ref, bf16[64,16,2,128,128]{4,3,2,1,0:T(8,128)(2,1)} %all_ref.9), custom_call_target="tpu_custom_call" | custom-call | flops 67108864 | bytes 16777216 | tf_op jit(solution)/shard_map/pallas_call | solution.py:425
  60.4 4.2 %all-to-all-start.1 = ((bf16[32,96,128]{2,1,0:T(8,128)(2,1)}), bf16[32,96,128]{2,1,0:T(8,128)(2,1)S(1)}, u32[]{:S(2)}, u32[]{:S(2)}) async-start(bf16[32,96,128]{2,1,0:T(8,128)(2,1)} %get-tuple-element.32), calls=%async_computation.1 | async-start | bytes 1572864 | tf_op jit(solution)/shard_map/all_to_all | solution.py:484
  64.6 0.9 constant_dynamic-slice_fusion.1.cot_ref
  65.5 3.3 %pad_maximum_fusion.state_ref = bf16[4,3,768,128]{3,2,1,0:T(8,128)(2,1)} fusion(bf16[1,3,768,128]{3,2,1,0:T(8,128)(2,1)} %bitcast.74, bf16[1,3,768,128]{3,2,1,0:T(8,128)(2,1)} %bitcast.75, bf16[1,3,768,128]{3,2,1,0:T(8,128)(2,1)} %bitcast.9, bf16[1,3,768,128]{3,2,1,0:T(8,128)(2,1)} %bitcast.70), kind=kLoop, calls=%fused_computation | loop fusion | flops 3538944 | bytes 4718592 | tf_op jit(solution)/shard_map/stack | solution.py:509
  68.8 17.8 %all-to-all-done.1.recv_ref = bf16[32,96,128]{2,1,0:T(8,128)(2,1)S(1)} async-done(((bf16[32,96,128]{2,1,0:T(8,128)(2,1)}), bf16[32,96,128]{2,1,0:T(8,128)(2,1)S(1)}, u32[]{:S(2)}, u32[]{:S(2)}) %all-to-all-start.1) | async-done | bytes 786464 | tf_op jit(solution)/shard_map/all_to_all | solution.py:484
  86.6 0.9 copy-done.2
  87.5 3.4 %shard_map.150.slope_ref = f32[3,768,128]{2,1,0:T(8,128)} custom-call(s32[1]{0:T(128)} %bitcast.sec_ref, bf16[32,96,128]{2,1,0:T(8,128)(2,1)} %copy-done.2, bf16[4,3,768,128]{3,2,1,0:T(8,128)(2,1)} %pad_maximum_fusion.state_ref, bf16[768,256]{1,0:T(8,128)(2,1)} %constant.75.clone.synth_ref, bf16[128,128]{1,0:T(8,128)(2,1)} %mix_ref.13, f32[1,128]{1,0:T(1,128)} %bitcast.88), custom_call_target="tpu_custom_call" | custom-call | flops 150994944 | bytes 2949120 | tf_op jit(solution)/shard_map/pallas_call | solution.py:425
  90.9 3.0 %shard_map.151 = (bf16[3,768,128]{2,1,0:T(8,128)(2,1)}, bf16[32,24,128]{2,1,0:T(8,128)(2,1)}, f32[128,128]{1,0:T(8,128)}) custom-call(s32[1]{0:T(128)} %bitcast.sec_ref, bf16[3,768,128]{2,1,0:T(8,128)(2,1)} %constant_dynamic-slice_fusion.1.cot_ref, f32[3,768,128]{2,1,0:T(8,128)} %shard_map.150.slope_ref, bf16[4,3,768,128]{3,2,1,0:T(8,128)(2,1)} %pad_maximum_fusion.state_ref, ...), custom_call_target="tpu_custom_call" | custom-call | flops 150994944 | bytes 2949120 | tf_op jit(solution)/shard_map/pallas_call | solution.py:425
  93.8 12.0 %all_to_all.50 = bf16[32,24,128]{2,1,0:T(8,128)(2,1)} all-to-all(bf16[32,24,128]{2,1,0:T(8,128)(2,1)} %get-tuple-element.37), channel_id=1, replica_groups=mesh['section'=4,'row'=8] {'section','row'}, dimensions={0} | all-to-all | bytes 393216 | tf_op jit(solution)/shard_map/all_to_all | solution.py:484
  105.9 10.1 %shard_map.152 = (bf16[512,128]{1,0:T(8,128)(2,1)}, bf16[768,128]{1,0:T(8,128)(2,1)}) custom-call(s32[1]{0:T(128)} %bitcast.sec_ref, bf16[768,128]{1,0:T(8,128)(2,1)} %bitcast.72, bf16[512,768]{1,0:T(8,128)(2,1)} %constant.77.clone.lat_ref, bf16[768,512]{1,0:T(8,128)(2,1)} %constant.78.clone.inv_ref, bf16[64,16,2,128,128]{4,3,2,1,0:T(8,128)(2,1)} %all_ref.9), custom_call_target="tpu_custom_call" | custom-call | flops 33554432 | bytes 16777216 | tf_op jit(solution)/shard_map/pallas_call | solution.py:425
  116.0 2.6 all-to-all-start.3
  118.6 0.9 fusion.carried_ref
  119.4 3.4 %shard_map.153.slope_ref = f32[3,768,128]{2,1,0:T(8,128)} custom-call(s32[1]{0:T(128)} %bitcast.sec_ref, bf16[32,96,128]{2,1,0:T(8,128)(2,1)} %copy-done.2, bf16[4,3,768,128]{3,2,1,0:T(8,128)(2,1)} %pad_maximum_fusion.state_ref, bf16[768,256]{1,0:T(8,128)(2,1)} %constant.75.clone.synth_ref, bf16[128,128]{1,0:T(8,128)(2,1)} %mix_ref.13, f32[1,128]{1,0:T(1,128)} %bitcast.89), custom_call_target="tpu_custom_call" | custom-call | flops 150994944 | bytes 2949120 | tf_op jit(solution)/shard_map/pallas_call | solution.py:425
  122.9 4.5 %all-to-all-done.3.recv_ref = bf16[32,24,128]{2,1,0:T(8,128)(2,1)S(1)} async-done(((bf16[32,24,128]{2,1,0:T(8,128)(2,1)}), bf16[32,24,128]{2,1,0:T(8,128)(2,1)S(1)}, u32[]{:S(2)}, u32[]{:S(2)}) %all-to-all-start.3) | async-done | bytes 196640 | tf_op jit(solution)/shard_map/all_to_all | solution.py:484
  127.3 0.7 copy-done.6
  128.0 4.1 %shard_map.154 = (bf16[4,3,768,128]{3,2,1,0:T(8,128)(2,1)}, bf16[3,768,128]{2,1,0:T(8,128)(2,1)}, bf16[32,24,128]{2,1,0:T(8,128)(2,1)}, f32[128,128]{1,0:T(8,128)}) custom-call(s32[1]{0:T(128)} %bitcast.sec_ref, bf16[32,24,128]{2,1,0:T(8,128)(2,1)} %copy-done.6, bf16[1,3,768,128]{3,2,1,0:T(8,128)(2,1)} %fusion.carried_ref, ...), custom_call_target="tpu_custom_call" | custom-call | flops 301989888 | bytes 4718592 | tf_op jit(solution)/shard_map/pallas_call | solution.py:425
  132.1 12.0 %all_to_all.51 = bf16[32,24,128]{2,1,0:T(8,128)(2,1)} all-to-all(bf16[32,24,128]{2,1,0:T(8,128)(2,1)} %get-tuple-element.41), channel_id=1, replica_groups=mesh['section'=4,'row'=8] {'section','row'}, dimensions={0} | all-to-all | bytes 393216 | tf_op jit(solution)/shard_map/all_to_all | solution.py:484
  144.1 10.1 %shard_map.155 = (bf16[512,128]{1,0:T(8,128)(2,1)}, bf16[768,128]{1,0:T(8,128)(2,1)}) custom-call(s32[1]{0:T(128)} %bitcast.sec_ref, bf16[768,128]{1,0:T(8,128)(2,1)} %bitcast.73, bf16[512,768]{1,0:T(8,128)(2,1)} %constant.77.clone.lat_ref, bf16[768,512]{1,0:T(8,128)(2,1)} %constant.78.clone.inv_ref, bf16[64,16,2,128,128]{4,3,2,1,0:T(8,128)(2,1)} %all_ref.9), custom_call_target="tpu_custom_call" | custom-call | flops 33554432 | bytes 16777216 | tf_op jit(solution)/shard_map/pallas_call | solution.py:425
  154.2 2.8 all-to-all-start.5
  157.0 3.4 %shard_map.156.slope_ref = f32[3,768,128]{2,1,0:T(8,128)} custom-call(s32[1]{0:T(128)} %bitcast.sec_ref, bf16[32,96,128]{2,1,0:T(8,128)(2,1)} %copy-done.2, bf16[4,3,768,128]{3,2,1,0:T(8,128)(2,1)} %pad_maximum_fusion.state_ref, bf16[768,256]{1,0:T(8,128)(2,1)} %constant.75.clone.synth_ref, bf16[128,128]{1,0:T(8,128)(2,1)} %mix_ref.13, f32[1,128]{1,0:T(1,128)} %bitcast.90), custom_call_target="tpu_custom_call" | custom-call | flops 150994944 | bytes 2949120 | tf_op jit(solution)/shard_map/pallas_call | solution.py:425
  160.5 5.1 %all-to-all-done.5.recv_ref = bf16[32,24,128]{2,1,0:T(8,128)(2,1)S(1)} async-done(((bf16[32,24,128]{2,1,0:T(8,128)(2,1)}), bf16[32,24,128]{2,1,0:T(8,128)(2,1)S(1)}, u32[]{:S(2)}, u32[]{:S(2)}) %all-to-all-start.5) | async-done | bytes 196640 | tf_op jit(solution)/shard_map/all_to_all | solution.py:484
  165.6 0.7 copy-done.8
  166.3 4.1 %shard_map.157 = (bf16[4,3,768,128]{3,2,1,0:T(8,128)(2,1)}, bf16[3,768,128]{2,1,0:T(8,128)(2,1)}, bf16[32,24,128]{2,1,0:T(8,128)(2,1)}, f32[128,128]{1,0:T(8,128)}) custom-call(s32[1]{0:T(128)} %bitcast.sec_ref, bf16[32,24,128]{2,1,0:T(8,128)(2,1)} %copy-done.8, ...), custom_call_target="tpu_custom_call", output_to_operand_aliasing={{0}: (2, {})} | custom-call | flops 301989888 | bytes 4718592 | tf_op jit(solution)/shard_map/pallas_call | solution.py:425
  170.3 12.0 %all_to_all.52 = bf16[32,24,128]{2,1,0:T(8,128)(2,1)} all-to-all(bf16[32,24,128]{2,1,0:T(8,128)(2,1)} %get-tuple-element.46), channel_id=1, replica_groups=mesh['section'=4,'row'=8] {'section','row'}, dimensions={0} | all-to-all | bytes 393216 | tf_op jit(solution)/shard_map/all_to_all | solution.py:484
  182.4 10.1 %shard_map.158 = (bf16[512,128]{1,0:T(8,128)(2,1)}, bf16[768,128]{1,0:T(8,128)(2,1)}) custom-call(s32[1]{0:T(128)} %bitcast.sec_ref, bf16[768,128]{1,0:T(8,128)(2,1)} %bitcast.71, bf16[512,768]{1,0:T(8,128)(2,1)} %constant.77.clone.lat_ref, bf16[768,512]{1,0:T(8,128)(2,1)} %constant.78.clone.inv_ref, bf16[64,16,2,128,128]{4,3,2,1,0:T(8,128)(2,1)} %all_ref.9), custom_call_target="tpu_custom_call" | custom-call | flops 33554432 | bytes 16777216 | tf_op jit(solution)/shard_map/pallas_call | solution.py:425
  192.4 2.6 all-to-all-start.7
  195.1 3.4 %shard_map.159.slope_ref = f32[3,768,128]{2,1,0:T(8,128)} custom-call(s32[1]{0:T(128)} %bitcast.sec_ref, bf16[32,96,128]{2,1,0:T(8,128)(2,1)} %copy-done.2, bf16[4,3,768,128]{3,2,1,0:T(8,128)(2,1)} %pad_maximum_fusion.state_ref, bf16[768,256]{1,0:T(8,128)(2,1)} %constant.75.clone.synth_ref, bf16[128,128]{1,0:T(8,128)(2,1)} %mix_ref.13, f32[1,128]{1,0:T(1,128)} %bitcast.91), custom_call_target="tpu_custom_call" | custom-call | flops 150994944 | bytes 2949120 | tf_op jit(solution)/shard_map/pallas_call | solution.py:425
  198.5 5.3 %all-to-all-done.7.recv_ref = bf16[32,24,128]{2,1,0:T(8,128)(2,1)S(1)} async-done(((bf16[32,24,128]{2,1,0:T(8,128)(2,1)}), bf16[32,24,128]{2,1,0:T(8,128)(2,1)S(1)}, u32[]{:S(2)}, u32[]{:S(2)}) %all-to-all-start.7) | async-done | bytes 196640 | tf_op jit(solution)/shard_map/all_to_all | solution.py:484
  203.8 0.7 copy-done.7
  204.5 5.6 %shard_map.160 = (bf16[4,3,768,128]{3,2,1,0:T(8,128)(2,1)}, bf16[3,768,128]{2,1,0:T(8,128)(2,1)}, bf16[32,40,128]{2,1,0:T(8,128)(2,1)}, f32[128,128]{1,0:T(8,128)}) custom-call(s32[1]{0:T(128)} %bitcast.sec_ref, bf16[32,24,128]{2,1,0:T(8,128)(2,1)} %copy-done.7, ...), custom_call_target="tpu_custom_call", output_to_operand_aliasing={{0}: (2, {})} | custom-call | flops 301989888 | bytes 4718592 | tf_op jit(solution)/shard_map/pallas_call | solution.py:425
  210.1 2.7 all-to-all-start.8
  212.8 1.3 pad_maximum_fusion.1
  214.1 0.9 dynamic-slice_bitcast_fusion.11
  215.0 2.7 collective-permute-start.11
  217.7 1.5 dynamic-slice_bitcast_fusion
  219.4 1.8 collective-permute-start.10
  221.1 1.5 collective-permute-start.9
  222.6 2.5 all-to-all-done.8.x_ref
  225.1 0.7 copy-done.4
  225.8 10.1 %shard_map.161 = (bf16[512,128]{1,0:T(8,128)(2,1)}, bf16[8,112,128]{2,1,0:T(8,128)(2,1)}) custom-call(s32[1]{0:T(128)} %bitcast.sec_ref, bf16[32,40,128]{2,1,0:T(8,128)(2,1)} %copy-done.4, bf16[512,768]{1,0:T(8,128)(2,1)} %constant.77.clone.lat_ref, bf16[768,512]{1,0:T(8,128)(2,1)} %constant.79.clone.inv_ref, bf16[64,16,2,128,128]{4,3,2,1,0:T(8,128)(2,1)} %all_ref.9), custom_call_target="tpu_custom_call" | custom-call | flops 33554432 | bytes 16777216 | tf_op jit(solution)/shard_map/pallas_call | solution.py:425
  235.9 3.4 %all-to-all-start.9 = ((bf16[8,112,128]{2,1,0:T(8,128)(2,1)}), bf16[8,112,128]{2,1,0:T(8,128)(2,1)S(1)}, u32[]{:S(2)}, u32[]{:S(2)}) async-start(bf16[8,112,128]{2,1,0:T(8,128)(2,1)} %get-tuple-element.53), calls=%async_computation.9 | async-start | bytes 458752 | tf_op jit(solution)/shard_map/all_to_all | solution.py:688
  240.4 0.8 constant_dynamic-slice_fusion
  241.2 2.3 collective-permute-done.10
  243.5 2.0 collective-permute-start.14
  245.5 0.6 collective-permute-start.13
  246.2 11.0 %collective-permute-done.14 = bf16[128,128]{1,0:T(8,128)(2,1)S(1)} collective-permute-done((bf16[128,128]{1,0:T(8,128)(2,1)S(1)}, bf16[128,128]{1,0:T(8,128)(2,1)S(1)}, u32[]{:S(2)}, u32[]{:S(2)}) %collective-permute-start.14) | collective-permute-done | bytes 32800 | tf_op jit(solution)/shard_map/ppermute | solution.py:487
  257.2 1.1 collective-permute-start.12
  258.3 2.2 pad_maximum_fusion.2.early_ref
  261.1 0.7 pad_maximum_fusion.3.late_ref
  261.8 1.3 collective-permute-start.8
  263.1 1.3 collective-permute-start.7
  264.4 1.3 collective-permute-start.6
  265.7 10.3 %shard_map.163 = bf16[16,16,2,128,128]{4,3,2,1,0:T(8,128)(2,1)} custom-call(s32[1]{0:T(128)} %bitcast.sec_ref, bf16[4,7,128,128]{3,2,1,0:T(8,128)(2,1)} %pad_maximum_fusion.2.early_ref, bf16[4,128,128]{2,1,0:T(8,128)(2,1)} %pad_maximum_fusion.3.late_ref), custom_call_target="tpu_custom_call" | custom-call | flops 134217728 | bytes 16777216 | tf_op jit(solution)/shard_map/pallas_call | solution.py:425
  276.0 0.6 convert_multiply_fusion
  276.7 0.8 copy-done.9
  277.7 4.9 %shard_map.162 = bf16[12,768,128]{2,1,0:T(8,128)(2,1)} custom-call(s32[1]{0:T(128)} %bitcast.sec_ref, bf16[3,768,128]{2,1,0:T(8,128)(2,1)} %get-tuple-element.62.refs_0_, bf16[3,768,128]{2,1,0:T(8,128)(2,1)} %collective-permute-done.3.refs_1_, bf16[3,768,128]{2,1,0:T(8,128)(2,1)} %copy-done.9, bf16[3,768,128]{2,1,0:T(8,128)(2,1)} %collective-permute-done.5.refs_3_, ...), custom_call_target="tpu_custom_call" | custom-call | flops 603979776 | bytes 9437184 | tf_op jit(solution)/shard_map/pallas_call | solution.py:425
  (46 shorter events, 3.0 us)
Async XLA Ops:
  0.6 64.0 %copy-start = (bf16[12,768,128]{2,1,0:T(8,128)(2,1)S(1)}, bf16[12,768,128]{2,1,0:T(8,128)(2,1)}, u32[]{:S(2)}) copy-start(bf16[12,768,128]{2,1,0:T(8,128)(2,1)} %param.14) | copy-start | bytes 7077892
  4.2 45.3 %all-to-all-start = ((bf16[32,96,128]{2,1,0:T(8,128)(2,1)}), bf16[32,96,128]{2,1,0:T(8,128)(2,1)S(1)}, u32[]{:S(2)}, u32[]{:S(2)}) async-start(bf16[32,96,128]{2,1,0:T(8,128)(2,1)} %shard_map.148), calls=%async_computation | async-start | bytes 1572864 | tf_op jit(solution)/shard_map/all_to_all | solution.py:484
  14.1 23.4 %collective-permute-start.2 = (bf16[3,768,128]{2,1,0:T(8,128)(2,1)S(1)}, bf16[3,768,128]{2,1,0:T(8,128)(2,1)S(1)}, u32[]{:S(2)}, u32[]{:S(2)}) collective-permute-start(bf16[3,768,128]{2,1,0:T(8,128)(2,1)S(1)} %get-tuple-element.63), channel_id=1, source_target_pairs={{0,24},{8,16},{16,8},{24,0},{1,25},{9,17},{17,9},{25,1},{2,26},{10... | collective-permute-start | bytes 1769480 | tf_op jit(solution)/shard_map/ppermute | solution.py:487
  16.7 31.9 %collective-permute-start.1 = (bf16[3,768,128]{2,1,0:T(8,128)(2,1)S(1)}, bf16[3,768,128]{2,1,0:T(8,128)(2,1)S(1)}, u32[]{:S(2)}, u32[]{:S(2)}) collective-permute-start(bf16[3,768,128]{2,1,0:T(8,128)(2,1)S(1)} %get-tuple-element.64), channel_id=1, source_target_pairs={{0,16},{8,24},{16,0},{24,8},{1,17},{9,25},{17,1},{25,9},{2,18},{10... | collective-permute-start | bytes 1769480 | tf_op jit(solution)/shard_map/ppermute | solution.py:487
  17.3 32.2 %collective-permute-start = (bf16[3,768,128]{2,1,0:T(8,128)(2,1)S(1)}, bf16[3,768,128]{2,1,0:T(8,128)(2,1)}, u32[]{:S(2)}, u32[]{:S(2)}) collective-permute-start(bf16[3,768,128]{2,1,0:T(8,128)(2,1)S(1)} %get-tuple-element.65), channel_id=1, source_target_pairs={{0,8},{8,0},{16,24},{24,16},{1,9},{9,1},{17,25},{25,17},{2,10},{10... | collective-permute-start | bytes 1769480 | tf_op jit(solution)/shard_map/ppermute | solution.py:487
  37.4 11.2 %copy-start.10 = (bf16[3,768,128]{2,1,0:T(8,128)(2,1)}, bf16[3,768,128]{2,1,0:T(8,128)(2,1)S(1)}, u32[]{:S(2)}) copy-start(bf16[3,768,128]{2,1,0:T(8,128)(2,1)S(1)} %collective-permute-done.2) | copy-start | bytes 1769476
  48.6 0.8 copy-start.11
  49.5 0.9 copy-start.3
  60.4 26.2 %all-to-all-start.1 = ((bf16[32,96,128]{2,1,0:T(8,128)(2,1)}), bf16[32,96,128]{2,1,0:T(8,128)(2,1)S(1)}, u32[]{:S(2)}, u32[]{:S(2)}) async-start(bf16[32,96,128]{2,1,0:T(8,128)(2,1)} %get-tuple-element.32), calls=%async_computation.1 | async-start | bytes 1572864 | tf_op jit(solution)/shard_map/all_to_all | solution.py:484
  86.6 0.9 copy-start.2
  116.0 11.4 %all-to-all-start.3 = ((bf16[32,24,128]{2,1,0:T(8,128)(2,1)}), bf16[32,24,128]{2,1,0:T(8,128)(2,1)S(1)}, u32[]{:S(2)}, u32[]{:S(2)}) async-start(bf16[32,24,128]{2,1,0:T(8,128)(2,1)} %bitcast.78), calls=%async_computation.3 | async-start | bytes 393216 | tf_op jit(solution)/shard_map/all_to_all | solution.py:484
  127.3 0.7 copy-start.6
  154.2 11.4 %all-to-all-start.5 = ((bf16[32,24,128]{2,1,0:T(8,128)(2,1)}), bf16[32,24,128]{2,1,0:T(8,128)(2,1)S(1)}, u32[]{:S(2)}, u32[]{:S(2)}) async-start(bf16[32,24,128]{2,1,0:T(8,128)(2,1)} %bitcast.79), calls=%async_computation.5 | async-start | bytes 393216 | tf_op jit(solution)/shard_map/all_to_all | solution.py:484
  165.6 0.7 copy-start.8
  192.4 11.4 %all-to-all-start.7 = ((bf16[32,24,128]{2,1,0:T(8,128)(2,1)}), bf16[32,24,128]{2,1,0:T(8,128)(2,1)S(1)}, u32[]{:S(2)}, u32[]{:S(2)}) async-start(bf16[32,24,128]{2,1,0:T(8,128)(2,1)} %bitcast.77), calls=%async_computation.7 | async-start | bytes 393216 | tf_op jit(solution)/shard_map/all_to_all | solution.py:484
  203.8 0.7 copy-start.7
  204.5 8.3 %copy-start.15 = (bf16[512,128]{1,0:T(8,128)(2,1)S(1)}, bf16[512,128]{1,0:T(8,128)(2,1)}, u32[]{:S(2)}) copy-start(bf16[512,128]{1,0:T(8,128)(2,1)} %get-tuple-element.57) | copy-start | bytes 393220
  204.5 8.3 %copy-start.16 = (bf16[512,128]{1,0:T(8,128)(2,1)S(1)}, bf16[512,128]{1,0:T(8,128)(2,1)}, u32[]{:S(2)}) copy-start(bf16[512,128]{1,0:T(8,128)(2,1)} %get-tuple-element.56) | copy-start | bytes 393220
  204.5 8.3 %copy-start.17 = (bf16[512,128]{1,0:T(8,128)(2,1)S(1)}, bf16[512,128]{1,0:T(8,128)(2,1)}, u32[]{:S(2)}) copy-start(bf16[512,128]{1,0:T(8,128)(2,1)} %get-tuple-element.55) | copy-start | bytes 393220
  210.1 15.0 %all-to-all-start.8 = ((bf16[32,40,128]{2,1,0:T(8,128)(2,1)}), bf16[32,40,128]{2,1,0:T(8,128)(2,1)S(1)}, u32[]{:S(2)}, u32[]{:S(2)}) async-start(bf16[32,40,128]{2,1,0:T(8,128)(2,1)} %get-tuple-element.52), calls=%async_computation.8 | async-start | bytes 655360 | tf_op jit(solution)/shard_map/all_to_all | solution.py:484
  212.8 4.9 %copy-start.1 = (bf16[4,3,768,128]{3,2,1,0:T(8,128)(2,1)S(1)}, bf16[4,3,768,128]{3,2,1,0:T(8,128)(2,1)}, u32[]{:S(2)}) copy-start(bf16[4,3,768,128]{3,2,1,0:T(8,128)(2,1)} %get-tuple-element.51) | copy-start | bytes 7077892
  215.0 25.0 %collective-permute-start.11 = (bf16[7,128,128]{2,1,0:T(8,128)(2,1)}, bf16[7,128,128]{2,1,0:T(8,128)(2,1)}, u32[]{:S(2)}, u32[]{:S(2)}) collective-permute-start(bf16[7,128,128]{2,1,0:T(8,128)(2,1)} %get-tuple-element.68), channel_id=1, source_target_pairs={{0,24},{8,16},{16,8},{24,0},{1,25},{9,17},{17,9},{25,1},{2,26},{10... | collective-permute-start | bytes 688136 | tf_op jit(solution)/shard_map/ppermute | solution.py:487
  219.1 45.2 %collective-permute-start.5 = (bf16[3,768,128]{2,1,0:T(8,128)(2,1)}, bf16[3,768,128]{2,1,0:T(8,128)(2,1)}, u32[]{:S(2)}, u32[]{:S(2)}) collective-permute-start(bf16[3,768,128]{2,1,0:T(8,128)(2,1)} %get-tuple-element.59), channel_id=1, source_target_pairs={{0,24},{8,16},{16,8},{24,0},{1,25},{9,17},{17,9},{25,1},{2,26},{10... | collective-permute-start | bytes 1769480 | tf_op jit(solution)/shard_map/ppermute | solution.py:487
  219.4 24.2 %collective-permute-start.10 = (bf16[7,128,128]{2,1,0:T(8,128)(2,1)}, bf16[7,128,128]{2,1,0:T(8,128)(2,1)}, u32[]{:S(2)}, u32[]{:S(2)}) collective-permute-start(bf16[7,128,128]{2,1,0:T(8,128)(2,1)} %get-tuple-element.69), channel_id=1, source_target_pairs={{0,16},{8,24},{16,0},{24,8},{1,17},{9,25},{17,1},{25,9},{2,18},{10... | collective-permute-start | bytes 688136 | tf_op jit(solution)/shard_map/ppermute | solution.py:487
  221.1 24.4 %collective-permute-start.9 = (bf16[7,128,128]{2,1,0:T(8,128)(2,1)}, bf16[7,128,128]{2,1,0:T(8,128)(2,1)}, u32[]{:S(2)}, u32[]{:S(2)}) collective-permute-start(bf16[7,128,128]{2,1,0:T(8,128)(2,1)} %get-tuple-element.70), channel_id=1, source_target_pairs={{0,8},{8,0},{16,24},{24,16},{1,9},{9,1},{17,25},{25,17},{2,10},{10... | collective-permute-start | bytes 688136 | tf_op jit(solution)/shard_map/ppermute | solution.py:487
  225.1 0.7 copy-start.4
  235.9 25.9 %all-to-all-start.9 = ((bf16[8,112,128]{2,1,0:T(8,128)(2,1)}), bf16[8,112,128]{2,1,0:T(8,128)(2,1)S(1)}, u32[]{:S(2)}, u32[]{:S(2)}) async-start(bf16[8,112,128]{2,1,0:T(8,128)(2,1)} %get-tuple-element.53), calls=%async_computation.9 | async-start | bytes 458752 | tf_op jit(solution)/shard_map/all_to_all | solution.py:688
  239.3 37.3 %collective-permute-start.4 = (bf16[3,768,128]{2,1,0:T(8,128)(2,1)}, bf16[3,768,128]{2,1,0:T(8,128)(2,1)S(1)}, u32[]{:S(2)}, u32[]{:S(2)}) collective-permute-start(bf16[3,768,128]{2,1,0:T(8,128)(2,1)} %get-tuple-element.60), channel_id=1, source_target_pairs={{0,16},{8,24},{16,0},{24,8},{1,17},{9,25},{17,1},{25,9},{2,18},{10... | collective-permute-start | bytes 1769480 | tf_op jit(solution)/shard_map/ppermute | solution.py:487
  239.9 36.7 %collective-permute-start.3 = (bf16[3,768,128]{2,1,0:T(8,128)(2,1)}, bf16[3,768,128]{2,1,0:T(8,128)(2,1)}, u32[]{:S(2)}, u32[]{:S(2)}) collective-permute-start(bf16[3,768,128]{2,1,0:T(8,128)(2,1)} %get-tuple-element.61), channel_id=1, source_target_pairs={{0,8},{8,0},{16,24},{24,16},{1,9},{9,1},{17,25},{25,17},{2,10},{10... | collective-permute-start | bytes 1769480 | tf_op jit(solution)/shard_map/ppermute | solution.py:487
  243.5 13.6 %collective-permute-start.14 = (bf16[128,128]{1,0:T(8,128)(2,1)S(1)}, bf16[128,128]{1,0:T(8,128)(2,1)S(1)}, u32[]{:S(2)}, u32[]{:S(2)}) collective-permute-start(bf16[128,128]{1,0:T(8,128)(2,1)S(1)} %get-tuple-element.72), channel_id=1, source_target_pairs={{0,24},{8,16},{16,8},{24,0},{1,25},{9,17},{17,9},{25,1},{2,26},{10... | collective-permute-start | bytes 98312 | tf_op jit(solution)/shard_map/ppermute | solution.py:487
  245.5 14.9 %collective-permute-start.13 = (bf16[128,128]{1,0:T(8,128)(2,1)S(1)}, bf16[128,128]{1,0:T(8,128)(2,1)S(1)}, u32[]{:S(2)}, u32[]{:S(2)}) collective-permute-start(bf16[128,128]{1,0:T(8,128)(2,1)S(1)} %get-tuple-element.73), channel_id=1, source_target_pairs={{0,16},{8,24},{16,0},{24,8},{1,17},{9,25},{17,1},{25,9},{2,18},{10... | collective-permute-start | bytes 98312 | tf_op jit(solution)/shard_map/ppermute | solution.py:487
  257.2 3.9 %collective-permute-start.12 = (bf16[128,128]{1,0:T(8,128)(2,1)S(1)}, bf16[128,128]{1,0:T(8,128)(2,1)S(1)}, u32[]{:S(2)}, u32[]{:S(2)}) collective-permute-start(bf16[128,128]{1,0:T(8,128)(2,1)S(1)} %get-tuple-element.74), channel_id=1, source_target_pairs={{0,8},{8,0},{16,24},{24,16},{1,9},{9,1},{17,25},{25,17},{2,10},{10... | collective-permute-start | bytes 98312 | tf_op jit(solution)/shard_map/ppermute | solution.py:487
  261.8 14.2 %copy-start.5 = (bf16[8,112,128]{2,1,0:T(8,128)(2,1)}, bf16[8,112,128]{2,1,0:T(8,128)(2,1)S(1)}, u32[]{:S(2)}) copy-start(bf16[8,112,128]{2,1,0:T(8,128)(2,1)S(1)} %all-to-all-done.9.refs_4_) | copy-start | bytes 688132
  261.8 14.9 %collective-permute-start.8 = (bf16[8,112,128]{2,1,0:T(8,128)(2,1)S(1)}, bf16[8,112,128]{2,1,0:T(8,128)(2,1)S(1)}, u32[]{:S(2)}, u32[]{:S(2)}) collective-permute-start(bf16[8,112,128]{2,1,0:T(8,128)(2,1)S(1)} %all-to-all-done.9.refs_4_), channel_id=1, source_target_pairs={{24,0},{25,1},{26,2},{27,3},{28,4},{29,5},{30,6},{31,7}} | collective-permute-start | bytes 688136 | tf_op jit(solution)/shard_map/ppermute | solution.py:695
  263.1 13.6 %collective-permute-start.7 = (bf16[8,112,128]{2,1,0:T(8,128)(2,1)S(1)}, bf16[8,112,128]{2,1,0:T(8,128)(2,1)S(1)}, u32[]{:S(2)}, u32[]{:S(2)}) collective-permute-start(bf16[8,112,128]{2,1,0:T(8,128)(2,1)S(1)} %all-to-all-done.9.refs_4_), channel_id=1, source_target_pairs={{16,0},{17,1},{18,2},{19,3},{20,4},{21,5},{22,6},{23,7}} | collective-permute-start | bytes 688136 | tf_op jit(solution)/shard_map/ppermute | solution.py:695
  264.4 12.3 %collective-permute-start.6 = (bf16[8,112,128]{2,1,0:T(8,128)(2,1)S(1)}, bf16[8,112,128]{2,1,0:T(8,128)(2,1)S(1)}, u32[]{:S(2)}, u32[]{:S(2)}) collective-permute-start(bf16[8,112,128]{2,1,0:T(8,128)(2,1)S(1)} %all-to-all-done.9.refs_4_), channel_id=1, source_target_pairs={{8,0},{9,1},{10,2},{11,3},{12,4},{13,5},{14,6},{15,7}} | collective-permute-start | bytes 688136 | tf_op jit(solution)/shard_map/ppermute | solution.py:695
  276.6 0.8 copy-start.9
  276.6 0.9 copy-start.12
  276.7 1.0 copy-start.13
  276.7 1.0 copy-start.14

commit v3 on v2

--- a/solution.py
+++ b/solution.py
@@ -15,7 +15,7 @@
 F32 = jnp.float32
 ALL = ("section", "row")
 VMEM_LIMIT = 56 * 1024 * 1024
-CHUNK = 16
+CHUNK = 32
 
 
 def gelu_derivative(values):
@@ -124,8 +124,9 @@
     return parts
 
 
-def weight_copies(sec_ref, all_ref, weights_ref, sems):
-    span = weights_ref.shape[0] // sems.shape[0]
+def start_copies(sec_ref, all_ref, weights_ref, sems, early, late=()):
+    chunks = sems.shape[0] - len(early) - len(late)
+    span = weights_ref.shape[0] // chunks
     modes = weights_ref.shape[1]
     first = sec_ref[0] * modes
 
@@ -136,16 +137,29 @@
             sems.at[n],
         )
 
-    for n in range(sems.shape[0]):
+    small = [
+        pltpu.make_async_copy(source, target, sems.at[chunks + n])
+        for n, (source, target) in enumerate((*early, *late))
+    ]
+    for copy in small[: len(early)]:
+        copy.start()
+    for n in range(chunks):
         chunk(n).start()
-    return chunk
+    for copy in small[len(early) :]:
+        copy.start()
+    return chunk, chunks, small
 
 
 def mix_kernel(
-    steps, packed, sec_ref, x_ref, lat_ref, inv_ref, all_ref, coeff_ref, out_ref, weights_ref,
-    lhs_ref, z_ref, sems
+    steps, packed, sec_ref, x_any, lat_any, inv_any, all_ref, coeff_ref, out_ref, weights_ref,
+    x_ref, lat_ref, inv_ref, lhs_ref, z_ref, sems
 ):
-    chunk = weight_copies(sec_ref, all_ref, weights_ref, sems)
+    chunk, chunks, small = start_copies(
+        sec_ref, all_ref, weights_ref, sems, [(x_any, x_ref), (lat_any, lat_ref)],
+        [(inv_any, inv_ref)],
+    )
+    small[0].wait()
+    small[1].wait()
     channels = x_ref.shape[-1]
     span = x_ref.shape[0] // steps
     groups = lat_ref.shape[0] // 8
@@ -159,10 +173,10 @@
     for n, part in enumerate(spread_pairs(tall, 4, -1.0)):
         lhs_ref[:, n * channels : (n + 1) * channels] = part
 
-    block = weights_ref.shape[0] // sems.shape[0]
-    per_chunk = groups // sems.shape[0]
-
-    @pl.loop(0, sems.shape[0])
+    block = weights_ref.shape[0] // chunks
+    per_chunk = groups // chunks
+
+    @pl.loop(0, chunks)
     def _(n):
         chunk(n).wait()
         here = weights_ref[pl.ds(n * block, block)].reshape(per_chunk, 8 * channels, channels)
@@ -173,6 +187,7 @@
             for s in range(steps):
                 z_ref[s, pl.ds(to, 8), :] = mixed[s * 8 : (s + 1) * 8]
 
+    small[2].wait()
     inv = inv_ref[...]
     results = [dot(inv, z_ref[s].astype(BF16)) for s in range(steps)]
     if packed:
@@ -185,12 +200,16 @@
 
 
 def adjoint_kernel(
-    extra, sec_ref, x_ref, lat_ref, inv_ref, all_ref, coeff_ref, out_ref, weights_ref,
-    lhs_ref, z_ref, sems
+    extra, sec_ref, x_any, lat_any, inv_any, all_ref, coeff_ref, out_ref, weights_ref, x_ref,
+    lat_ref, inv_ref, lhs_ref, z_ref, sems
 ):
-    chunk = weight_copies(sec_ref, all_ref, weights_ref, sems)
+    copies = start_copies(
+        sec_ref, all_ref, weights_ref, sems, [(x_any, x_ref), (lat_any, lat_ref)],
+        [(inv_any, inv_ref)],
+    )
+    copies[2][0].wait()
+    copies[2][1].wait()
     channels = x_ref.shape[-1]
-    groups = lat_ref.shape[0] // 16
     if extra:
         wide = x_ref[...].astype(F32)
         size = wide.shape[1] - extra
@@ -200,13 +219,26 @@
         x = x_ref[...]
     value = dot(lat_ref[...], x).astype(BF16)
     coeff_ref[...] = value
+    result = adjoint_mix(value, copies, weights_ref, inv_ref, lhs_ref, z_ref)
+    if extra:
+        count = out_ref.shape[0]
+        result = result.reshape(count, -1, channels)
+        sums = jnp.broadcast_to(sums[None], (count, extra, channels))
+        result = jnp.concatenate([result, sums], axis=1)
+    out_ref[...] = result.astype(BF16)
+
+
+def adjoint_mix(value, copies, weights_ref, inv_ref, lhs_ref, z_ref):
+    chunk, chunks, small = copies
+    channels = value.shape[-1]
+    groups = value.shape[0] // 16
     for n, part in enumerate(spread_pairs(value.astype(F32), 8, 1.0)):
         lhs_ref[:, n * channels : (n + 1) * channels] = part
 
-    block = weights_ref.shape[0] // sems.shape[0]
-    per_chunk = groups // sems.shape[0]
-
-    @pl.loop(0, sems.shape[0])
+    block = weights_ref.shape[0] // chunks
+    per_chunk = groups // chunks
+
+    @pl.loop(0, chunks)
     def _(n):
         chunk(n).wait()
         here = weights_ref[pl.ds(n * block, block)].reshape(per_chunk, 8, 2, channels, channels)
@@ -219,13 +251,8 @@
                 mixed = mixed + dot(left, right, ((1,), (1,)))
             z_ref[pl.ds(at, 16), :] = mixed
 
-    result = dot(inv_ref[...], z_ref[...].astype(BF16))
-    if extra:
-        count = out_ref.shape[0]
-        result = result.reshape(count, -1, channels)
-        sums = jnp.broadcast_to(sums[None], (count, extra, channels))
-        result = jnp.concatenate([result, sums], axis=1)
-    out_ref[...] = result.astype(BF16)
+    small[-1].wait()
+    return dot(inv_ref[...], z_ref[...].astype(BF16))
 
 
 def slope_kernel(
@@ -379,13 +406,12 @@
                     out_ref[r, w : w + tile, :] = total.astype(BF16)
 
 
-def weight_kernel(steps, sec_ref, early_ref, late_ref, out_ref):
+def weight_kernel(steps, sec_ref, first_ref, late_ref, out_ref):
     channels = out_ref.shape[-1]
-    tall = early_ref.shape[2]
+    tall = late_ref.shape[2]
     groups = tall // 8
-    lefts = [early_ref[0, s] for s in range(steps)]
-    rights = [early_ref[0, steps + s] for s in range(steps - 1)] + [late_ref[0]]
-    rights = [rights[-1]] + rights[:-1]
+    lefts = [first_ref[0, s] for s in range(steps)]
+    rights = [late_ref[0, s] for s in range(steps - 1)] + [first_ref[0, steps]]
 
     def tallied(values):
         wide = [v.astype(F32).reshape(groups, 8, channels) for v in values]
@@ -504,14 +530,17 @@
     if not packed:
         spectra = outer_pack(spectra, devices)
     gathered = exchange(spectra)
-    gathered, *pieces = lax.optimization_barrier((gathered, *pieces))
+    near = sections - 1
+    gathered, *pieces[:near] = lax.optimization_barrier((gathered, *pieces[:near]))
     gathered = gathered.reshape(sections * grid_rows, channels)
-    all_states = jnp.stack(pieces, 0)
+    all_states = jnp.stack(pieces[:near] + [jnp.zeros_like(pieces[0])], 0)
+    all_states = lax.optimization_barrier(all_states)
+    all_states = lax.dynamic_update_slice_in_dim(all_states, pieces[near][None], near, 0)
 
     chunk_j = max(1, min(freqs, CHUNK // modes))
     weight_scratch = [pltpu.VMEM((freqs, modes, 2, channels, channels), BF16)]
-    weight_sems = [pltpu.SemaphoreType.DMA((freqs // chunk_j,))]
-    weight_spec = pl.BlockSpec(memory_space=pl.ANY)
+    chunks = freqs // chunk_j
+    anywhere = pl.BlockSpec(memory_space=pl.ANY)
     weight_bytes = 4 * freqs * modes * channels * channels
     mixed_shape = (
         (devices, sections * rows * parts, channels)
@@ -524,14 +553,17 @@
             jax.ShapeDtypeStruct((sections, mode_rows, channels), BF16),
             jax.ShapeDtypeStruct(mixed_shape, BF16),
         ],
-        [whole(gathered.shape), whole(lat_plain.shape), whole(inv_shared.shape), weight_spec],
+        [anywhere] * 4,
         (gathered, lat_plain, inv_shared, spec_weights),
         scratch=weight_scratch
         + [
+            pltpu.VMEM(gathered.shape, BF16),
+            pltpu.VMEM(lat_plain.shape, BF16),
+            pltpu.VMEM(inv_shared.shape, BF16),
             pltpu.VMEM((sections * mode_rows, 8 * channels), BF16),
             pltpu.VMEM((sections, mode_rows, channels), F32),
-        ]
-        + weight_sems,
+            pltpu.SemaphoreType.DMA((chunks + 3,)),
+        ],
         prefetch=sec,
         flops=4 * weight_bytes,
         moved=weight_bytes,
@@ -589,47 +621,42 @@
     slot = channels // row_devs
     store = carried[None]
     store_shape = (sections,) + shape3
-    for s in range(sections - 1, -1, -1):
-        extra = 0
-        if s == 0:
-            extra = slot
-            if not packed:
-                terms = acc.reshape(row_devs, slot, channels).astype(BF16)
-                terms = jnp.concatenate([terms] * sections, axis=0)
-                send = jnp.concatenate([outer_pack(send, devices), terms], axis=1)
-        elif not packed:
+    part = mode_rows // sections
+
+    def adjoint_scratch(*small):
+        return (
+            weight_scratch
+            + [pltpu.VMEM(a.shape, BF16) for a in small]
+            + [pltpu.VMEM((mode_rows, 16 * channels), BF16), pltpu.VMEM((mode_rows, channels), F32)]
+            + [pltpu.SemaphoreType.DMA((chunks + len(small),))]
+        )
+
+    def gather_modes(values):
+        split = jnp.stack(values, 0).reshape(len(values), sections, part, channels)
+        mine = [lax.dynamic_index_in_dim(split, section ^ d, 1, False) for d in range(sections)]
+        return [mine[0]] + [share(mine[d], d) for d in range(1, sections)]
+
+    for s in range(sections - 1, 0, -1):
+        if not packed:
             send = outer_pack(send, devices)
         got = exchange(send)
-        if extra and not packed:
-            sums = jnp.sum(got[:, rows * parts :].astype(F32), 0)
-            got = got[:, : rows * parts]
-        inside = extra if packed else 0
-        if not inside:
-            got = got.reshape(grid_rows, channels)
-        inner_shape = (grid_rows, channels)
-        if inside:
-            inner_shape = (row_devs, grid_rows // row_devs + extra, channels)
-        inverse = inv_shared if s > 0 else inv_plain
+        if s == sections - 2:
+            first_modes = gather_modes([coeffs[n] for n in range(sections)] + [cots[s + 1]])
+            got, first_modes = lax.optimization_barrier((got, first_modes))
+        got = got.reshape(grid_rows, channels)
         cots[s], inner = call(
-            functools.partial(adjoint_kernel, inside),
+            functools.partial(adjoint_kernel, 0),
             [
                 jax.ShapeDtypeStruct((mode_rows, channels), BF16),
-                jax.ShapeDtypeStruct(inner_shape, BF16),
+                jax.ShapeDtypeStruct((grid_rows, channels), BF16),
             ],
-            [whole(got.shape), whole(lat_shared.shape), whole(inverse.shape), weight_spec],
-            (got, lat_shared, inverse, spec_weights),
-            scratch=weight_scratch
-            + [
-                pltpu.VMEM((mode_rows, 16 * channels), BF16),
-                pltpu.VMEM((mode_rows, channels), F32),
-            ]
-            + weight_sems,
+            [anywhere] * 4,
+            (got, lat_shared, inv_shared, spec_weights),
+            scratch=adjoint_scratch(got, lat_shared, inv_shared),
             prefetch=sec,
             flops=2 * weight_bytes,
             moved=weight_bytes,
         )
-        if s == 0:
-            break
         got = exchange(inner.reshape(devices, rows * parts, channels))
         if not packed:
             got = outer_unpack(got, rows)
@@ -671,42 +698,48 @@
     for d in range(1, sections):
         parts_of.append(share(lax.dynamic_index_in_dim(store, section ^ d, 0, False), d))
 
-    part = mode_rows // sections
-
-    def gather_modes(values):
-        mine = [lax.dynamic_index_in_dim(values, section ^ d, 0, False) for d in range(sections)]
-        return jnp.stack([mine[0]] + [share(mine[d], d) for d in range(1, sections)], 0)
-
-    early = jnp.concatenate([coeffs, jnp.stack(cots[1:], 0)], 0)
-    early = early.reshape(-1, sections, part, channels).swapaxes(0, 1)
-    early = gather_modes(early)
-
+    if not packed:
+        terms = acc.reshape(row_devs, slot, channels).astype(BF16)
+        terms = jnp.concatenate([terms] * sections, axis=0)
+        send = jnp.concatenate([outer_pack(send, devices), terms], axis=1)
+    got = exchange(send)
+    inner_shape = (row_devs, grid_rows // row_devs + slot, channels)
+    if not packed:
+        sums = jnp.sum(got[:, rows * parts :].astype(F32), 0)
+        got = got[:, : rows * parts].reshape(grid_rows, channels)
+        inner_shape = (grid_rows, channels)
+    cots[0], inner = call(
+        functools.partial(adjoint_kernel, slot if packed else 0),
+        [
+            jax.ShapeDtypeStruct((mode_rows, channels), BF16),
+            jax.ShapeDtypeStruct(inner_shape, BF16),
+        ],
+        [anywhere] * 4,
+        (got, lat_shared, inv_plain, spec_weights),
+        scratch=adjoint_scratch(got, lat_shared, inv_plain),
+        prefetch=sec,
+        flops=2 * weight_bytes,
+        moved=weight_bytes,
+    )
+    late_modes = gather_modes(cots[:-1])
     if not packed:
         inner = inner.reshape(row_devs, grid_rows // row_devs, channels)
         both = jnp.broadcast_to(sums.astype(BF16)[None], (row_devs, slot, channels))
         inner = jnp.concatenate([inner, both], axis=1)
     got = lax.all_to_all(inner, "row", 0, 0, tiled=True)
-    size = grid_rows // row_devs
-    local_total = got[:, size:].reshape(channels, channels).astype(F32)
-    d_local = local_total * lax.rsqrt(jnp.float32(sections * lat_cells * cells))
-    if not packed:
-        got = outer_unpack(got[:, :size], rows_here)
-    mode_parts = [got] + [
-        lax.ppermute(got, "section", [(d, 0)]) for d in range(1, sections)
-    ]
-
-    late = gather_modes(cots[0].reshape(sections, part, channels))
+
     own_freqs = freqs // sections
     own_j = max(1, min(own_freqs, 32 // modes))
     tall = own_j * parts
+    first_modes, late_modes = jnp.stack(first_modes, 0), jnp.stack(late_modes, 0)
     (d_spectral,) = call(
         functools.partial(weight_kernel, sections),
         [jax.ShapeDtypeStruct((own_freqs, row_modes, 2, channels, channels), BF16)],
         [
-            pl.BlockSpec((1, 2 * sections - 1, tall, channels), lambda a, b, i: (a, 0, b, 0)),
-            pl.BlockSpec((1, tall, channels), lambda a, b, i: (a, b, 0)),
+            pl.BlockSpec((1, m.shape[1], tall, channels), lambda a, b, i: (a, 0, b, 0))
+            for m in (first_modes, late_modes)
         ],
-        (early, late),
+        (first_modes, late_modes),
         grid=(sections, own_freqs // own_j),
         out_specs=[
             pl.BlockSpec(
@@ -718,10 +751,18 @@
         moved=weight_bytes,
     )
 
+    size = grid_rows // row_devs
+    local_total = got[:, size:].reshape(channels, channels).astype(F32)
+    d_local = local_total * lax.rsqrt(jnp.float32(sections * lat_cells * cells))
+    if not packed:
+        got = outer_unpack(got[:, :size], rows_here)
+    mode_parts = [got] + [
+        lax.ppermute(got, "section", [(d, 0)]) for d in range(1, sections)
+    ]
     (grad_states,) = call(
         functools.partial(close_kernel, packed),
         [jax.ShapeDtypeStruct((rows_here, cells, channels), BF16)],
-        [whole(shape3)] * sections + [whole(got.shape)] * sections + [whole(basis.shape)],
+        [whole(shape3)] * len(parts_of) + [whole(got.shape)] * sections + [whole(basis.shape)],
         (*parts_of, *mode_parts, basis),
         grid=(sections,),
         out_specs=[pl.BlockSpec(shape3, lambda d, i: (i[0] ^ d, 0, 0))],

time: 284 us -> 270 us (0.951)
  blocking collectives: 36.1 us -> 24.6 us
  Pallas kernels: 99.4 us -> 91.2 us
  starting transfers between devices: 44 us -> 49.7 us
  local copies, waits for them, and re-layouts: 13.9 us -> 17.1 us
  waiting for transfers between devices: 80.2 us -> 77.1 us
    all_to_all x6 -> x7, waiting for transfers between devices: 35.2 us -> 20.7 us  [exchange(): return lax.all_to_all(values, ALL, 0, 0, tiled=True)]
    all_to_all x3 -> x2, blocking collectives: 36.1 us -> 24.6 us  [exchange(): return lax.all_to_all(values, ALL, 0, 0, tiled=True)]
    ppermute x12, waiting for transfers between devices: 45 us -> 56.3 us  [share(): return lax.ppermute(piece, 'section', [(i, i ^ d) for i in range(sections)])]
    pallas_call x16, Pallas kernels: 99.4 us -> 91.2 us  [call(): pl.pallas_call(kernel, out_shape=outs, grid_spec=pltpu.PrefetchScalarGrid...]
    all_to_all x6 -> x7, starting transfers between devices: 22.3 us -> 26.8 us  [exchange(): return lax.all_to_all(values, ALL, 0, 0, tiled=True)]
    another operation x3 -> x4, other arithmetic: 6.16 us -> 6.97 us  [the longest x1 3.1 us: local(): all_states = jnp.stack(pieces[:near] + [jnp.zeros_like(pieces[0])], 0)]
  transfers between devices with their start and end apart: 22 -> 23, of which waited for: 10 -> 10; matrix products, arithmetic and copies ran while one was open for 6% -> 6% of each run, Pallas kernels for 11% -> 11%
where the time goes in v3:
time: 270 us; the launch traced here: 268 us
  Pallas kernels  91.2 us (34%)
  waiting for transfers between devices  77.1 us (29%)
  starting transfers between devices  49.7 us (18%)
  blocking collectives  24.6 us (9%)
  local copies, waits for them, and re-layouts  17.1 us (6%)
  other arithmetic  7.67 us (3%)
    pallas_call x16, Pallas kernels, call(): pl.pallas_call(kernel, out_shape=outs, grid_spec=pltpu.PrefetchScalarGrid...  91.2 us
    ppermute x12, waiting for transfers between devices, share(): return lax.ppermute(piece, 'section', [(i, i ^ d) for i in range(sections)])  56.3 us
    all_to_all x7, starting transfers between devices, exchange(): return lax.all_to_all(values, ALL, 0, 0, tiled=True)  26.8 us
    all_to_all x2, blocking collectives, exchange(): return lax.all_to_all(values, ALL, 0, 0, tiled=True)  24.6 us
    all_to_all x7, waiting for transfers between devices, exchange(): return lax.all_to_all(values, ALL, 0, 0, tiled=True)  20.7 us
    ppermute x12, starting transfers between devices, share(): return lax.ppermute(piece, 'section', [(i, i ^ d) for i in range(sections)])  15.6 us
    unnamed x36, local copies, waits for them, and re-layouts  7.55 us
  transfers between devices with their start and end apart: 23, of which 10 were waited for; matrix products, arithmetic and copies ran while one was open for 6% of the time, Pallas kernels for 11%

profile of v3, /device:TPU:0, one launch (start us, length us, event | category | flops | bytes accessed | tf_op | source)
XLA Modules:
  0.0 268.2 jit_solution(7813786132417923601)
XLA Ops:
  0.6 3.5 %shard_map.148 = bf16[32,96,128]{2,1,0:T(8,128)(2,1)} custom-call(bf16[12,768,128]{2,1,0:T(8,128)(2,1)} %bitcast.73, bf16[256,768]{1,0:T(8,128)(2,1)} %constant.75.clone.basis_ref), custom_call_target="tpu_custom_call" | custom-call | flops 603979776 | bytes 4718592 | tf_op jit(solution)/shard_map/pallas_call | solution.py:451
  4.2 7.3 %all-to-all-start = ((bf16[32,96,128]{2,1,0:T(8,128)(2,1)}), bf16[32,96,128]{2,1,0:T(8,128)(2,1)S(1)}, u32[]{:S(2)}, u32[]{:S(2)}) async-start(bf16[32,96,128]{2,1,0:T(8,128)(2,1)} %shard_map.148), calls=%async_computation | async-start | bytes 1572864 | tf_op jit(solution)/shard_map/all_to_all | solution.py:510
  11.5 2.8 %dynamic-slice_bitcast_fusion.4 = (bf16[3,768,128]{2,1,0:T(8,128)(2,1)}, bf16[3,768,128]{2,1,0:T(8,128)(2,1)S(1)}, bf16[3,768,128]{2,1,0:T(8,128)(2,1)S(1)}, bf16[3,768,128]{2,1,0:T(8,128)(2,1)}) fusion(bf16[4,3,768,128]{3,2,1,0:T(8,128)(2,1)} %bitcast.74, s32[]{:T(128)S(6)} %select_n.34, s32[]{:T(128)S(6)} %select_n.33, s32[]{:T(128)S(6)} %select_n.32, ...), kind=kLoop, calls=%fused_computation.15 | loop fusion | bytes 4718608 | tf_op jit(solution)/shard_map/jit(dynamic_index_in_dim)/squeeze | solution.py:518
  14.3 1.8 collective-permute-start.1
  16.1 1.5 collective-permute-start
  17.5 18.2 %collective-permute-done.1 = bf16[3,768,128]{2,1,0:T(8,128)(2,1)S(1)} collective-permute-done((bf16[3,768,128]{2,1,0:T(8,128)(2,1)S(1)}, bf16[3,768,128]{2,1,0:T(8,128)(2,1)S(1)}, u32[]{:S(2)}, u32[]{:S(2)}) %collective-permute-start.1) | collective-permute-done | bytes 589856 | tf_op jit(solution)/shard_map/ppermute | solution.py:513
  35.8 0.8 copy-done.10
  36.6 0.9 copy-done.2
  37.5 8.7 %shard_map.149 = (bf16[4,512,128]{2,1,0:T(8,128)(2,1)}, bf16[32,96,128]{2,1,0:T(8,128)(2,1)}) custom-call(s32[1]{0:T(128)} %bitcast.sec_ref, bf16[3072,128]{1,0:T(8,128)(2,1)} %bitcast.75, bf16[512,768]{1,0:T(8,128)(2,1)} %constant.78.clone.lat_any, bf16[768,512]{1,0:T(8,128)(2,1)} %constant.80.clone.inv_any, bf16[64,16,2,128,128]{4,3,2,1,0:T(8,128)(2,1)} %all_ref.9), custom_call_target="tpu_custom_call" | custom-call | flops 67108864 | bytes 16777216 | tf_op jit(solution)/shard_map/pallas_call | solution.py:451
  46.2 4.4 %all-to-all-start.1 = ((bf16[32,96,128]{2,1,0:T(8,128)(2,1)}), bf16[32,96,128]{2,1,0:T(8,128)(2,1)S(1)}, u32[]{:S(2)}, u32[]{:S(2)}) async-start(bf16[32,96,128]{2,1,0:T(8,128)(2,1)} %get-tuple-element.36), calls=%async_computation.1 | async-start | bytes 1572864 | tf_op jit(solution)/shard_map/all_to_all | solution.py:510
  50.7 2.7 %collective-permute-start.2 = (bf16[3,768,128]{2,1,0:T(8,128)(2,1)}, bf16[3,768,128]{2,1,0:T(8,128)(2,1)}, u32[]{:S(2)}, u32[]{:S(2)}) collective-permute-start(bf16[3,768,128]{2,1,0:T(8,128)(2,1)} %get-tuple-element.71), channel_id=1, source_target_pairs={{0,24},{8,16},{16,8},{24,0},{1,25},{9,17},{17,9},{25,1},{2,26},{10... | collective-permute-start | bytes 1769480 | tf_op jit(solution)/shard_map/ppermute | solution.py:513
  53.5 0.9 constant_dynamic-slice_fusion.cot_ref
  54.3 3.1 %maximum_maximum_fusion = bf16[4,3,768,128]{3,2,1,0:T(8,128)(2,1)} fusion(bf16[1,3,768,128]{3,2,1,0:T(8,128)(2,1)} %bitcast.82, bf16[1,3,768,128]{3,2,1,0:T(8,128)(2,1)} %bitcast.8, bf16[1,3,768,128]{3,2,1,0:T(8,128)(2,1)} %bitcast.77, bf16[4]{0:T(256)(128)(2,1)S(1)} %pad.16.clone), kind=kLoop, calls=%fused_computation | loop fusion | flops 3538944 | bytes 4128776 | tf_op jit(solution)/shard_map/stack | solution.py:536
  57.4 19.0 %collective-permute-done.2 = bf16[3,768,128]{2,1,0:T(8,128)(2,1)} collective-permute-done((bf16[3,768,128]{2,1,0:T(8,128)(2,1)}, bf16[3,768,128]{2,1,0:T(8,128)(2,1)}, u32[]{:S(2)}, u32[]{:S(2)}) %collective-permute-start.2) | collective-permute-done | bytes 589856 | tf_op jit(solution)/shard_map/ppermute | solution.py:513
  76.4 1.9 bitcast_dynamic-update-slice_fusion.state_ref
  78.3 0.9 copy-done.1
  79.2 3.4 %shard_map.150.slope_ref = f32[3,768,128]{2,1,0:T(8,128)} custom-call(s32[1]{0:T(128)} %bitcast.sec_ref, bf16[32,96,128]{2,1,0:T(8,128)(2,1)} %copy-done.1, bf16[4,3,768,128]{3,2,1,0:T(8,128)(2,1)} %bitcast_dynamic-update-slice_fusion.state_ref, bf16[768,256]{1,0:T(8,128)(2,1)} %constant.77.clone.synth_ref, bf16[128,128]{1,0:T(8,128)(2,1)} %mix_ref.13, ...), custom_call_target="tpu_custom_call" | custom-call | flops 150994944 | bytes 2949120 | tf_op jit(solution)/shard_map/pallas_call | solution.py:451
  82.6 3.0 %shard_map.151 = (bf16[3,768,128]{2,1,0:T(8,128)(2,1)}, bf16[32,24,128]{2,1,0:T(8,128)(2,1)}, f32[128,128]{1,0:T(8,128)}) custom-call(s32[1]{0:T(128)} %bitcast.sec_ref, bf16[3,768,128]{2,1,0:T(8,128)(2,1)} %constant_dynamic-slice_fusion.cot_ref, f32[3,768,128]{2,1,0:T(8,128)} %shard_map.150.slope_ref, ...), custom_call_target="tpu_custom_call" | custom-call | flops 150994944 | bytes 2949120 | tf_op jit(solution)/shard_map/pallas_call | solution.py:451
  85.5 12.6 %all_to_all.50 = bf16[32,24,128]{2,1,0:T(8,128)(2,1)} all-to-all(bf16[32,24,128]{2,1,0:T(8,128)(2,1)} %get-tuple-element.40), channel_id=1, replica_groups=mesh['section'=4,'row'=8] {'section','row'}, dimensions={0} | all-to-all | bytes 393216 | tf_op jit(solution)/shard_map/all_to_all | solution.py:510
  98.1 8.3 %shard_map.152 = (bf16[512,128]{1,0:T(8,128)(2,1)}, bf16[768,128]{1,0:T(8,128)(2,1)}) custom-call(s32[1]{0:T(128)} %bitcast.sec_ref, bf16[768,128]{1,0:T(8,128)(2,1)} %bitcast.80, bf16[512,768]{1,0:T(8,128)(2,1)} %constant.79.clone.lat_any, bf16[768,512]{1,0:T(8,128)(2,1)} %constant.80.clone.inv_any, bf16[64,16,2,128,128]{4,3,2,1,0:T(8,128)(2,1)} %all_ref.9), custom_call_target="tpu_custom_call" | custom-call | flops 33554432 | bytes 16777216 | tf_op jit(solution)/shard_map/pallas_call | solution.py:451
  106.5 2.7 %all-to-all-start.3 = ((bf16[32,24,128]{2,1,0:T(8,128)(2,1)}), bf16[32,24,128]{2,1,0:T(8,128)(2,1)S(1)}, u32[]{:S(2)}, u32[]{:S(2)}) async-start(bf16[32,24,128]{2,1,0:T(8,128)(2,1)} %bitcast.85), calls=%async_computation.3 | async-start | bytes 393216 | tf_op jit(solution)/shard_map/all_to_all | solution.py:510
  109.2 0.9 fusion.8.carried_ref
  110.1 3.4 %shard_map.153.slope_ref = f32[3,768,128]{2,1,0:T(8,128)} custom-call(s32[1]{0:T(128)} %bitcast.sec_ref, bf16[32,96,128]{2,1,0:T(8,128)(2,1)} %copy-done.1, bf16[4,3,768,128]{3,2,1,0:T(8,128)(2,1)} %bitcast_dynamic-update-slice_fusion.state_ref, bf16[768,256]{1,0:T(8,128)(2,1)} %constant.77.clone.synth_ref, bf16[128,128]{1,0:T(8,128)(2,1)} %mix_ref.13, ...), custom_call_target="tpu_custom_call" | custom-call | flops 150994944 | bytes 2949120 | tf_op jit(solution)/shard_map/pallas_call | solution.py:451
  113.5 4.5 %all-to-all-done.3.recv_ref = bf16[32,24,128]{2,1,0:T(8,128)(2,1)S(1)} async-done(((bf16[32,24,128]{2,1,0:T(8,128)(2,1)}), bf16[32,24,128]{2,1,0:T(8,128)(2,1)S(1)}, u32[]{:S(2)}, u32[]{:S(2)}) %all-to-all-start.3) | async-done | bytes 196640 | tf_op jit(solution)/shard_map/all_to_all | solution.py:510
  117.9 0.7 copy-done.5
  118.6 4.1 %shard_map.154 = (bf16[4,3,768,128]{3,2,1,0:T(8,128)(2,1)}, bf16[3,768,128]{2,1,0:T(8,128)(2,1)}, bf16[32,24,128]{2,1,0:T(8,128)(2,1)}, f32[128,128]{1,0:T(8,128)}) custom-call(s32[1]{0:T(128)} %bitcast.sec_ref, bf16[32,24,128]{2,1,0:T(8,128)(2,1)} %copy-done.5, bf16[1,3,768,128]{3,2,1,0:T(8,128)(2,1)} %fusion.8.carried_ref, ...), custom_call_target="tpu_custom_call" | custom-call | flops 301989888 | bytes 4718592 | tf_op jit(solution)/shard_map/pallas_call | solution.py:451
  122.8 2.7 %all-to-all-start.4 = ((bf16[32,24,128]{2,1,0:T(8,128)(2,1)}), bf16[32,24,128]{2,1,0:T(8,128)(2,1)S(1)}, u32[]{:S(2)}, u32[]{:S(2)}) async-start(bf16[32,24,128]{2,1,0:T(8,128)(2,1)} %get-tuple-element.44), calls=%async_computation.4 | async-start | bytes 393216 | tf_op jit(solution)/shard_map/all_to_all | solution.py:510
  125.6 2.7 %collective-permute-start.5 = (bf16[5,128,128]{2,1,0:T(8,128)(2,1)S(1)}, bf16[5,128,128]{2,1,0:T(8,128)(2,1)S(1)}, u32[]{:S(2)}, u32[]{:S(2)}) collective-permute-start(bf16[5,128,128]{2,1,0:T(8,128)(2,1)S(1)} %get-tuple-element.75), channel_id=1, source_target_pairs={{0,24},{8,16},{16,8},{24,0},{1,25},{9,17},{17,9},{25,1},{2,26},{10... | collective-permute-start | bytes 491528 | tf_op jit(solution)/shard_map/ppermute | solution.py:513
  129.2 6.3 %collective-permute-done.5 = bf16[5,128,128]{2,1,0:T(8,128)(2,1)S(1)} collective-permute-done((bf16[5,128,128]{2,1,0:T(8,128)(2,1)S(1)}, bf16[5,128,128]{2,1,0:T(8,128)(2,1)S(1)}, u32[]{:S(2)}, u32[]{:S(2)}) %collective-permute-start.5) | collective-permute-done | bytes 163872 | tf_op jit(solution)/shard_map/ppermute | solution.py:513
  135.5 2.6 collective-permute-done.3
  138.1 0.7 copy-done.16
  138.8 0.7 copy-done.8
  139.5 8.3 %shard_map.155 = (bf16[512,128]{1,0:T(8,128)(2,1)}, bf16[768,128]{1,0:T(8,128)(2,1)}) custom-call(s32[1]{0:T(128)} %bitcast.sec_ref, bf16[768,128]{1,0:T(8,128)(2,1)} %bitcast.78, bf16[512,768]{1,0:T(8,128)(2,1)} %constant.79.clone.lat_any, bf16[768,512]{1,0:T(8,128)(2,1)} %constant.80.clone.inv_any, bf16[64,16,2,128,128]{4,3,2,1,0:T(8,128)(2,1)} %all_ref.9), custom_call_target="tpu_custom_call" | custom-call | flops 33554432 | bytes 16777216 | tf_op jit(solution)/shard_map/pallas_call | solution.py:451
  147.8 4.2 %all-to-all-start.5 = ((bf16[32,24,128]{2,1,0:T(8,128)(2,1)}), bf16[32,24,128]{2,1,0:T(8,128)(2,1)S(1)}, u32[]{:S(2)}, u32[]{:S(2)}) async-start(bf16[32,24,128]{2,1,0:T(8,128)(2,1)} %bitcast.86), calls=%async_computation.5 | async-start | bytes 393216 | tf_op jit(solution)/shard_map/all_to_all | solution.py:510
  152.1 3.4 %shard_map.156.slope_ref = f32[3,768,128]{2,1,0:T(8,128)} custom-call(s32[1]{0:T(128)} %bitcast.sec_ref, bf16[32,96,128]{2,1,0:T(8,128)(2,1)} %copy-done.1, bf16[4,3,768,128]{3,2,1,0:T(8,128)(2,1)} %bitcast_dynamic-update-slice_fusion.state_ref, bf16[768,256]{1,0:T(8,128)(2,1)} %constant.77.clone.synth_ref, bf16[128,128]{1,0:T(8,128)(2,1)} %mix_ref.13, ...), custom_call_target="tpu_custom_call" | custom-call | flops 150994944 | bytes 2949120 | tf_op jit(solution)/shard_map/pallas_call | solution.py:451
  155.5 5.1 %all-to-all-done.5.recv_ref = bf16[32,24,128]{2,1,0:T(8,128)(2,1)S(1)} async-done(((bf16[32,24,128]{2,1,0:T(8,128)(2,1)}), bf16[32,24,128]{2,1,0:T(8,128)(2,1)S(1)}, u32[]{:S(2)}, u32[]{:S(2)}) %all-to-all-start.5) | async-done | bytes 196640 | tf_op jit(solution)/shard_map/all_to_all | solution.py:510
  160.6 0.7 copy-done.7
  161.3 4.1 %shard_map.157 = (bf16[4,3,768,128]{3,2,1,0:T(8,128)(2,1)}, bf16[3,768,128]{2,1,0:T(8,128)(2,1)}, bf16[32,24,128]{2,1,0:T(8,128)(2,1)}, f32[128,128]{1,0:T(8,128)}) custom-call(s32[1]{0:T(128)} %bitcast.sec_ref, bf16[32,24,128]{2,1,0:T(8,128)(2,1)} %copy-done.7, ...), custom_call_target="tpu_custom_call", output_to_operand_aliasing={{0}: (2, {})} | custom-call | flops 301989888 | bytes 4718592 | tf_op jit(solution)/shard_map/pallas_call | solution.py:451
  165.4 12.0 %all_to_all.51 = bf16[32,24,128]{2,1,0:T(8,128)(2,1)} all-to-all(bf16[32,24,128]{2,1,0:T(8,128)(2,1)} %get-tuple-element.52), channel_id=1, replica_groups=mesh['section'=4,'row'=8] {'section','row'}, dimensions={0} | all-to-all | bytes 393216 | tf_op jit(solution)/shard_map/all_to_all | solution.py:510
  177.4 8.4 %shard_map.158 = (bf16[512,128]{1,0:T(8,128)(2,1)}, bf16[768,128]{1,0:T(8,128)(2,1)}) custom-call(s32[1]{0:T(128)} %bitcast.sec_ref, bf16[768,128]{1,0:T(8,128)(2,1)} %bitcast.79, bf16[512,768]{1,0:T(8,128)(2,1)} %constant.79.clone.lat_any, bf16[768,512]{1,0:T(8,128)(2,1)} %constant.80.clone.inv_any, bf16[64,16,2,128,128]{4,3,2,1,0:T(8,128)(2,1)} %all_ref.9), custom_call_target="tpu_custom_call" | custom-call | flops 33554432 | bytes 16777216 | tf_op jit(solution)/shard_map/pallas_call | solution.py:451
  185.8 2.6 all-to-all-start.7
  188.4 3.4 %shard_map.159.slope_ref = f32[3,768,128]{2,1,0:T(8,128)} custom-call(s32[1]{0:T(128)} %bitcast.sec_ref, bf16[32,96,128]{2,1,0:T(8,128)(2,1)} %copy-done.1, bf16[4,3,768,128]{3,2,1,0:T(8,128)(2,1)} %bitcast_dynamic-update-slice_fusion.state_ref, bf16[768,256]{1,0:T(8,128)(2,1)} %constant.77.clone.synth_ref, bf16[128,128]{1,0:T(8,128)(2,1)} %mix_ref.13, ...), custom_call_target="tpu_custom_call" | custom-call | flops 150994944 | bytes 2949120 | tf_op jit(solution)/shard_map/pallas_call | solution.py:451
  191.8 5.3 %all-to-all-done.7.recv_ref = bf16[32,24,128]{2,1,0:T(8,128)(2,1)S(1)} async-done(((bf16[32,24,128]{2,1,0:T(8,128)(2,1)}), bf16[32,24,128]{2,1,0:T(8,128)(2,1)S(1)}, u32[]{:S(2)}, u32[]{:S(2)}) %all-to-all-start.7) | async-done | bytes 196640 | tf_op jit(solution)/shard_map/all_to_all | solution.py:510
  197.2 0.7 copy-done.6
  197.8 5.5 %shard_map.160 = (bf16[4,3,768,128]{3,2,1,0:T(8,128)(2,1)}, bf16[3,768,128]{2,1,0:T(8,128)(2,1)}, bf16[32,40,128]{2,1,0:T(8,128)(2,1)}, f32[128,128]{1,0:T(8,128)}) custom-call(s32[1]{0:T(128)} %bitcast.sec_ref, bf16[32,24,128]{2,1,0:T(8,128)(2,1)} %copy-done.6, ...), custom_call_target="tpu_custom_call", output_to_operand_aliasing={{0}: (2, {})} | custom-call | flops 301989888 | bytes 4718592 | tf_op jit(solution)/shard_map/pallas_call | solution.py:451
  203.3 2.7 %all-to-all-start.8 = ((bf16[32,40,128]{2,1,0:T(8,128)(2,1)}), bf16[32,40,128]{2,1,0:T(8,128)(2,1)S(1)}, u32[]{:S(2)}, u32[]{:S(2)}) async-start(bf16[32,40,128]{2,1,0:T(8,128)(2,1)} %get-tuple-element.58), calls=%async_computation.8 | async-start | bytes 655360 | tf_op jit(solution)/shard_map/all_to_all | solution.py:510
  206.1 3.0 %dynamic-slice_bitcast_fusion = (bf16[3,768,128]{2,1,0:T(8,128)(2,1)}, bf16[3,768,128]{2,1,0:T(8,128)(2,1)}, bf16[3,768,128]{2,1,0:T(8,128)(2,1)}, bf16[3,768,128]{2,1,0:T(8,128)(2,1)}) fusion(bf16[4,3,768,128]{3,2,1,0:T(8,128)(2,1)} %get-tuple-element.57, s32[]{:T(128)S(6)} %select_n.34, s32[]{:T(128)S(6)} %select_n.33, s32[]{:T(128)S(6)} %select_n.32, ...), kind=kLoop, calls=%fused_computation.11 | loop fusion | bytes 4718608 | tf_op jit(solution)/shard_map/jit(dynamic_index_in_dim)/squeeze | solution.py:699
  209.1 2.7 collective-permute-start.8
  212.6 5.8 %all-to-all-done.8.x_any = bf16[32,40,128]{2,1,0:T(8,128)(2,1)S(1)} async-done(((bf16[32,40,128]{2,1,0:T(8,128)(2,1)}), bf16[32,40,128]{2,1,0:T(8,128)(2,1)S(1)}, u32[]{:S(2)}, u32[]{:S(2)}) %all-to-all-start.8) | async-done | bytes 327712 | tf_op jit(solution)/shard_map/all_to_all | solution.py:510
  218.4 0.7 copy-done.3
  219.1 8.4 %shard_map.161 = (bf16[512,128]{1,0:T(8,128)(2,1)}, bf16[8,112,128]{2,1,0:T(8,128)(2,1)}) custom-call(s32[1]{0:T(128)} %bitcast.sec_ref, bf16[32,40,128]{2,1,0:T(8,128)(2,1)} %copy-done.3, bf16[512,768]{1,0:T(8,128)(2,1)} %constant.79.clone.lat_any, bf16[768,512]{1,0:T(8,128)(2,1)} %constant.81.clone.inv_any, bf16[64,16,2,128,128]{4,3,2,1,0:T(8,128)(2,1)} %all_ref.9), custom_call_target="tpu_custom_call" | custom-call | flops 33554432 | bytes 16777216 | tf_op jit(solution)/shard_map/pallas_call | solution.py:451
  227.5 3.4 %all-to-all-start.9 = ((bf16[8,112,128]{2,1,0:T(8,128)(2,1)}), bf16[8,112,128]{2,1,0:T(8,128)(2,1)S(1)}, u32[]{:S(2)}, u32[]{:S(2)}) async-start(bf16[8,112,128]{2,1,0:T(8,128)(2,1)} %get-tuple-element.59), calls=%async_computation.9 | async-start | bytes 458752 | tf_op jit(solution)/shard_map/all_to_all | solution.py:729
  230.9 1.1 pad_maximum_fusion.1
  232.5 0.7 collective-permute-start.13
  233.3 9.0 %collective-permute-done.14 = bf16[3,128,128]{2,1,0:T(8,128)(2,1)S(1)} collective-permute-done((bf16[3,128,128]{2,1,0:T(8,128)(2,1)S(1)}, bf16[3,128,128]{2,1,0:T(8,128)(2,1)S(1)}, u32[]{:S(2)}, u32[]{:S(2)}) %collective-permute-start.14) | collective-permute-done | bytes 98336 | tf_op jit(solution)/shard_map/ppermute | solution.py:513
  242.3 1.4 collective-permute-start.12
  243.7 2.0 pad_maximum_fusion.first_ref
  245.7 1.2 collective-permute-done.12
  246.9 0.8 pad_maximum_fusion.2.late_ref
  247.7 1.3 collective-permute-start.11
  249.0 1.3 collective-permute-start.10
  250.3 1.3 collective-permute-start.9
  251.6 10.3 %shard_map.163 = bf16[16,16,2,128,128]{4,3,2,1,0:T(8,128)(2,1)} custom-call(s32[1]{0:T(128)} %bitcast.sec_ref, bf16[4,5,128,128]{3,2,1,0:T(8,128)(2,1)} %pad_maximum_fusion.first_ref, bf16[4,3,128,128]{3,2,1,0:T(8,128)(2,1)} %pad_maximum_fusion.2.late_ref), custom_call_target="tpu_custom_call" | custom-call | flops 134217728 | bytes 16777216 | tf_op jit(solution)/shard_map/pallas_call | solution.py:451
  263.4 4.8 %shard_map.162 = bf16[12,768,128]{2,1,0:T(8,128)(2,1)} custom-call(s32[1]{0:T(128)} %bitcast.sec_ref, bf16[3,768,128]{2,1,0:T(8,128)(2,1)} %get-tuple-element.70.refs_0_, bf16[3,768,128]{2,1,0:T(8,128)(2,1)} %collective-permute-done.6.refs_1_, bf16[3,768,128]{2,1,0:T(8,128)(2,1)} %collective-permute-done.7.refs_2_, bf16[3,768,128]{2,1,0:T(8,128)(2,1)} %copy-done.9, ...), custom_call_target="tpu_custom_call" | custom-call | flops 603979776 | bytes 9437184 | tf_op jit(solution)/shard_map/pallas_call | solution.py:451
  (49 shorter events, 3.8 us)
Async XLA Ops:
  0.6 52.8 %copy-start = (bf16[12,768,128]{2,1,0:T(8,128)(2,1)S(1)}, bf16[12,768,128]{2,1,0:T(8,128)(2,1)}, u32[]{:S(2)}) copy-start(bf16[12,768,128]{2,1,0:T(8,128)(2,1)} %param.14) | copy-start | bytes 7077892
  4.2 32.4 %all-to-all-start = ((bf16[32,96,128]{2,1,0:T(8,128)(2,1)}), bf16[32,96,128]{2,1,0:T(8,128)(2,1)S(1)}, u32[]{:S(2)}, u32[]{:S(2)}) async-start(bf16[32,96,128]{2,1,0:T(8,128)(2,1)} %shard_map.148), calls=%async_computation | async-start | bytes 1572864 | tf_op jit(solution)/shard_map/all_to_all | solution.py:510
  14.3 21.5 %collective-permute-start.1 = (bf16[3,768,128]{2,1,0:T(8,128)(2,1)S(1)}, bf16[3,768,128]{2,1,0:T(8,128)(2,1)S(1)}, u32[]{:S(2)}, u32[]{:S(2)}) collective-permute-start(bf16[3,768,128]{2,1,0:T(8,128)(2,1)S(1)} %get-tuple-element.72), channel_id=1, source_target_pairs={{0,16},{8,24},{16,0},{24,8},{1,17},{9,25},{17,1},{25,9},{2,18},{10... | collective-permute-start | bytes 1769480 | tf_op jit(solution)/shard_map/ppermute | solution.py:513
  16.1 20.5 %collective-permute-start = (bf16[3,768,128]{2,1,0:T(8,128)(2,1)S(1)}, bf16[3,768,128]{2,1,0:T(8,128)(2,1)}, u32[]{:S(2)}, u32[]{:S(2)}) collective-permute-start(bf16[3,768,128]{2,1,0:T(8,128)(2,1)S(1)} %get-tuple-element.73), channel_id=1, source_target_pairs={{0,8},{8,0},{16,24},{24,16},{1,9},{9,1},{17,25},{25,17},{2,10},{10... | collective-permute-start | bytes 1769480 | tf_op jit(solution)/shard_map/ppermute | solution.py:513
  35.8 0.8 copy-start.10
  36.6 0.9 copy-start.2
  46.2 32.1 %all-to-all-start.1 = ((bf16[32,96,128]{2,1,0:T(8,128)(2,1)}), bf16[32,96,128]{2,1,0:T(8,128)(2,1)S(1)}, u32[]{:S(2)}, u32[]{:S(2)}) async-start(bf16[32,96,128]{2,1,0:T(8,128)(2,1)} %get-tuple-element.36), calls=%async_computation.1 | async-start | bytes 1572864 | tf_op jit(solution)/shard_map/all_to_all | solution.py:510
  50.7 25.7 %collective-permute-start.2 = (bf16[3,768,128]{2,1,0:T(8,128)(2,1)}, bf16[3,768,128]{2,1,0:T(8,128)(2,1)}, u32[]{:S(2)}, u32[]{:S(2)}) collective-permute-start(bf16[3,768,128]{2,1,0:T(8,128)(2,1)} %get-tuple-element.71), channel_id=1, source_target_pairs={{0,24},{8,16},{16,8},{24,0},{1,25},{9,17},{17,9},{25,1},{2,26},{10... | collective-permute-start | bytes 1769480 | tf_op jit(solution)/shard_map/ppermute | solution.py:513
  78.3 0.9 copy-start.1
  106.5 11.5 %all-to-all-start.3 = ((bf16[32,24,128]{2,1,0:T(8,128)(2,1)}), bf16[32,24,128]{2,1,0:T(8,128)(2,1)S(1)}, u32[]{:S(2)}, u32[]{:S(2)}) async-start(bf16[32,24,128]{2,1,0:T(8,128)(2,1)} %bitcast.85), calls=%async_computation.3 | async-start | bytes 393216 | tf_op jit(solution)/shard_map/all_to_all | solution.py:510
  117.9 0.7 copy-start.5
  118.6 6.9 %copy-start.11 = (bf16[4,512,128]{2,1,0:T(8,128)(2,1)S(1)}, bf16[4,512,128]{2,1,0:T(8,128)(2,1)}, u32[]{:S(2)}) copy-start(bf16[4,512,128]{2,1,0:T(8,128)(2,1)} %get-tuple-element.45) | copy-start | bytes 1572868
  118.6 6.9 %copy-start.17 = (bf16[512,128]{1,0:T(8,128)(2,1)S(1)}, bf16[512,128]{1,0:T(8,128)(2,1)}, u32[]{:S(2)}) copy-start(bf16[512,128]{1,0:T(8,128)(2,1)} %get-tuple-element.46) | copy-start | bytes 393220
  122.8 16.0 %all-to-all-start.4 = ((bf16[32,24,128]{2,1,0:T(8,128)(2,1)}), bf16[32,24,128]{2,1,0:T(8,128)(2,1)S(1)}, u32[]{:S(2)}, u32[]{:S(2)}) async-start(bf16[32,24,128]{2,1,0:T(8,128)(2,1)} %get-tuple-element.44), calls=%async_computation.4 | async-start | bytes 393216 | tf_op jit(solution)/shard_map/all_to_all | solution.py:510
  125.6 9.8 %collective-permute-start.5 = (bf16[5,128,128]{2,1,0:T(8,128)(2,1)S(1)}, bf16[5,128,128]{2,1,0:T(8,128)(2,1)S(1)}, u32[]{:S(2)}, u32[]{:S(2)}) collective-permute-start(bf16[5,128,128]{2,1,0:T(8,128)(2,1)S(1)} %get-tuple-element.75), channel_id=1, source_target_pairs={{0,24},{8,16},{16,8},{24,0},{1,25},{9,17},{17,9},{25,1},{2,26},{10... | collective-permute-start | bytes 491528 | tf_op jit(solution)/shard_map/ppermute | solution.py:513
  128.3 9.8 %collective-permute-start.3 = (bf16[5,128,128]{2,1,0:T(8,128)(2,1)S(1)}, bf16[5,128,128]{2,1,0:T(8,128)(2,1)S(1)}, u32[]{:S(2)}, u32[]{:S(2)}) collective-permute-start(bf16[5,128,128]{2,1,0:T(8,128)(2,1)S(1)} %get-tuple-element.77), channel_id=1, source_target_pairs={{0,8},{8,0},{16,24},{24,16},{1,9},{9,1},{17,25},{25,17},{2,10},{10... | collective-permute-start | bytes 491528 | tf_op jit(solution)/shard_map/ppermute | solution.py:513
  128.9 9.9 %collective-permute-start.4 = (bf16[5,128,128]{2,1,0:T(8,128)(2,1)S(1)}, bf16[5,128,128]{2,1,0:T(8,128)(2,1)}, u32[]{:S(2)}, u32[]{:S(2)}) collective-permute-start(bf16[5,128,128]{2,1,0:T(8,128)(2,1)S(1)} %get-tuple-element.78), channel_id=1, source_target_pairs={{0,16},{8,24},{16,0},{24,8},{1,17},{9,25},{17,1},{25,9},{2,18},{10... | collective-permute-start | bytes 491528 | tf_op jit(solution)/shard_map/ppermute | solution.py:513
  135.5 2.6 copy-start.15
  138.1 0.7 copy-start.16
  138.8 0.7 copy-start.8
  147.8 12.8 %all-to-all-start.5 = ((bf16[32,24,128]{2,1,0:T(8,128)(2,1)}), bf16[32,24,128]{2,1,0:T(8,128)(2,1)S(1)}, u32[]{:S(2)}, u32[]{:S(2)}) async-start(bf16[32,24,128]{2,1,0:T(8,128)(2,1)} %bitcast.86), calls=%async_computation.5 | async-start | bytes 393216 | tf_op jit(solution)/shard_map/all_to_all | solution.py:510
  160.6 0.7 copy-start.7
  185.8 11.4 %all-to-all-start.7 = ((bf16[32,24,128]{2,1,0:T(8,128)(2,1)}), bf16[32,24,128]{2,1,0:T(8,128)(2,1)S(1)}, u32[]{:S(2)}, u32[]{:S(2)}) async-start(bf16[32,24,128]{2,1,0:T(8,128)(2,1)} %bitcast.84), calls=%async_computation.7 | async-start | bytes 393216 | tf_op jit(solution)/shard_map/all_to_all | solution.py:510
  197.2 0.7 copy-start.6
  203.3 15.0 %all-to-all-start.8 = ((bf16[32,40,128]{2,1,0:T(8,128)(2,1)}), bf16[32,40,128]{2,1,0:T(8,128)(2,1)S(1)}, u32[]{:S(2)}, u32[]{:S(2)}) async-start(bf16[32,40,128]{2,1,0:T(8,128)(2,1)} %get-tuple-element.58), calls=%async_computation.8 | async-start | bytes 655360 | tf_op jit(solution)/shard_map/all_to_all | solution.py:510
  209.1 41.2 %collective-permute-start.8 = (bf16[3,768,128]{2,1,0:T(8,128)(2,1)}, bf16[3,768,128]{2,1,0:T(8,128)(2,1)S(1)}, u32[]{:S(2)}, u32[]{:S(2)}) collective-permute-start(bf16[3,768,128]{2,1,0:T(8,128)(2,1)} %get-tuple-element.67), channel_id=1, source_target_pairs={{0,24},{8,16},{16,8},{24,0},{1,25},{9,17},{17,9},{25,1},{2,26},{10... | collective-permute-start | bytes 1769480 | tf_op jit(solution)/shard_map/ppermute | solution.py:513
  211.8 50.8 %collective-permute-start.7 = (bf16[3,768,128]{2,1,0:T(8,128)(2,1)}, bf16[3,768,128]{2,1,0:T(8,128)(2,1)}, u32[]{:S(2)}, u32[]{:S(2)}) collective-permute-start(bf16[3,768,128]{2,1,0:T(8,128)(2,1)} %get-tuple-element.68), channel_id=1, source_target_pairs={{0,16},{8,24},{16,0},{24,8},{1,17},{9,25},{17,1},{25,9},{2,18},{10... | collective-permute-start | bytes 1769480 | tf_op jit(solution)/shard_map/ppermute | solution.py:513
  212.3 50.2 %collective-permute-start.6 = (bf16[3,768,128]{2,1,0:T(8,128)(2,1)}, bf16[3,768,128]{2,1,0:T(8,128)(2,1)}, u32[]{:S(2)}, u32[]{:S(2)}) collective-permute-start(bf16[3,768,128]{2,1,0:T(8,128)(2,1)} %get-tuple-element.69), channel_id=1, source_target_pairs={{0,8},{8,0},{16,24},{24,16},{1,9},{9,1},{17,25},{25,17},{2,10},{10... | collective-permute-start | bytes 1769480 | tf_op jit(solution)/shard_map/ppermute | solution.py:513
  218.4 0.7 copy-start.3
  227.5 20.2 %all-to-all-start.9 = ((bf16[8,112,128]{2,1,0:T(8,128)(2,1)}), bf16[8,112,128]{2,1,0:T(8,128)(2,1)S(1)}, u32[]{:S(2)}, u32[]{:S(2)}) async-start(bf16[8,112,128]{2,1,0:T(8,128)(2,1)} %get-tuple-element.59), calls=%async_computation.9 | async-start | bytes 458752 | tf_op jit(solution)/shard_map/all_to_all | solution.py:729
  232.1 10.2 %collective-permute-start.14 = (bf16[3,128,128]{2,1,0:T(8,128)(2,1)S(1)}, bf16[3,128,128]{2,1,0:T(8,128)(2,1)S(1)}, u32[]{:S(2)}, u32[]{:S(2)}) collective-permute-start(bf16[3,128,128]{2,1,0:T(8,128)(2,1)S(1)} %get-tuple-element.80), channel_id=1, source_target_pairs={{0,24},{8,16},{16,8},{24,0},{1,25},{9,17},{17,9},{25,1},{2,26},{10... | collective-permute-start | bytes 294920 | tf_op jit(solution)/shard_map/ppermute | solution.py:513
  232.5 13.1 %collective-permute-start.13 = (bf16[3,128,128]{2,1,0:T(8,128)(2,1)S(1)}, bf16[3,128,128]{2,1,0:T(8,128)(2,1)S(1)}, u32[]{:S(2)}, u32[]{:S(2)}) collective-permute-start(bf16[3,128,128]{2,1,0:T(8,128)(2,1)S(1)} %get-tuple-element.81), channel_id=1, source_target_pairs={{0,16},{8,24},{16,0},{24,8},{1,17},{9,25},{17,1},{25,9},{2,18},{10... | collective-permute-start | bytes 294920 | tf_op jit(solution)/shard_map/ppermute | solution.py:513
  242.3 4.6 %collective-permute-start.12 = (bf16[3,128,128]{2,1,0:T(8,128)(2,1)S(1)}, bf16[3,128,128]{2,1,0:T(8,128)(2,1)S(1)}, u32[]{:S(2)}, u32[]{:S(2)}) collective-permute-start(bf16[3,128,128]{2,1,0:T(8,128)(2,1)S(1)} %get-tuple-element.82), channel_id=1, source_target_pairs={{0,8},{8,0},{16,24},{24,16},{1,9},{9,1},{17,25},{25,17},{2,10},{10... | collective-permute-start | bytes 294920 | tf_op jit(solution)/shard_map/ppermute | solution.py:513
  247.7 14.2 %copy-start.4 = (bf16[8,112,128]{2,1,0:T(8,128)(2,1)}, bf16[8,112,128]{2,1,0:T(8,128)(2,1)S(1)}, u32[]{:S(2)}) copy-start(bf16[8,112,128]{2,1,0:T(8,128)(2,1)S(1)} %all-to-all-done.9.refs_4_) | copy-start | bytes 688132
  247.7 14.8 %collective-permute-start.11 = (bf16[8,112,128]{2,1,0:T(8,128)(2,1)S(1)}, bf16[8,112,128]{2,1,0:T(8,128)(2,1)S(1)}, u32[]{:S(2)}, u32[]{:S(2)}) collective-permute-start(bf16[8,112,128]{2,1,0:T(8,128)(2,1)S(1)} %all-to-all-done.9.refs_4_), channel_id=1, source_target_pairs={{24,0},{25,1},{26,2},{27,3},{28,4},{29,5},{30,6},{31,7}} | collective-permute-start | bytes 688136 | tf_op jit(solution)/shard_map/ppermute | solution.py:760
  249.0 13.6 %collective-permute-start.10 = (bf16[8,112,128]{2,1,0:T(8,128)(2,1)S(1)}, bf16[8,112,128]{2,1,0:T(8,128)(2,1)S(1)}, u32[]{:S(2)}, u32[]{:S(2)}) collective-permute-start(bf16[8,112,128]{2,1,0:T(8,128)(2,1)S(1)} %all-to-all-done.9.refs_4_), channel_id=1, source_target_pairs={{16,0},{17,1},{18,2},{19,3},{20,4},{21,5},{22,6},{23,7}} | collective-permute-start | bytes 688136 | tf_op jit(solution)/shard_map/ppermute | solution.py:760
  250.3 11.6 %copy-start.9 = (bf16[3,768,128]{2,1,0:T(8,128)(2,1)}, bf16[3,768,128]{2,1,0:T(8,128)(2,1)S(1)}, u32[]{:S(2)}) copy-start(bf16[3,768,128]{2,1,0:T(8,128)(2,1)S(1)} %collective-permute-done.8.refs_3_) | copy-start | bytes 1769476
  250.3 12.3 %collective-permute-start.9 = (bf16[8,112,128]{2,1,0:T(8,128)(2,1)S(1)}, bf16[8,112,128]{2,1,0:T(8,128)(2,1)S(1)}, u32[]{:S(2)}, u32[]{:S(2)}) collective-permute-start(bf16[8,112,128]{2,1,0:T(8,128)(2,1)S(1)} %all-to-all-done.9.refs_4_), channel_id=1, source_target_pairs={{8,0},{9,1},{10,2},{11,3},{12,4},{13,5},{14,6},{15,7}} | collective-permute-start | bytes 688136 | tf_op jit(solution)/shard_map/ppermute | solution.py:760
  262.5 0.7 copy-start.12
  262.6 0.8 copy-start.13
  262.6 0.8 copy-start.14

commit v4 on v3

--- a/solution.py
+++ b/solution.py
@@ -14,7 +14,7 @@
 BF16 = jnp.bfloat16
 F32 = jnp.float32
 ALL = ("section", "row")
-VMEM_LIMIT = 56 * 1024 * 1024
+VMEM_LIMIT = 63 * 1024 * 1024
 CHUNK = 32
 
 
@@ -282,19 +282,27 @@
 
 
 def start_kernel(
-    packed, devices, sec_ref, cot_ref, slope_ref, state_ref, synth_ref, low_ref, send_ref, acc_ref
+    step, packed, devices, sec_ref, recv_ref, cot_ref, state_ref, synth_t_ref, synth_ref, mix_ref,
+    bias_ref, low_ref, send_ref, acc_ref
 ):
     rows, cells, channels = cot_ref.shape
+    modes = unpack_rows(recv_ref[...], range(step * rows, (step + 1) * rows), packed)
+    mixing = mix_ref[...]
+    bias = bias_ref[...]
     tile = 256
     spec, acc = None, None
     for w in range(0, cells, tile):
+        smooth = dot(synth_t_ref[w : w + tile, :], modes)
         lows = []
         for r in range(rows):
-            low, term = finish_tile(
-                r, w, tile, cot_ref[r, w : w + tile, :], slope_ref, state_ref, low_ref
-            )
+            field = state_ref[0, r, w : w + tile, :]
+            pre = smooth[:, r * channels : (r + 1) * channels] + dot(field, mixing) + bias
+            low = cot_ref[r, w : w + tile, :].astype(F32) * gelu_derivative(pre)
+            low = low.astype(BF16)
+            low_ref[r, w : w + tile, :] = low
+            term = dot(field, low, ((0,), (0,)))
+            acc = term if acc is None else acc + term
             lows.append(low)
-            acc = term if acc is None else acc + term
         part = dot(synth_ref[:, w : w + tile], jnp.concatenate(lows, axis=1))
         spec = part if spec is None else spec + part
     acc_ref[...] = acc
@@ -579,7 +587,7 @@
     shape3 = (rows, cells, channels)
     bias2 = bias.reshape(1, channels)
     slopes = [None] * sections
-    for s in range(sections - 1, -1, -1):
+    for s in range(sections - 2, -1, -1):
         (slopes[s],) = call(
             functools.partial(slope_kernel, s, rows, packed),
             [jax.ShapeDtypeStruct(shape3, F32)],
@@ -609,10 +617,18 @@
     s = sections - 1
     carried = lax.dynamic_slice_in_dim(cotangent, section * rows, rows, 0)
     low, send, acc = call(
-        functools.partial(start_kernel, packed, devices),
+        functools.partial(start_kernel, s, packed, devices),
         turn_outs,
-        [whole(shape3), whole(shape3), state_spec(s), whole(synth.shape)],
-        (carried, slopes[s], all_states, synth),
+        [
+            whole(back.shape),
+            whole(shape3),
+            state_spec(s),
+            whole(synth_t.shape),
+            whole(synth.shape),
+            whole(local_weight.shape),
+            whole(bias2.shape),
+        ],
+        (back, carried, all_states, synth_t, synth, local_weight, bias2),
         prefetch=sec,
         flops=2 * total * cells * rows * channels,
         moved=10 * rows * cells * channels,

time: 270 us -> 267 us (0.989)
    pallas_call x16 -> x15, Pallas kernels: 91.2 us -> 88.8 us  [call(): pl.pallas_call(kernel, out_shape=outs, grid_spec=pltpu.PrefetchScalarGrid...]
    unnamed x36 -> x28, local copies, waits for them, and re-layouts: 7.55 us -> 6.82 us
  transfers between devices with their start and end apart: 23 -> 23, of which waited for: 10 -> 11; matrix products, arithmetic and copies ran while one was open for 6% -> 7% of each run, Pallas kernels for 11% -> 11%
where the time goes in v4:
time: 267 us; the launch traced here: 265 us
  Pallas kernels  88.8 us (33%)
  waiting for transfers between devices  76.2 us (29%)
  starting transfers between devices  50 us (19%)
  blocking collectives  24.6 us (9%)
  local copies, waits for them, and re-layouts  17.5 us (7%)
  other arithmetic  7.05 us (3%)
    pallas_call x15, Pallas kernels, call(): pl.pallas_call(kernel, out_shape=outs, grid_spec=pltpu.PrefetchScalarGrid...  88.8 us
    ppermute x12, waiting for transfers between devices, share(): return lax.ppermute(piece, 'section', [(i, i ^ d) for i in range(sections)])  56.7 us
    all_to_all x7, starting transfers between devices, exchange(): return lax.all_to_all(values, ALL, 0, 0, tiled=True)  27.1 us
    all_to_all x2, blocking collectives, exchange(): return lax.all_to_all(values, ALL, 0, 0, tiled=True)  24.6 us
    all_to_all x7, waiting for transfers between devices, exchange(): return lax.all_to_all(values, ALL, 0, 0, tiled=True)  19.6 us
    ppermute x12, starting transfers between devices, share(): return lax.ppermute(piece, 'section', [(i, i ^ d) for i in range(sections)])  15.6 us
    unnamed x28, local copies, waits for them, and re-layouts  6.82 us
  transfers between devices with their start and end apart: 23, of which 11 were waited for; matrix products, arithmetic and copies ran while one was open for 7% of the time, Pallas kernels for 11%

profile of v4, /device:TPU:0, one launch (start us, length us, event | category | flops | bytes accessed | tf_op | source)
XLA Modules:
  0.0 265.1 jit_solution(4399998528092936248)
XLA Ops:
  0.6 3.4 %shard_map.148 = bf16[32,96,128]{2,1,0:T(8,128)(2,1)} custom-call(bf16[12,768,128]{2,1,0:T(8,128)(2,1)} %bitcast.73, bf16[256,768]{1,0:T(8,128)(2,1)} %constant.75.clone.basis_ref), custom_call_target="tpu_custom_call" | custom-call | flops 603979776 | bytes 4718592 | tf_op jit(solution)/shard_map/pallas_call | solution.py:459
  4.0 7.3 %all-to-all-start = ((bf16[32,96,128]{2,1,0:T(8,128)(2,1)}), bf16[32,96,128]{2,1,0:T(8,128)(2,1)S(1)}, u32[]{:S(2)}, u32[]{:S(2)}) async-start(bf16[32,96,128]{2,1,0:T(8,128)(2,1)} %shard_map.148), calls=%async_computation | async-start | bytes 1572864 | tf_op jit(solution)/shard_map/all_to_all | solution.py:518
  11.3 2.8 %dynamic-slice_bitcast_fusion.4 = (bf16[3,768,128]{2,1,0:T(8,128)(2,1)}, bf16[3,768,128]{2,1,0:T(8,128)(2,1)S(1)}, bf16[3,768,128]{2,1,0:T(8,128)(2,1)S(1)}, bf16[3,768,128]{2,1,0:T(8,128)(2,1)}) fusion(bf16[4,3,768,128]{3,2,1,0:T(8,128)(2,1)} %bitcast.74, s32[]{:T(128)S(6)} %select_n.34, s32[]{:T(128)S(6)} %select_n.32, s32[]{:T(128)S(6)} %select_n.31, ...), kind=kLoop, calls=%fused_computation.15 | loop fusion | bytes 4718608 | tf_op jit(solution)/shard_map/jit(dynamic_index_in_dim)/squeeze | solution.py:526
  14.1 1.8 collective-permute-start.1
  15.9 1.5 collective-permute-start
  17.4 18.3 %collective-permute-done.1 = bf16[3,768,128]{2,1,0:T(8,128)(2,1)S(1)} collective-permute-done((bf16[3,768,128]{2,1,0:T(8,128)(2,1)S(1)}, bf16[3,768,128]{2,1,0:T(8,128)(2,1)S(1)}, u32[]{:S(2)}, u32[]{:S(2)}) %collective-permute-start.1) | collective-permute-done | bytes 589856 | tf_op jit(solution)/shard_map/ppermute | solution.py:521
  35.6 0.8 copy-done.9
  36.5 0.9 copy-done.1
  37.3 8.7 %shard_map.149 = (bf16[4,512,128]{2,1,0:T(8,128)(2,1)}, bf16[32,96,128]{2,1,0:T(8,128)(2,1)}) custom-call(s32[1]{0:T(128)} %bitcast.sec_ref, bf16[3072,128]{1,0:T(8,128)(2,1)} %bitcast.75, bf16[512,768]{1,0:T(8,128)(2,1)} %constant.78.clone.lat_any, bf16[768,512]{1,0:T(8,128)(2,1)} %constant.80.clone.inv_any, bf16[64,16,2,128,128]{4,3,2,1,0:T(8,128)(2,1)} %all_ref.9), custom_call_target="tpu_custom_call" | custom-call | flops 67108864 | bytes 16777216 | tf_op jit(solution)/shard_map/pallas_call | solution.py:459
  46.1 4.4 %all-to-all-start.1 = ((bf16[32,96,128]{2,1,0:T(8,128)(2,1)}), bf16[32,96,128]{2,1,0:T(8,128)(2,1)S(1)}, u32[]{:S(2)}, u32[]{:S(2)}) async-start(bf16[32,96,128]{2,1,0:T(8,128)(2,1)} %get-tuple-element.36), calls=%async_computation.1 | async-start | bytes 1572864 | tf_op jit(solution)/shard_map/all_to_all | solution.py:518
  50.5 2.7 %collective-permute-start.2 = (bf16[3,768,128]{2,1,0:T(8,128)(2,1)}, bf16[3,768,128]{2,1,0:T(8,128)(2,1)S(1)}, u32[]{:S(2)}, u32[]{:S(2)}) collective-permute-start(bf16[3,768,128]{2,1,0:T(8,128)(2,1)} %get-tuple-element.71), channel_id=1, source_target_pairs={{0,24},{8,16},{16,8},{24,0},{1,25},{9,17},{17,9},{25,1},{2,26},{10... | collective-permute-start | bytes 1769480 | tf_op jit(solution)/shard_map/ppermute | solution.py:521
  53.3 1.9 constant_dynamic-slice_fusion.cot_ref
  55.2 2.7 %maximum_maximum_fusion = bf16[4,3,768,128]{3,2,1,0:T(8,128)(2,1)} fusion(bf16[1,3,768,128]{3,2,1,0:T(8,128)(2,1)S(1)} %bitcast.82, bf16[1,3,768,128]{3,2,1,0:T(8,128)(2,1)} %bitcast.8, bf16[1,3,768,128]{3,2,1,0:T(8,128)(2,1)S(1)} %bitcast.77, bf16[4]{0:T(256)(128)(2,1)S(1)} %pad.16.clone), kind=kLoop, calls=%fused_computation | loop fusion | flops 3538944 | bytes 4128776 | tf_op jit(solution)/shard_map/stack | solution.py:544
  58.0 18.1 %collective-permute-done.2 = bf16[3,768,128]{2,1,0:T(8,128)(2,1)S(1)} collective-permute-done((bf16[3,768,128]{2,1,0:T(8,128)(2,1)}, bf16[3,768,128]{2,1,0:T(8,128)(2,1)S(1)}, u32[]{:S(2)}, u32[]{:S(2)}) %collective-permute-start.2) | collective-permute-done | bytes 589856 | tf_op jit(solution)/shard_map/ppermute | solution.py:521
  76.1 0.9 bitcast_dynamic-update-slice_fusion.state_ref
  77.0 0.9 copy-done
  77.9 4.1 %shard_map.150 = (bf16[3,768,128]{2,1,0:T(8,128)(2,1)}, bf16[32,24,128]{2,1,0:T(8,128)(2,1)}, f32[128,128]{1,0:T(8,128)}) custom-call(s32[1]{0:T(128)} %bitcast.sec_ref, bf16[32,96,128]{2,1,0:T(8,128)(2,1)} %copy-done, bf16[3,768,128]{2,1,0:T(8,128)(2,1)} %constant_dynamic-slice_fusion.cot_ref, ...), custom_call_target="tpu_custom_call" | custom-call | flops 150994944 | bytes 2949120 | tf_op jit(solution)/shard_map/pallas_call | solution.py:459
  82.0 12.6 %all_to_all.50 = bf16[32,24,128]{2,1,0:T(8,128)(2,1)} all-to-all(bf16[32,24,128]{2,1,0:T(8,128)(2,1)} %get-tuple-element.40), channel_id=1, replica_groups=mesh['section'=4,'row'=8] {'section','row'}, dimensions={0} | all-to-all | bytes 393216 | tf_op jit(solution)/shard_map/all_to_all | solution.py:518
  94.6 8.3 %shard_map.151 = (bf16[512,128]{1,0:T(8,128)(2,1)}, bf16[768,128]{1,0:T(8,128)(2,1)}) custom-call(s32[1]{0:T(128)} %bitcast.sec_ref, bf16[768,128]{1,0:T(8,128)(2,1)} %bitcast.80, bf16[512,768]{1,0:T(8,128)(2,1)} %constant.79.clone.lat_any, bf16[768,512]{1,0:T(8,128)(2,1)} %constant.80.clone.inv_any, bf16[64,16,2,128,128]{4,3,2,1,0:T(8,128)(2,1)} %all_ref.9), custom_call_target="tpu_custom_call" | custom-call | flops 33554432 | bytes 16777216 | tf_op jit(solution)/shard_map/pallas_call | solution.py:459
  103.0 2.7 %all-to-all-start.3 = ((bf16[32,24,128]{2,1,0:T(8,128)(2,1)}), bf16[32,24,128]{2,1,0:T(8,128)(2,1)S(1)}, u32[]{:S(2)}, u32[]{:S(2)}) async-start(bf16[32,24,128]{2,1,0:T(8,128)(2,1)} %bitcast.85), calls=%async_computation.3 | async-start | bytes 393216 | tf_op jit(solution)/shard_map/all_to_all | solution.py:518
  105.7 1.9 fusion.8.carried_ref
  107.6 3.4 %shard_map.152.slope_ref = f32[3,768,128]{2,1,0:T(8,128)} custom-call(s32[1]{0:T(128)} %bitcast.sec_ref, bf16[32,96,128]{2,1,0:T(8,128)(2,1)} %copy-done, bf16[4,3,768,128]{3,2,1,0:T(8,128)(2,1)} %bitcast_dynamic-update-slice_fusion.state_ref, bf16[768,256]{1,0:T(8,128)(2,1)} %constant.77.clone.synth_t_ref.synth_ref, bf16[128,128]{1,0:T(8,128)(2,1)} %mix_ref.13, ...), custom_call_target="tpu_custom_call" | custom-call | flops 150994944 | bytes 2949120 | tf_op jit(solution)/shard_map/pallas_call | solution.py:459
  111.0 3.4 %all-to-all-done.3.recv_ref = bf16[32,24,128]{2,1,0:T(8,128)(2,1)S(1)} async-done(((bf16[32,24,128]{2,1,0:T(8,128)(2,1)}), bf16[32,24,128]{2,1,0:T(8,128)(2,1)S(1)}, u32[]{:S(2)}, u32[]{:S(2)}) %all-to-all-start.3) | async-done | bytes 196640 | tf_op jit(solution)/shard_map/all_to_all | solution.py:518
  114.4 0.7 copy-done.5
  115.1 4.1 %shard_map.153 = (bf16[4,3,768,128]{3,2,1,0:T(8,128)(2,1)}, bf16[3,768,128]{2,1,0:T(8,128)(2,1)}, bf16[32,24,128]{2,1,0:T(8,128)(2,1)}, f32[128,128]{1,0:T(8,128)}) custom-call(s32[1]{0:T(128)} %bitcast.sec_ref, bf16[32,24,128]{2,1,0:T(8,128)(2,1)} %copy-done.5, bf16[1,3,768,128]{3,2,1,0:T(8,128)(2,1)} %fusion.8.carried_ref, ...), custom_call_target="tpu_custom_call" | custom-call | flops 301989888 | bytes 4718592 | tf_op jit(solution)/shard_map/pallas_call | solution.py:459
  119.3 2.7 %all-to-all-start.4 = ((bf16[32,24,128]{2,1,0:T(8,128)(2,1)}), bf16[32,24,128]{2,1,0:T(8,128)(2,1)S(1)}, u32[]{:S(2)}, u32[]{:S(2)}) async-start(bf16[32,24,128]{2,1,0:T(8,128)(2,1)} %get-tuple-element.44), calls=%async_computation.4 | async-start | bytes 393216 | tf_op jit(solution)/shard_map/all_to_all | solution.py:518
  122.0 0.9 fusion.1
  122.9 2.7 %collective-permute-start.5 = (bf16[5,128,128]{2,1,0:T(8,128)(2,1)S(1)}, bf16[5,128,128]{2,1,0:T(8,128)(2,1)S(1)}, u32[]{:S(2)}, u32[]{:S(2)}) collective-permute-start(bf16[5,128,128]{2,1,0:T(8,128)(2,1)S(1)} %get-tuple-element.75), channel_id=1, source_target_pairs={{0,24},{8,16},{16,8},{24,0},{1,25},{9,17},{17,9},{25,1},{2,26},{10... | collective-permute-start | bytes 491528 | tf_op jit(solution)/shard_map/ppermute | solution.py:521
  126.4 5.7 %collective-permute-done.5 = bf16[5,128,128]{2,1,0:T(8,128)(2,1)S(1)} collective-permute-done((bf16[5,128,128]{2,1,0:T(8,128)(2,1)S(1)}, bf16[5,128,128]{2,1,0:T(8,128)(2,1)S(1)}, u32[]{:S(2)}, u32[]{:S(2)}) %collective-permute-start.5) | collective-permute-done | bytes 163872 | tf_op jit(solution)/shard_map/ppermute | solution.py:521
  132.1 2.9 %collective-permute-done.3 = bf16[5,128,128]{2,1,0:T(8,128)(2,1)S(1)} collective-permute-done((bf16[5,128,128]{2,1,0:T(8,128)(2,1)S(1)}, bf16[5,128,128]{2,1,0:T(8,128)(2,1)S(1)}, u32[]{:S(2)}, u32[]{:S(2)}) %collective-permute-start.3) | collective-permute-done | bytes 163872 | tf_op jit(solution)/shard_map/ppermute | solution.py:521
  135.3 0.7 copy-done.8
  136.0 8.3 %shard_map.154 = (bf16[512,128]{1,0:T(8,128)(2,1)}, bf16[768,128]{1,0:T(8,128)(2,1)}) custom-call(s32[1]{0:T(128)} %bitcast.sec_ref, bf16[768,128]{1,0:T(8,128)(2,1)} %bitcast.78, bf16[512,768]{1,0:T(8,128)(2,1)} %constant.79.clone.lat_any, bf16[768,512]{1,0:T(8,128)(2,1)} %constant.80.clone.inv_any, bf16[64,16,2,128,128]{4,3,2,1,0:T(8,128)(2,1)} %all_ref.9), custom_call_target="tpu_custom_call" | custom-call | flops 33554432 | bytes 16777216 | tf_op jit(solution)/shard_map/pallas_call | solution.py:459
  144.4 4.6 %all-to-all-start.5 = ((bf16[32,24,128]{2,1,0:T(8,128)(2,1)}), bf16[32,24,128]{2,1,0:T(8,128)(2,1)S(1)}, u32[]{:S(2)}, u32[]{:S(2)}) async-start(bf16[32,24,128]{2,1,0:T(8,128)(2,1)} %bitcast.86), calls=%async_computation.5 | async-start | bytes 393216 | tf_op jit(solution)/shard_map/all_to_all | solution.py:518
  149.0 3.4 %shard_map.155.slope_ref = f32[3,768,128]{2,1,0:T(8,128)} custom-call(s32[1]{0:T(128)} %bitcast.sec_ref, bf16[32,96,128]{2,1,0:T(8,128)(2,1)} %copy-done, bf16[4,3,768,128]{3,2,1,0:T(8,128)(2,1)} %bitcast_dynamic-update-slice_fusion.state_ref, bf16[768,256]{1,0:T(8,128)(2,1)} %constant.77.clone.synth_t_ref.synth_ref, bf16[128,128]{1,0:T(8,128)(2,1)} %mix_ref.13, ...), custom_call_target="tpu_custom_call" | custom-call | flops 150994944 | bytes 2949120 | tf_op jit(solution)/shard_map/pallas_call | solution.py:459
  152.4 5.1 %all-to-all-done.5.recv_ref = bf16[32,24,128]{2,1,0:T(8,128)(2,1)S(1)} async-done(((bf16[32,24,128]{2,1,0:T(8,128)(2,1)}), bf16[32,24,128]{2,1,0:T(8,128)(2,1)S(1)}, u32[]{:S(2)}, u32[]{:S(2)}) %all-to-all-start.5) | async-done | bytes 196640 | tf_op jit(solution)/shard_map/all_to_all | solution.py:518
  157.5 0.7 copy-done.7
  158.2 4.1 %shard_map.156 = (bf16[4,3,768,128]{3,2,1,0:T(8,128)(2,1)}, bf16[3,768,128]{2,1,0:T(8,128)(2,1)}, bf16[32,24,128]{2,1,0:T(8,128)(2,1)}, f32[128,128]{1,0:T(8,128)}) custom-call(s32[1]{0:T(128)} %bitcast.sec_ref, bf16[32,24,128]{2,1,0:T(8,128)(2,1)} %copy-done.7, ...), custom_call_target="tpu_custom_call", output_to_operand_aliasing={{0}: (2, {})} | custom-call | flops 301989888 | bytes 4718592 | tf_op jit(solution)/shard_map/pallas_call | solution.py:459
  162.3 12.0 %all_to_all.51 = bf16[32,24,128]{2,1,0:T(8,128)(2,1)} all-to-all(bf16[32,24,128]{2,1,0:T(8,128)(2,1)} %get-tuple-element.52), channel_id=1, replica_groups=mesh['section'=4,'row'=8] {'section','row'}, dimensions={0} | all-to-all | bytes 393216 | tf_op jit(solution)/shard_map/all_to_all | solution.py:518
  174.3 8.4 %shard_map.157 = (bf16[512,128]{1,0:T(8,128)(2,1)}, bf16[768,128]{1,0:T(8,128)(2,1)}) custom-call(s32[1]{0:T(128)} %bitcast.sec_ref, bf16[768,128]{1,0:T(8,128)(2,1)} %bitcast.79, bf16[512,768]{1,0:T(8,128)(2,1)} %constant.79.clone.lat_any, bf16[768,512]{1,0:T(8,128)(2,1)} %constant.80.clone.inv_any, bf16[64,16,2,128,128]{4,3,2,1,0:T(8,128)(2,1)} %all_ref.9), custom_call_target="tpu_custom_call" | custom-call | flops 33554432 | bytes 16777216 | tf_op jit(solution)/shard_map/pallas_call | solution.py:459
  182.7 2.6 all-to-all-start.7
  185.3 3.4 %shard_map.158.slope_ref = f32[3,768,128]{2,1,0:T(8,128)} custom-call(s32[1]{0:T(128)} %bitcast.sec_ref, bf16[32,96,128]{2,1,0:T(8,128)(2,1)} %copy-done, bf16[4,3,768,128]{3,2,1,0:T(8,128)(2,1)} %bitcast_dynamic-update-slice_fusion.state_ref, bf16[768,256]{1,0:T(8,128)(2,1)} %constant.77.clone.synth_t_ref.synth_ref, bf16[128,128]{1,0:T(8,128)(2,1)} %mix_ref.13, ...), custom_call_target="tpu_custom_call" | custom-call | flops 150994944 | bytes 2949120 | tf_op jit(solution)/shard_map/pallas_call | solution.py:459
  188.7 5.3 %all-to-all-done.7.recv_ref = bf16[32,24,128]{2,1,0:T(8,128)(2,1)S(1)} async-done(((bf16[32,24,128]{2,1,0:T(8,128)(2,1)}), bf16[32,24,128]{2,1,0:T(8,128)(2,1)S(1)}, u32[]{:S(2)}, u32[]{:S(2)}) %all-to-all-start.7) | async-done | bytes 196640 | tf_op jit(solution)/shard_map/all_to_all | solution.py:518
  194.1 0.7 copy-done.6
  194.7 5.5 %shard_map.159 = (bf16[4,3,768,128]{3,2,1,0:T(8,128)(2,1)}, bf16[3,768,128]{2,1,0:T(8,128)(2,1)}, bf16[32,40,128]{2,1,0:T(8,128)(2,1)}, f32[128,128]{1,0:T(8,128)}) custom-call(s32[1]{0:T(128)} %bitcast.sec_ref, bf16[32,24,128]{2,1,0:T(8,128)(2,1)} %copy-done.6, ...), custom_call_target="tpu_custom_call", output_to_operand_aliasing={{0}: (2, {})} | custom-call | flops 301989888 | bytes 4718592 | tf_op jit(solution)/shard_map/pallas_call | solution.py:459
  200.2 2.7 %all-to-all-start.8 = ((bf16[32,40,128]{2,1,0:T(8,128)(2,1)}), bf16[32,40,128]{2,1,0:T(8,128)(2,1)S(1)}, u32[]{:S(2)}, u32[]{:S(2)}) async-start(bf16[32,40,128]{2,1,0:T(8,128)(2,1)} %get-tuple-element.58), calls=%async_computation.8 | async-start | bytes 655360 | tf_op jit(solution)/shard_map/all_to_all | solution.py:518
  203.0 3.1 %dynamic-slice_bitcast_fusion = (bf16[3,768,128]{2,1,0:T(8,128)(2,1)}, bf16[3,768,128]{2,1,0:T(8,128)(2,1)}, bf16[3,768,128]{2,1,0:T(8,128)(2,1)}, bf16[3,768,128]{2,1,0:T(8,128)(2,1)}) fusion(bf16[4,3,768,128]{3,2,1,0:T(8,128)(2,1)} %get-tuple-element.57, s32[]{:T(128)S(6)} %select_n.34, s32[]{:T(128)S(6)} %select_n.32, s32[]{:T(128)S(6)} %select_n.31, ...), kind=kLoop, calls=%fused_computation.11 | loop fusion | bytes 4718608 | tf_op jit(solution)/shard_map/jit(dynamic_index_in_dim)/squeeze | solution.py:715
  206.1 2.7 %collective-permute-start.8 = (bf16[3,768,128]{2,1,0:T(8,128)(2,1)}, bf16[3,768,128]{2,1,0:T(8,128)(2,1)}, u32[]{:S(2)}, u32[]{:S(2)}) collective-permute-start(bf16[3,768,128]{2,1,0:T(8,128)(2,1)} %get-tuple-element.67), channel_id=1, source_target_pairs={{0,24},{8,16},{16,8},{24,0},{1,25},{9,17},{17,9},{25,1},{2,26},{10... | collective-permute-start | bytes 1769480 | tf_op jit(solution)/shard_map/ppermute | solution.py:521
  209.5 5.7 %all-to-all-done.8.x_any = bf16[32,40,128]{2,1,0:T(8,128)(2,1)S(1)} async-done(((bf16[32,40,128]{2,1,0:T(8,128)(2,1)}), bf16[32,40,128]{2,1,0:T(8,128)(2,1)S(1)}, u32[]{:S(2)}, u32[]{:S(2)}) %all-to-all-start.8) | async-done | bytes 327712 | tf_op jit(solution)/shard_map/all_to_all | solution.py:518
  215.2 0.7 copy-done.3
  216.0 8.4 %shard_map.160 = (bf16[512,128]{1,0:T(8,128)(2,1)}, bf16[8,112,128]{2,1,0:T(8,128)(2,1)}) custom-call(s32[1]{0:T(128)} %bitcast.sec_ref, bf16[32,40,128]{2,1,0:T(8,128)(2,1)} %copy-done.3, bf16[512,768]{1,0:T(8,128)(2,1)} %constant.79.clone.lat_any, bf16[768,512]{1,0:T(8,128)(2,1)} %constant.81.clone.inv_any, bf16[64,16,2,128,128]{4,3,2,1,0:T(8,128)(2,1)} %all_ref.9), custom_call_target="tpu_custom_call" | custom-call | flops 33554432 | bytes 16777216 | tf_op jit(solution)/shard_map/pallas_call | solution.py:459
  224.4 3.4 %all-to-all-start.9 = ((bf16[8,112,128]{2,1,0:T(8,128)(2,1)}), bf16[8,112,128]{2,1,0:T(8,128)(2,1)S(1)}, u32[]{:S(2)}, u32[]{:S(2)}) async-start(bf16[8,112,128]{2,1,0:T(8,128)(2,1)} %get-tuple-element.59), calls=%async_computation.9 | async-start | bytes 458752 | tf_op jit(solution)/shard_map/all_to_all | solution.py:745
  227.8 1.1 pad_maximum_fusion.1
  229.4 0.7 collective-permute-start.13
  230.1 9.1 %collective-permute-done.14 = bf16[3,128,128]{2,1,0:T(8,128)(2,1)S(1)} collective-permute-done((bf16[3,128,128]{2,1,0:T(8,128)(2,1)S(1)}, bf16[3,128,128]{2,1,0:T(8,128)(2,1)S(1)}, u32[]{:S(2)}, u32[]{:S(2)}) %collective-permute-start.14) | collective-permute-done | bytes 98336 | tf_op jit(solution)/shard_map/ppermute | solution.py:521
  239.2 1.4 collective-permute-start.12
  240.6 0.9 pad_maximum_fusion.first_ref
  241.6 2.3 collective-permute-done.12
  243.8 0.8 pad_maximum_fusion.2.late_ref
  244.7 1.3 collective-permute-start.11
  245.9 1.3 collective-permute-start.10
  247.3 1.3 collective-permute-start.9
  248.6 10.3 %shard_map.162 = bf16[16,16,2,128,128]{4,3,2,1,0:T(8,128)(2,1)} custom-call(s32[1]{0:T(128)} %bitcast.sec_ref, bf16[4,5,128,128]{3,2,1,0:T(8,128)(2,1)} %pad_maximum_fusion.first_ref, bf16[4,3,128,128]{3,2,1,0:T(8,128)(2,1)} %pad_maximum_fusion.2.late_ref), custom_call_target="tpu_custom_call" | custom-call | flops 134217728 | bytes 16777216 | tf_op jit(solution)/shard_map/pallas_call | solution.py:459
  259.5 0.7 copy-done.12
  260.3 4.8 %shard_map.161 = bf16[12,768,128]{2,1,0:T(8,128)(2,1)} custom-call(s32[1]{0:T(128)} %bitcast.sec_ref, bf16[3,768,128]{2,1,0:T(8,128)(2,1)} %get-tuple-element.70.refs_0_, bf16[3,768,128]{2,1,0:T(8,128)(2,1)} %collective-permute-done.6.refs_1_, bf16[3,768,128]{2,1,0:T(8,128)(2,1)} %collective-permute-done.7.refs_2_, ...), custom_call_target="tpu_custom_call" | custom-call | flops 603979776 | bytes 9437184 | tf_op jit(solution)/shard_map/pallas_call | solution.py:459
  (40 shorter events, 3.3 us)
Async XLA Ops:
  4.0 32.4 %all-to-all-start = ((bf16[32,96,128]{2,1,0:T(8,128)(2,1)}), bf16[32,96,128]{2,1,0:T(8,128)(2,1)S(1)}, u32[]{:S(2)}, u32[]{:S(2)}) async-start(bf16[32,96,128]{2,1,0:T(8,128)(2,1)} %shard_map.148), calls=%async_computation | async-start | bytes 1572864 | tf_op jit(solution)/shard_map/all_to_all | solution.py:518
  14.1 21.5 %collective-permute-start.1 = (bf16[3,768,128]{2,1,0:T(8,128)(2,1)S(1)}, bf16[3,768,128]{2,1,0:T(8,128)(2,1)S(1)}, u32[]{:S(2)}, u32[]{:S(2)}) collective-permute-start(bf16[3,768,128]{2,1,0:T(8,128)(2,1)S(1)} %get-tuple-element.72), channel_id=1, source_target_pairs={{0,16},{8,24},{16,0},{24,8},{1,17},{9,25},{17,1},{25,9},{2,18},{10... | collective-permute-start | bytes 1769480 | tf_op jit(solution)/shard_map/ppermute | solution.py:521
  15.9 20.6 %collective-permute-start = (bf16[3,768,128]{2,1,0:T(8,128)(2,1)S(1)}, bf16[3,768,128]{2,1,0:T(8,128)(2,1)}, u32[]{:S(2)}, u32[]{:S(2)}) collective-permute-start(bf16[3,768,128]{2,1,0:T(8,128)(2,1)S(1)} %get-tuple-element.73), channel_id=1, source_target_pairs={{0,8},{8,0},{16,24},{24,16},{1,9},{9,1},{17,25},{25,17},{2,10},{10... | collective-permute-start | bytes 1769480 | tf_op jit(solution)/shard_map/ppermute | solution.py:521
  35.6 0.8 copy-start.9
  36.4 0.9 copy-start.1
  46.0 9.2 %copy-start.2 = (bf16[3,768,128]{2,1,0:T(8,128)(2,1)S(1)}, bf16[3,768,128]{2,1,0:T(8,128)(2,1)}, u32[]{:S(2)}) copy-start(bf16[3,768,128]{2,1,0:T(8,128)(2,1)} %get-tuple-element.37) | copy-start | bytes 1769476
  46.1 9.2 %copy-start.10 = (bf16[3,768,128]{2,1,0:T(8,128)(2,1)S(1)}, bf16[3,768,128]{2,1,0:T(8,128)(2,1)}, u32[]{:S(2)}) copy-start(bf16[3,768,128]{2,1,0:T(8,128)(2,1)} %copy-done.9) | copy-start | bytes 1769476
  46.1 30.9 %all-to-all-start.1 = ((bf16[32,96,128]{2,1,0:T(8,128)(2,1)}), bf16[32,96,128]{2,1,0:T(8,128)(2,1)S(1)}, u32[]{:S(2)}, u32[]{:S(2)}) async-start(bf16[32,96,128]{2,1,0:T(8,128)(2,1)} %get-tuple-element.36), calls=%async_computation.1 | async-start | bytes 1572864 | tf_op jit(solution)/shard_map/all_to_all | solution.py:518
  50.5 25.6 %collective-permute-start.2 = (bf16[3,768,128]{2,1,0:T(8,128)(2,1)}, bf16[3,768,128]{2,1,0:T(8,128)(2,1)S(1)}, u32[]{:S(2)}, u32[]{:S(2)}) collective-permute-start(bf16[3,768,128]{2,1,0:T(8,128)(2,1)} %get-tuple-element.71), channel_id=1, source_target_pairs={{0,24},{8,16},{16,8},{24,0},{1,25},{9,17},{17,9},{25,1},{2,26},{10... | collective-permute-start | bytes 1769480 | tf_op jit(solution)/shard_map/ppermute | solution.py:521
  77.0 0.9 copy-start
  103.0 11.5 %all-to-all-start.3 = ((bf16[32,24,128]{2,1,0:T(8,128)(2,1)}), bf16[32,24,128]{2,1,0:T(8,128)(2,1)S(1)}, u32[]{:S(2)}, u32[]{:S(2)}) async-start(bf16[32,24,128]{2,1,0:T(8,128)(2,1)} %bitcast.85), calls=%async_computation.3 | async-start | bytes 393216 | tf_op jit(solution)/shard_map/all_to_all | solution.py:518
  114.4 0.7 copy-start.5
  115.1 6.9 %copy-start.11 = (bf16[4,512,128]{2,1,0:T(8,128)(2,1)S(1)}, bf16[4,512,128]{2,1,0:T(8,128)(2,1)}, u32[]{:S(2)}) copy-start(bf16[4,512,128]{2,1,0:T(8,128)(2,1)} %get-tuple-element.45) | copy-start | bytes 1572868
  119.3 16.1 %all-to-all-start.4 = ((bf16[32,24,128]{2,1,0:T(8,128)(2,1)}), bf16[32,24,128]{2,1,0:T(8,128)(2,1)S(1)}, u32[]{:S(2)}, u32[]{:S(2)}) async-start(bf16[32,24,128]{2,1,0:T(8,128)(2,1)} %get-tuple-element.44), calls=%async_computation.4 | async-start | bytes 393216 | tf_op jit(solution)/shard_map/all_to_all | solution.py:518
  122.9 9.3 %collective-permute-start.5 = (bf16[5,128,128]{2,1,0:T(8,128)(2,1)S(1)}, bf16[5,128,128]{2,1,0:T(8,128)(2,1)S(1)}, u32[]{:S(2)}, u32[]{:S(2)}) collective-permute-start(bf16[5,128,128]{2,1,0:T(8,128)(2,1)S(1)} %get-tuple-element.75), channel_id=1, source_target_pairs={{0,24},{8,16},{16,8},{24,0},{1,25},{9,17},{17,9},{25,1},{2,26},{10... | collective-permute-start | bytes 491528 | tf_op jit(solution)/shard_map/ppermute | solution.py:521
  125.6 9.4 %collective-permute-start.3 = (bf16[5,128,128]{2,1,0:T(8,128)(2,1)S(1)}, bf16[5,128,128]{2,1,0:T(8,128)(2,1)S(1)}, u32[]{:S(2)}, u32[]{:S(2)}) collective-permute-start(bf16[5,128,128]{2,1,0:T(8,128)(2,1)S(1)} %get-tuple-element.77), channel_id=1, source_target_pairs={{0,8},{8,0},{16,24},{24,16},{1,9},{9,1},{17,25},{25,17},{2,10},{10... | collective-permute-start | bytes 491528 | tf_op jit(solution)/shard_map/ppermute | solution.py:521
  126.2 9.2 %collective-permute-start.4 = (bf16[5,128,128]{2,1,0:T(8,128)(2,1)S(1)}, bf16[5,128,128]{2,1,0:T(8,128)(2,1)S(1)}, u32[]{:S(2)}, u32[]{:S(2)}) collective-permute-start(bf16[5,128,128]{2,1,0:T(8,128)(2,1)S(1)} %get-tuple-element.78), channel_id=1, source_target_pairs={{0,16},{8,24},{16,0},{24,8},{1,17},{9,25},{17,1},{25,9},{2,18},{10... | collective-permute-start | bytes 491528 | tf_op jit(solution)/shard_map/ppermute | solution.py:521
  135.3 0.7 copy-start.8
  144.4 13.2 %all-to-all-start.5 = ((bf16[32,24,128]{2,1,0:T(8,128)(2,1)}), bf16[32,24,128]{2,1,0:T(8,128)(2,1)S(1)}, u32[]{:S(2)}, u32[]{:S(2)}) async-start(bf16[32,24,128]{2,1,0:T(8,128)(2,1)} %bitcast.86), calls=%async_computation.5 | async-start | bytes 393216 | tf_op jit(solution)/shard_map/all_to_all | solution.py:518
  157.5 0.7 copy-start.7
  182.7 11.4 %all-to-all-start.7 = ((bf16[32,24,128]{2,1,0:T(8,128)(2,1)}), bf16[32,24,128]{2,1,0:T(8,128)(2,1)S(1)}, u32[]{:S(2)}, u32[]{:S(2)}) async-start(bf16[32,24,128]{2,1,0:T(8,128)(2,1)} %bitcast.84), calls=%async_computation.7 | async-start | bytes 393216 | tf_op jit(solution)/shard_map/all_to_all | solution.py:518
  194.1 0.7 copy-start.6
  200.2 15.0 %all-to-all-start.8 = ((bf16[32,40,128]{2,1,0:T(8,128)(2,1)}), bf16[32,40,128]{2,1,0:T(8,128)(2,1)S(1)}, u32[]{:S(2)}, u32[]{:S(2)}) async-start(bf16[32,40,128]{2,1,0:T(8,128)(2,1)} %get-tuple-element.58), calls=%async_computation.8 | async-start | bytes 655360 | tf_op jit(solution)/shard_map/all_to_all | solution.py:518
  206.1 41.2 %collective-permute-start.8 = (bf16[3,768,128]{2,1,0:T(8,128)(2,1)}, bf16[3,768,128]{2,1,0:T(8,128)(2,1)}, u32[]{:S(2)}, u32[]{:S(2)}) collective-permute-start(bf16[3,768,128]{2,1,0:T(8,128)(2,1)} %get-tuple-element.67), channel_id=1, source_target_pairs={{0,24},{8,16},{16,8},{24,0},{1,25},{9,17},{17,9},{25,1},{2,26},{10... | collective-permute-start | bytes 1769480 | tf_op jit(solution)/shard_map/ppermute | solution.py:521
  208.7 50.7 %collective-permute-start.7 = (bf16[3,768,128]{2,1,0:T(8,128)(2,1)}, bf16[3,768,128]{2,1,0:T(8,128)(2,1)}, u32[]{:S(2)}, u32[]{:S(2)}) collective-permute-start(bf16[3,768,128]{2,1,0:T(8,128)(2,1)} %get-tuple-element.68), channel_id=1, source_target_pairs={{0,16},{8,24},{16,0},{24,8},{1,17},{9,25},{17,1},{25,9},{2,18},{10... | collective-permute-start | bytes 1769480 | tf_op jit(solution)/shard_map/ppermute | solution.py:521
  209.3 50.2 %collective-permute-start.6 = (bf16[3,768,128]{2,1,0:T(8,128)(2,1)}, bf16[3,768,128]{2,1,0:T(8,128)(2,1)}, u32[]{:S(2)}, u32[]{:S(2)}) collective-permute-start(bf16[3,768,128]{2,1,0:T(8,128)(2,1)} %get-tuple-element.69), channel_id=1, source_target_pairs={{0,8},{8,0},{16,24},{24,16},{1,9},{9,1},{17,25},{25,17},{2,10},{10... | collective-permute-start | bytes 1769480 | tf_op jit(solution)/shard_map/ppermute | solution.py:521
  215.2 0.7 copy-start.3
  224.4 20.3 %all-to-all-start.9 = ((bf16[8,112,128]{2,1,0:T(8,128)(2,1)}), bf16[8,112,128]{2,1,0:T(8,128)(2,1)S(1)}, u32[]{:S(2)}, u32[]{:S(2)}) async-start(bf16[8,112,128]{2,1,0:T(8,128)(2,1)} %get-tuple-element.59), calls=%async_computation.9 | async-start | bytes 458752 | tf_op jit(solution)/shard_map/all_to_all | solution.py:745
  228.9 10.3 %collective-permute-start.14 = (bf16[3,128,128]{2,1,0:T(8,128)(2,1)S(1)}, bf16[3,128,128]{2,1,0:T(8,128)(2,1)S(1)}, u32[]{:S(2)}, u32[]{:S(2)}) collective-permute-start(bf16[3,128,128]{2,1,0:T(8,128)(2,1)S(1)} %get-tuple-element.80), channel_id=1, source_target_pairs={{0,24},{8,16},{16,8},{24,0},{1,25},{9,17},{17,9},{25,1},{2,26},{10... | collective-permute-start | bytes 294920 | tf_op jit(solution)/shard_map/ppermute | solution.py:521
  229.4 12.1 %collective-permute-start.13 = (bf16[3,128,128]{2,1,0:T(8,128)(2,1)S(1)}, bf16[3,128,128]{2,1,0:T(8,128)(2,1)S(1)}, u32[]{:S(2)}, u32[]{:S(2)}) collective-permute-start(bf16[3,128,128]{2,1,0:T(8,128)(2,1)S(1)} %get-tuple-element.81), channel_id=1, source_target_pairs={{0,16},{8,24},{16,0},{24,8},{1,17},{9,25},{17,1},{25,9},{2,18},{10... | collective-permute-start | bytes 294920 | tf_op jit(solution)/shard_map/ppermute | solution.py:521
  239.2 4.6 %collective-permute-start.12 = (bf16[3,128,128]{2,1,0:T(8,128)(2,1)S(1)}, bf16[3,128,128]{2,1,0:T(8,128)(2,1)S(1)}, u32[]{:S(2)}, u32[]{:S(2)}) collective-permute-start(bf16[3,128,128]{2,1,0:T(8,128)(2,1)S(1)} %get-tuple-element.82), channel_id=1, source_target_pairs={{0,8},{8,0},{16,24},{24,16},{1,9},{9,1},{17,25},{25,17},{2,10},{10... | collective-permute-start | bytes 294920 | tf_op jit(solution)/shard_map/ppermute | solution.py:521
  244.7 14.2 %copy-start.4 = (bf16[8,112,128]{2,1,0:T(8,128)(2,1)}, bf16[8,112,128]{2,1,0:T(8,128)(2,1)S(1)}, u32[]{:S(2)}) copy-start(bf16[8,112,128]{2,1,0:T(8,128)(2,1)S(1)} %all-to-all-done.9.refs_4_) | copy-start | bytes 688132
  244.7 14.8 %collective-permute-start.11 = (bf16[8,112,128]{2,1,0:T(8,128)(2,1)S(1)}, bf16[8,112,128]{2,1,0:T(8,128)(2,1)S(1)}, u32[]{:S(2)}, u32[]{:S(2)}) collective-permute-start(bf16[8,112,128]{2,1,0:T(8,128)(2,1)S(1)} %all-to-all-done.9.refs_4_), channel_id=1, source_target_pairs={{24,0},{25,1},{26,2},{27,3},{28,4},{29,5},{30,6},{31,7}} | collective-permute-start | bytes 688136 | tf_op jit(solution)/shard_map/ppermute | solution.py:776
  245.9 13.5 %collective-permute-start.10 = (bf16[8,112,128]{2,1,0:T(8,128)(2,1)S(1)}, bf16[8,112,128]{2,1,0:T(8,128)(2,1)S(1)}, u32[]{:S(2)}, u32[]{:S(2)}) collective-permute-start(bf16[8,112,128]{2,1,0:T(8,128)(2,1)S(1)} %all-to-all-done.9.refs_4_), channel_id=1, source_target_pairs={{16,0},{17,1},{18,2},{19,3},{20,4},{21,5},{22,6},{23,7}} | collective-permute-start | bytes 688136 | tf_op jit(solution)/shard_map/ppermute | solution.py:776
  247.3 12.3 %collective-permute-start.9 = (bf16[8,112,128]{2,1,0:T(8,128)(2,1)S(1)}, bf16[8,112,128]{2,1,0:T(8,128)(2,1)}, u32[]{:S(2)}, u32[]{:S(2)}) collective-permute-start(bf16[8,112,128]{2,1,0:T(8,128)(2,1)S(1)} %all-to-all-done.9.refs_4_), channel_id=1, source_target_pairs={{8,0},{9,1},{10,2},{11,3},{12,4},{13,5},{14,6},{15,7}} | collective-permute-start | bytes 688136 | tf_op jit(solution)/shard_map/ppermute | solution.py:776
  259.5 0.7 copy-start.12
  259.5 0.8 copy-start.13

commit v5 on v4

--- a/solution.py
+++ b/solution.py
@@ -414,36 +414,58 @@
                     out_ref[r, w : w + tile, :] = total.astype(BF16)
 
 
-def weight_kernel(steps, sec_ref, first_ref, late_ref, out_ref):
-    channels = out_ref.shape[-1]
-    tall = late_ref.shape[2]
+def weight_kernel(steps, tall, sec_ref, first_ref, late_ref, out_any, out_v, sems):
+    channels = out_v.shape[-1]
+    modes = out_v.shape[3]
+    span_j = out_v.shape[2]
+    blocks = out_v.shape[1]
     groups = tall // 8
-    lefts = [first_ref[0, s] for s in range(steps)]
-    rights = [late_ref[0, s] for s in range(steps - 1)] + [first_ref[0, steps]]
+    span = steps * 8
+    block = 4 * span
+
+    def leave(n):
+        a, b = n // blocks, n % blocks
+        return pltpu.make_async_copy(
+            out_v.at[a, b],
+            out_any.at[pl.ds(b * span_j, span_j), pl.ds((sec_ref[0] ^ a) * modes, modes)],
+            sems.at[n],
+        )
 
     def tallied(values):
         wide = [v.astype(F32).reshape(groups, 8, channels) for v in values]
-        return jnp.concatenate(wide, axis=1).reshape(groups * steps * 8, channels)
-
-    span = steps * 8
-    left, right = tallied(lefts), tallied(rights)
-    ids = lax.broadcasted_iota(jnp.int32, right.shape, 0)
-    turned = jnp.where(
-        ids % 2 == 0,
-        pltpu.roll(right, groups * span - 1, 0),
-        -pltpu.roll(right, 1, 0),
-    )
-    right = jnp.concatenate([right, turned], axis=1).astype(BF16)
-    pair = (ids // 2) % 4
-    lefts = [jnp.where(pair == t, left, 0.0).astype(BF16) for t in range(4)]
-    per_j = out_ref.shape[1]
-    for g in range(groups):
-        rhs = right[g * span : (g + 1) * span]
-        for t in range(4):
-            product = dot(lefts[t][g * span : (g + 1) * span], rhs, ((0,), (0,))).astype(BF16)
-            j, k = divmod(g * 4 + t, per_j)
-            out_ref[j, k, 0] = product[:, :channels]
-            out_ref[j, k, 1] = product[:, channels:]
+        return jnp.concatenate(wide, axis=1).reshape(groups * span, channels)
+
+    @pl.loop(0, steps * blocks)
+    def _(n):
+        a, b = n // blocks, n % blocks
+        here = pl.ds(pl.multiple_of(b * tall, tall), tall)
+        left = tallied([first_ref[a, s, here] for s in range(steps)])
+        cots = [late_ref[a, s, here] for s in range(steps - 1)] + [first_ref[a, steps, here]]
+        right = tallied(cots)
+        ids = lax.broadcasted_iota(jnp.int32, right.shape, 0)
+        turned = jnp.where(
+            ids % 2 == 0,
+            pltpu.roll(right, groups * span - 1, 0),
+            -pltpu.roll(right, 1, 0),
+        )
+        right = jnp.concatenate([right, turned], axis=1).astype(BF16)
+        ids = lax.broadcasted_iota(jnp.int32, (channels, block), 1)
+        for first in range(0, groups, 4):
+            rhs = right[first * span : first * span + block]
+            turned_left = left[first * span : first * span + block].T
+            for g in range(4):
+                for t in range(4):
+                    mine = (ids // span == g) & ((ids // 2) % 4 == t)
+                    lhs = jnp.where(mine, turned_left, 0.0).astype(BF16)
+                    product = dot(lhs, rhs).astype(BF16)
+                    j, k = divmod((first + g) * 4 + t, modes)
+                    out_v[a, b, j, k, 0] = product[:, :channels]
+                    out_v[a, b, j, k, 1] = product[:, channels:]
+        leave(n).start()
+
+    @pl.loop(0, steps * blocks)
+    def _(n):
+        leave(n).wait()
 
 
 def whole(shape):
@@ -748,19 +770,16 @@
     own_j = max(1, min(own_freqs, 32 // modes))
     tall = own_j * parts
     first_modes, late_modes = jnp.stack(first_modes, 0), jnp.stack(late_modes, 0)
+    blocks = own_freqs // own_j
     (d_spectral,) = call(
-        functools.partial(weight_kernel, sections),
+        functools.partial(weight_kernel, sections, tall),
         [jax.ShapeDtypeStruct((own_freqs, row_modes, 2, channels, channels), BF16)],
-        [
-            pl.BlockSpec((1, m.shape[1], tall, channels), lambda a, b, i: (a, 0, b, 0))
-            for m in (first_modes, late_modes)
-        ],
+        [whole(first_modes.shape), whole(late_modes.shape)],
         (first_modes, late_modes),
-        grid=(sections, own_freqs // own_j),
-        out_specs=[
-            pl.BlockSpec(
-                (own_j, modes, 2, channels, channels), lambda a, b, i: (b, i[0] ^ a, 0, 0, 0)
-            )
+        out_specs=[anywhere],
+        scratch=[
+            pltpu.VMEM((sections, blocks, own_j, modes, 2, channels, channels), BF16),
+            pltpu.SemaphoreType.DMA((sections * blocks,)),
         ],
         prefetch=sec,
         flops=8 * weight_bytes,

time: 267 us -> 265 us (level)
  transfers between devices with their start and end apart: 23 -> 23, of which waited for: 11 -> 12; matrix products, arithmetic and copies ran while one was open for 7% -> 7% of each run, Pallas kernels for 11% -> 10%
where the time goes in v5:
time: 265 us; the launch traced here: 264 us
  Pallas kernels  87.2 us (33%)
  waiting for transfers between devices  76.7 us (29%)
  starting transfers between devices  50 us (19%)
  blocking collectives  24.6 us (9%)
  local copies, waits for them, and re-layouts  17.5 us (7%)
  other arithmetic  7.05 us (3%)
    pallas_call x15, Pallas kernels, call(): pl.pallas_call(kernel, out_shape=outs, grid_spec=pltpu.PrefetchScalarGrid...  87.2 us
    ppermute x12, waiting for transfers between devices, share(): return lax.ppermute(piece, 'section', [(i, i ^ d) for i in range(sections)])  56.7 us
    all_to_all x7, starting transfers between devices, exchange(): return lax.all_to_all(values, ALL, 0, 0, tiled=True)  27.1 us
    all_to_all x2, blocking collectives, exchange(): return lax.all_to_all(values, ALL, 0, 0, tiled=True)  24.6 us
    all_to_all x7, waiting for transfers between devices, exchange(): return lax.all_to_all(values, ALL, 0, 0, tiled=True)  19.6 us
    ppermute x12, starting transfers between devices, share(): return lax.ppermute(piece, 'section', [(i, i ^ d) for i in range(sections)])  15.6 us
    unnamed x28, local copies, waits for them, and re-layouts  6.76 us
  transfers between devices with their start and end apart: 23, of which 12 were waited for; matrix products, arithmetic and copies ran while one was open for 7% of the time, Pallas kernels for 10%

profile of v5, /device:TPU:0, one launch (start us, length us, event | category | flops | bytes accessed | tf_op | source)
XLA Modules:
  0.0 263.9 jit_solution(5414306869094031947)
XLA Ops:
  0.6 3.4 %shard_map.148 = bf16[32,96,128]{2,1,0:T(8,128)(2,1)} custom-call(bf16[12,768,128]{2,1,0:T(8,128)(2,1)} %bitcast.73, bf16[256,768]{1,0:T(8,128)(2,1)} %constant.75.clone.basis_ref), custom_call_target="tpu_custom_call" | custom-call | flops 603979776 | bytes 4718592 | tf_op jit(solution)/shard_map/pallas_call | solution.py:481
  4.0 7.3 %all-to-all-start = ((bf16[32,96,128]{2,1,0:T(8,128)(2,1)}), bf16[32,96,128]{2,1,0:T(8,128)(2,1)S(1)}, u32[]{:S(2)}, u32[]{:S(2)}) async-start(bf16[32,96,128]{2,1,0:T(8,128)(2,1)} %shard_map.148), calls=%async_computation | async-start | bytes 1572864 | tf_op jit(solution)/shard_map/all_to_all | solution.py:540
  11.3 2.8 %dynamic-slice_bitcast_fusion.4 = (bf16[3,768,128]{2,1,0:T(8,128)(2,1)}, bf16[3,768,128]{2,1,0:T(8,128)(2,1)S(1)}, bf16[3,768,128]{2,1,0:T(8,128)(2,1)S(1)}, bf16[3,768,128]{2,1,0:T(8,128)(2,1)}) fusion(bf16[4,3,768,128]{3,2,1,0:T(8,128)(2,1)} %bitcast.74, s32[]{:T(128)S(6)} %select_n.34, s32[]{:T(128)S(6)} %select_n.32, s32[]{:T(128)S(6)} %select_n.31, ...), kind=kLoop, calls=%fused_computation.15 | loop fusion | bytes 4718608 | tf_op jit(solution)/shard_map/jit(dynamic_index_in_dim)/squeeze | solution.py:548
  14.1 1.8 collective-permute-start.1
  15.9 1.5 collective-permute-start
  17.4 18.3 %collective-permute-done.1 = bf16[3,768,128]{2,1,0:T(8,128)(2,1)S(1)} collective-permute-done((bf16[3,768,128]{2,1,0:T(8,128)(2,1)S(1)}, bf16[3,768,128]{2,1,0:T(8,128)(2,1)S(1)}, u32[]{:S(2)}, u32[]{:S(2)}) %collective-permute-start.1) | collective-permute-done | bytes 589856 | tf_op jit(solution)/shard_map/ppermute | solution.py:543
  35.6 0.8 copy-done.9
  36.5 0.9 copy-done.1
  37.3 8.7 %shard_map.149 = (bf16[4,512,128]{2,1,0:T(8,128)(2,1)}, bf16[32,96,128]{2,1,0:T(8,128)(2,1)}) custom-call(s32[1]{0:T(128)} %bitcast.sec_ref, bf16[3072,128]{1,0:T(8,128)(2,1)} %bitcast.75, bf16[512,768]{1,0:T(8,128)(2,1)} %constant.78.clone.lat_any, bf16[768,512]{1,0:T(8,128)(2,1)} %constant.80.clone.inv_any, bf16[64,16,2,128,128]{4,3,2,1,0:T(8,128)(2,1)} %all_ref.9), custom_call_target="tpu_custom_call" | custom-call | flops 67108864 | bytes 16777216 | tf_op jit(solution)/shard_map/pallas_call | solution.py:481
  46.1 4.4 %all-to-all-start.1 = ((bf16[32,96,128]{2,1,0:T(8,128)(2,1)}), bf16[32,96,128]{2,1,0:T(8,128)(2,1)S(1)}, u32[]{:S(2)}, u32[]{:S(2)}) async-start(bf16[32,96,128]{2,1,0:T(8,128)(2,1)} %get-tuple-element.36), calls=%async_computation.1 | async-start | bytes 1572864 | tf_op jit(solution)/shard_map/all_to_all | solution.py:540
  50.5 2.7 %collective-permute-start.2 = (bf16[3,768,128]{2,1,0:T(8,128)(2,1)}, bf16[3,768,128]{2,1,0:T(8,128)(2,1)S(1)}, u32[]{:S(2)}, u32[]{:S(2)}) collective-permute-start(bf16[3,768,128]{2,1,0:T(8,128)(2,1)} %get-tuple-element.71), channel_id=1, source_target_pairs={{0,24},{8,16},{16,8},{24,0},{1,25},{9,17},{17,9},{25,1},{2,26},{10... | collective-permute-start | bytes 1769480 | tf_op jit(solution)/shard_map/ppermute | solution.py:543
  53.3 1.9 constant_dynamic-slice_fusion.cot_ref
  55.2 2.7 %maximum_maximum_fusion = bf16[4,3,768,128]{3,2,1,0:T(8,128)(2,1)} fusion(bf16[1,3,768,128]{3,2,1,0:T(8,128)(2,1)S(1)} %bitcast.82, bf16[1,3,768,128]{3,2,1,0:T(8,128)(2,1)} %bitcast.8, bf16[1,3,768,128]{3,2,1,0:T(8,128)(2,1)S(1)} %bitcast.77, bf16[4]{0:T(256)(128)(2,1)S(1)} %pad.16.clone), kind=kLoop, calls=%fused_computation | loop fusion | flops 3538944 | bytes 4128776 | tf_op jit(solution)/shard_map/stack | solution.py:566
  58.0 18.1 %collective-permute-done.2 = bf16[3,768,128]{2,1,0:T(8,128)(2,1)S(1)} collective-permute-done((bf16[3,768,128]{2,1,0:T(8,128)(2,1)}, bf16[3,768,128]{2,1,0:T(8,128)(2,1)S(1)}, u32[]{:S(2)}, u32[]{:S(2)}) %collective-permute-start.2) | collective-permute-done | bytes 589856 | tf_op jit(solution)/shard_map/ppermute | solution.py:543
  76.1 0.9 bitcast_dynamic-update-slice_fusion.state_ref
  77.0 0.9 copy-done
  77.9 4.1 %shard_map.150 = (bf16[3,768,128]{2,1,0:T(8,128)(2,1)}, bf16[32,24,128]{2,1,0:T(8,128)(2,1)}, f32[128,128]{1,0:T(8,128)}) custom-call(s32[1]{0:T(128)} %bitcast.sec_ref, bf16[32,96,128]{2,1,0:T(8,128)(2,1)} %copy-done, bf16[3,768,128]{2,1,0:T(8,128)(2,1)} %constant_dynamic-slice_fusion.cot_ref, ...), custom_call_target="tpu_custom_call" | custom-call | flops 150994944 | bytes 2949120 | tf_op jit(solution)/shard_map/pallas_call | solution.py:481
  82.0 12.6 %all_to_all.50 = bf16[32,24,128]{2,1,0:T(8,128)(2,1)} all-to-all(bf16[32,24,128]{2,1,0:T(8,128)(2,1)} %get-tuple-element.40), channel_id=1, replica_groups=mesh['section'=4,'row'=8] {'section','row'}, dimensions={0} | all-to-all | bytes 393216 | tf_op jit(solution)/shard_map/all_to_all | solution.py:540
  94.6 8.3 %shard_map.151 = (bf16[512,128]{1,0:T(8,128)(2,1)}, bf16[768,128]{1,0:T(8,128)(2,1)}) custom-call(s32[1]{0:T(128)} %bitcast.sec_ref, bf16[768,128]{1,0:T(8,128)(2,1)} %bitcast.80, bf16[512,768]{1,0:T(8,128)(2,1)} %constant.79.clone.lat_any, bf16[768,512]{1,0:T(8,128)(2,1)} %constant.80.clone.inv_any, bf16[64,16,2,128,128]{4,3,2,1,0:T(8,128)(2,1)} %all_ref.9), custom_call_target="tpu_custom_call" | custom-call | flops 33554432 | bytes 16777216 | tf_op jit(solution)/shard_map/pallas_call | solution.py:481
  103.0 2.7 %all-to-all-start.3 = ((bf16[32,24,128]{2,1,0:T(8,128)(2,1)}), bf16[32,24,128]{2,1,0:T(8,128)(2,1)S(1)}, u32[]{:S(2)}, u32[]{:S(2)}) async-start(bf16[32,24,128]{2,1,0:T(8,128)(2,1)} %bitcast.85), calls=%async_computation.3 | async-start | bytes 393216 | tf_op jit(solution)/shard_map/all_to_all | solution.py:540
  105.7 1.9 fusion.8.carried_ref
  107.6 3.4 %shard_map.152.slope_ref = f32[3,768,128]{2,1,0:T(8,128)} custom-call(s32[1]{0:T(128)} %bitcast.sec_ref, bf16[32,96,128]{2,1,0:T(8,128)(2,1)} %copy-done, bf16[4,3,768,128]{3,2,1,0:T(8,128)(2,1)} %bitcast_dynamic-update-slice_fusion.state_ref, bf16[768,256]{1,0:T(8,128)(2,1)} %constant.77.clone.synth_t_ref.synth_ref, bf16[128,128]{1,0:T(8,128)(2,1)} %mix_ref.13, ...), custom_call_target="tpu_custom_call" | custom-call | flops 150994944 | bytes 2949120 | tf_op jit(solution)/shard_map/pallas_call | solution.py:481
  111.0 3.4 %all-to-all-done.3.recv_ref = bf16[32,24,128]{2,1,0:T(8,128)(2,1)S(1)} async-done(((bf16[32,24,128]{2,1,0:T(8,128)(2,1)}), bf16[32,24,128]{2,1,0:T(8,128)(2,1)S(1)}, u32[]{:S(2)}, u32[]{:S(2)}) %all-to-all-start.3) | async-done | bytes 196640 | tf_op jit(solution)/shard_map/all_to_all | solution.py:540
  114.4 0.7 copy-done.5
  115.1 4.1 %shard_map.153 = (bf16[4,3,768,128]{3,2,1,0:T(8,128)(2,1)}, bf16[3,768,128]{2,1,0:T(8,128)(2,1)}, bf16[32,24,128]{2,1,0:T(8,128)(2,1)}, f32[128,128]{1,0:T(8,128)}) custom-call(s32[1]{0:T(128)} %bitcast.sec_ref, bf16[32,24,128]{2,1,0:T(8,128)(2,1)} %copy-done.5, bf16[1,3,768,128]{3,2,1,0:T(8,128)(2,1)} %fusion.8.carried_ref, ...), custom_call_target="tpu_custom_call" | custom-call | flops 301989888 | bytes 4718592 | tf_op jit(solution)/shard_map/pallas_call | solution.py:481
  119.3 2.7 %all-to-all-start.4 = ((bf16[32,24,128]{2,1,0:T(8,128)(2,1)}), bf16[32,24,128]{2,1,0:T(8,128)(2,1)S(1)}, u32[]{:S(2)}, u32[]{:S(2)}) async-start(bf16[32,24,128]{2,1,0:T(8,128)(2,1)} %get-tuple-element.44), calls=%async_computation.4 | async-start | bytes 393216 | tf_op jit(solution)/shard_map/all_to_all | solution.py:540
  122.0 0.9 fusion.1
  122.9 2.7 %collective-permute-start.5 = (bf16[5,128,128]{2,1,0:T(8,128)(2,1)S(1)}, bf16[5,128,128]{2,1,0:T(8,128)(2,1)S(1)}, u32[]{:S(2)}, u32[]{:S(2)}) collective-permute-start(bf16[5,128,128]{2,1,0:T(8,128)(2,1)S(1)} %get-tuple-element.75), channel_id=1, source_target_pairs={{0,24},{8,16},{16,8},{24,0},{1,25},{9,17},{17,9},{25,1},{2,26},{10... | collective-permute-start | bytes 491528 | tf_op jit(solution)/shard_map/ppermute | solution.py:543
  126.4 5.7 %collective-permute-done.5 = bf16[5,128,128]{2,1,0:T(8,128)(2,1)S(1)} collective-permute-done((bf16[5,128,128]{2,1,0:T(8,128)(2,1)S(1)}, bf16[5,128,128]{2,1,0:T(8,128)(2,1)S(1)}, u32[]{:S(2)}, u32[]{:S(2)}) %collective-permute-start.5) | collective-permute-done | bytes 163872 | tf_op jit(solution)/shard_map/ppermute | solution.py:543
  132.1 2.9 %collective-permute-done.3 = bf16[5,128,128]{2,1,0:T(8,128)(2,1)S(1)} collective-permute-done((bf16[5,128,128]{2,1,0:T(8,128)(2,1)S(1)}, bf16[5,128,128]{2,1,0:T(8,128)(2,1)S(1)}, u32[]{:S(2)}, u32[]{:S(2)}) %collective-permute-start.3) | collective-permute-done | bytes 163872 | tf_op jit(solution)/shard_map/ppermute | solution.py:543
  135.3 0.7 copy-done.8
  136.0 8.3 %shard_map.154 = (bf16[512,128]{1,0:T(8,128)(2,1)}, bf16[768,128]{1,0:T(8,128)(2,1)}) custom-call(s32[1]{0:T(128)} %bitcast.sec_ref, bf16[768,128]{1,0:T(8,128)(2,1)} %bitcast.78, bf16[512,768]{1,0:T(8,128)(2,1)} %constant.79.clone.lat_any, bf16[768,512]{1,0:T(8,128)(2,1)} %constant.80.clone.inv_any, bf16[64,16,2,128,128]{4,3,2,1,0:T(8,128)(2,1)} %all_ref.9), custom_call_target="tpu_custom_call" | custom-call | flops 33554432 | bytes 16777216 | tf_op jit(solution)/shard_map/pallas_call | solution.py:481
  144.4 4.6 %all-to-all-start.5 = ((bf16[32,24,128]{2,1,0:T(8,128)(2,1)}), bf16[32,24,128]{2,1,0:T(8,128)(2,1)S(1)}, u32[]{:S(2)}, u32[]{:S(2)}) async-start(bf16[32,24,128]{2,1,0:T(8,128)(2,1)} %bitcast.86), calls=%async_computation.5 | async-start | bytes 393216 | tf_op jit(solution)/shard_map/all_to_all | solution.py:540
  149.0 3.4 %shard_map.155.slope_ref = f32[3,768,128]{2,1,0:T(8,128)} custom-call(s32[1]{0:T(128)} %bitcast.sec_ref, bf16[32,96,128]{2,1,0:T(8,128)(2,1)} %copy-done, bf16[4,3,768,128]{3,2,1,0:T(8,128)(2,1)} %bitcast_dynamic-update-slice_fusion.state_ref, bf16[768,256]{1,0:T(8,128)(2,1)} %constant.77.clone.synth_t_ref.synth_ref, bf16[128,128]{1,0:T(8,128)(2,1)} %mix_ref.13, ...), custom_call_target="tpu_custom_call" | custom-call | flops 150994944 | bytes 2949120 | tf_op jit(solution)/shard_map/pallas_call | solution.py:481
  152.4 5.1 %all-to-all-done.5.recv_ref = bf16[32,24,128]{2,1,0:T(8,128)(2,1)S(1)} async-done(((bf16[32,24,128]{2,1,0:T(8,128)(2,1)}), bf16[32,24,128]{2,1,0:T(8,128)(2,1)S(1)}, u32[]{:S(2)}, u32[]{:S(2)}) %all-to-all-start.5) | async-done | bytes 196640 | tf_op jit(solution)/shard_map/all_to_all | solution.py:540
  157.5 0.7 copy-done.7
  158.2 4.1 %shard_map.156 = (bf16[4,3,768,128]{3,2,1,0:T(8,128)(2,1)}, bf16[3,768,128]{2,1,0:T(8,128)(2,1)}, bf16[32,24,128]{2,1,0:T(8,128)(2,1)}, f32[128,128]{1,0:T(8,128)}) custom-call(s32[1]{0:T(128)} %bitcast.sec_ref, bf16[32,24,128]{2,1,0:T(8,128)(2,1)} %copy-done.7, ...), custom_call_target="tpu_custom_call", output_to_operand_aliasing={{0}: (2, {})} | custom-call | flops 301989888 | bytes 4718592 | tf_op jit(solution)/shard_map/pallas_call | solution.py:481
  162.3 12.0 %all_to_all.51 = bf16[32,24,128]{2,1,0:T(8,128)(2,1)} all-to-all(bf16[32,24,128]{2,1,0:T(8,128)(2,1)} %get-tuple-element.52), channel_id=1, replica_groups=mesh['section'=4,'row'=8] {'section','row'}, dimensions={0} | all-to-all | bytes 393216 | tf_op jit(solution)/shard_map/all_to_all | solution.py:540
  174.3 8.4 %shard_map.157 = (bf16[512,128]{1,0:T(8,128)(2,1)}, bf16[768,128]{1,0:T(8,128)(2,1)}) custom-call(s32[1]{0:T(128)} %bitcast.sec_ref, bf16[768,128]{1,0:T(8,128)(2,1)} %bitcast.79, bf16[512,768]{1,0:T(8,128)(2,1)} %constant.79.clone.lat_any, bf16[768,512]{1,0:T(8,128)(2,1)} %constant.80.clone.inv_any, bf16[64,16,2,128,128]{4,3,2,1,0:T(8,128)(2,1)} %all_ref.9), custom_call_target="tpu_custom_call" | custom-call | flops 33554432 | bytes 16777216 | tf_op jit(solution)/shard_map/pallas_call | solution.py:481
  182.7 2.6 all-to-all-start.7
  185.3 3.4 %shard_map.158.slope_ref = f32[3,768,128]{2,1,0:T(8,128)} custom-call(s32[1]{0:T(128)} %bitcast.sec_ref, bf16[32,96,128]{2,1,0:T(8,128)(2,1)} %copy-done, bf16[4,3,768,128]{3,2,1,0:T(8,128)(2,1)} %bitcast_dynamic-update-slice_fusion.state_ref, bf16[768,256]{1,0:T(8,128)(2,1)} %constant.77.clone.synth_t_ref.synth_ref, bf16[128,128]{1,0:T(8,128)(2,1)} %mix_ref.13, ...), custom_call_target="tpu_custom_call" | custom-call | flops 150994944 | bytes 2949120 | tf_op jit(solution)/shard_map/pallas_call | solution.py:481
  188.7 5.3 %all-to-all-done.7.recv_ref = bf16[32,24,128]{2,1,0:T(8,128)(2,1)S(1)} async-done(((bf16[32,24,128]{2,1,0:T(8,128)(2,1)}), bf16[32,24,128]{2,1,0:T(8,128)(2,1)S(1)}, u32[]{:S(2)}, u32[]{:S(2)}) %all-to-all-start.7) | async-done | bytes 196640 | tf_op jit(solution)/shard_map/all_to_all | solution.py:540
  194.1 0.7 copy-done.6
  194.7 5.5 %shard_map.159 = (bf16[4,3,768,128]{3,2,1,0:T(8,128)(2,1)}, bf16[3,768,128]{2,1,0:T(8,128)(2,1)}, bf16[32,40,128]{2,1,0:T(8,128)(2,1)}, f32[128,128]{1,0:T(8,128)}) custom-call(s32[1]{0:T(128)} %bitcast.sec_ref, bf16[32,24,128]{2,1,0:T(8,128)(2,1)} %copy-done.6, ...), custom_call_target="tpu_custom_call", output_to_operand_aliasing={{0}: (2, {})} | custom-call | flops 301989888 | bytes 4718592 | tf_op jit(solution)/shard_map/pallas_call | solution.py:481
  200.2 2.7 %all-to-all-start.8 = ((bf16[32,40,128]{2,1,0:T(8,128)(2,1)}), bf16[32,40,128]{2,1,0:T(8,128)(2,1)S(1)}, u32[]{:S(2)}, u32[]{:S(2)}) async-start(bf16[32,40,128]{2,1,0:T(8,128)(2,1)} %get-tuple-element.58), calls=%async_computation.8 | async-start | bytes 655360 | tf_op jit(solution)/shard_map/all_to_all | solution.py:540
  203.0 3.1 %dynamic-slice_bitcast_fusion = (bf16[3,768,128]{2,1,0:T(8,128)(2,1)}, bf16[3,768,128]{2,1,0:T(8,128)(2,1)}, bf16[3,768,128]{2,1,0:T(8,128)(2,1)}, bf16[3,768,128]{2,1,0:T(8,128)(2,1)}) fusion(bf16[4,3,768,128]{3,2,1,0:T(8,128)(2,1)} %get-tuple-element.57, s32[]{:T(128)S(6)} %select_n.34, s32[]{:T(128)S(6)} %select_n.32, s32[]{:T(128)S(6)} %select_n.31, ...), kind=kLoop, calls=%fused_computation.11 | loop fusion | bytes 4718608 | tf_op jit(solution)/shard_map/jit(dynamic_index_in_dim)/squeeze | solution.py:737
  206.1 2.7 %collective-permute-start.8 = (bf16[3,768,128]{2,1,0:T(8,128)(2,1)}, bf16[3,768,128]{2,1,0:T(8,128)(2,1)}, u32[]{:S(2)}, u32[]{:S(2)}) collective-permute-start(bf16[3,768,128]{2,1,0:T(8,128)(2,1)} %get-tuple-element.67), channel_id=1, source_target_pairs={{0,24},{8,16},{16,8},{24,0},{1,25},{9,17},{17,9},{25,1},{2,26},{10... | collective-permute-start | bytes 1769480 | tf_op jit(solution)/shard_map/ppermute | solution.py:543
  209.5 5.7 %all-to-all-done.8.x_any = bf16[32,40,128]{2,1,0:T(8,128)(2,1)S(1)} async-done(((bf16[32,40,128]{2,1,0:T(8,128)(2,1)}), bf16[32,40,128]{2,1,0:T(8,128)(2,1)S(1)}, u32[]{:S(2)}, u32[]{:S(2)}) %all-to-all-start.8) | async-done | bytes 327712 | tf_op jit(solution)/shard_map/all_to_all | solution.py:540
  215.2 0.7 copy-done.3
  216.0 8.4 %shard_map.160 = (bf16[512,128]{1,0:T(8,128)(2,1)}, bf16[8,112,128]{2,1,0:T(8,128)(2,1)}) custom-call(s32[1]{0:T(128)} %bitcast.sec_ref, bf16[32,40,128]{2,1,0:T(8,128)(2,1)} %copy-done.3, bf16[512,768]{1,0:T(8,128)(2,1)} %constant.79.clone.lat_any, bf16[768,512]{1,0:T(8,128)(2,1)} %constant.81.clone.inv_any, bf16[64,16,2,128,128]{4,3,2,1,0:T(8,128)(2,1)} %all_ref.9), custom_call_target="tpu_custom_call" | custom-call | flops 33554432 | bytes 16777216 | tf_op jit(solution)/shard_map/pallas_call | solution.py:481
  224.4 3.4 %all-to-all-start.9 = ((bf16[8,112,128]{2,1,0:T(8,128)(2,1)}), bf16[8,112,128]{2,1,0:T(8,128)(2,1)S(1)}, u32[]{:S(2)}, u32[]{:S(2)}) async-start(bf16[8,112,128]{2,1,0:T(8,128)(2,1)} %get-tuple-element.59), calls=%async_computation.9 | async-start | bytes 458752 | tf_op jit(solution)/shard_map/all_to_all | solution.py:767
  227.8 1.1 pad_maximum_fusion.1
  229.4 0.7 collective-permute-start.13
  230.1 9.1 %collective-permute-done.14 = bf16[3,128,128]{2,1,0:T(8,128)(2,1)S(1)} collective-permute-done((bf16[3,128,128]{2,1,0:T(8,128)(2,1)S(1)}, bf16[3,128,128]{2,1,0:T(8,128)(2,1)S(1)}, u32[]{:S(2)}, u32[]{:S(2)}) %collective-permute-start.14) | collective-permute-done | bytes 98336 | tf_op jit(solution)/shard_map/ppermute | solution.py:543
  239.2 1.4 collective-permute-start.12
  240.6 0.9 pad_maximum_fusion.first_ref
  241.6 2.3 collective-permute-done.12
  243.8 0.8 pad_maximum_fusion.2.late_ref
  244.7 1.3 collective-permute-start.11
  245.9 1.3 collective-permute-start.10
  247.3 1.3 collective-permute-start.9
  248.6 8.7 %shard_map.162 = bf16[16,16,2,128,128]{4,3,2,1,0:T(8,128)(2,1)} custom-call(s32[1]{0:T(128)} %bitcast.sec_ref, bf16[4,5,128,128]{3,2,1,0:T(8,128)(2,1)} %pad_maximum_fusion.first_ref, bf16[4,3,128,128]{3,2,1,0:T(8,128)(2,1)} %pad_maximum_fusion.2.late_ref), custom_call_target="tpu_custom_call" | custom-call | flops 134217728 | bytes 16777216 | tf_op jit(solution)/shard_map/pallas_call | solution.py:481
  257.2 0.6 convert_multiply_fusion
  259.1 4.8 %shard_map.161 = bf16[12,768,128]{2,1,0:T(8,128)(2,1)} custom-call(s32[1]{0:T(128)} %bitcast.sec_ref, bf16[3,768,128]{2,1,0:T(8,128)(2,1)} %get-tuple-element.70.refs_0_, bf16[3,768,128]{2,1,0:T(8,128)(2,1)} %collective-permute-done.6.refs_1_, bf16[3,768,128]{2,1,0:T(8,128)(2,1)} %collective-permute-done.7.refs_2_, ...), custom_call_target="tpu_custom_call" | custom-call | flops 603979776 | bytes 9437184 | tf_op jit(solution)/shard_map/pallas_call | solution.py:481
  (40 shorter events, 3.8 us)
Async XLA Ops:
  4.0 32.4 %all-to-all-start = ((bf16[32,96,128]{2,1,0:T(8,128)(2,1)}), bf16[32,96,128]{2,1,0:T(8,128)(2,1)S(1)}, u32[]{:S(2)}, u32[]{:S(2)}) async-start(bf16[32,96,128]{2,1,0:T(8,128)(2,1)} %shard_map.148), calls=%async_computation | async-start | bytes 1572864 | tf_op jit(solution)/shard_map/all_to_all | solution.py:540
  14.1 21.5 %collective-permute-start.1 = (bf16[3,768,128]{2,1,0:T(8,128)(2,1)S(1)}, bf16[3,768,128]{2,1,0:T(8,128)(2,1)S(1)}, u32[]{:S(2)}, u32[]{:S(2)}) collective-permute-start(bf16[3,768,128]{2,1,0:T(8,128)(2,1)S(1)} %get-tuple-element.72), channel_id=1, source_target_pairs={{0,16},{8,24},{16,0},{24,8},{1,17},{9,25},{17,1},{25,9},{2,18},{10... | collective-permute-start | bytes 1769480 | tf_op jit(solution)/shard_map/ppermute | solution.py:543
  15.9 20.6 %collective-permute-start = (bf16[3,768,128]{2,1,0:T(8,128)(2,1)S(1)}, bf16[3,768,128]{2,1,0:T(8,128)(2,1)}, u32[]{:S(2)}, u32[]{:S(2)}) collective-permute-start(bf16[3,768,128]{2,1,0:T(8,128)(2,1)S(1)} %get-tuple-element.73), channel_id=1, source_target_pairs={{0,8},{8,0},{16,24},{24,16},{1,9},{9,1},{17,25},{25,17},{2,10},{10... | collective-permute-start | bytes 1769480 | tf_op jit(solution)/shard_map/ppermute | solution.py:543
  35.6 0.8 copy-start.9
  36.4 0.9 copy-start.1
  46.0 9.2 %copy-start.2 = (bf16[3,768,128]{2,1,0:T(8,128)(2,1)S(1)}, bf16[3,768,128]{2,1,0:T(8,128)(2,1)}, u32[]{:S(2)}) copy-start(bf16[3,768,128]{2,1,0:T(8,128)(2,1)} %get-tuple-element.37) | copy-start | bytes 1769476
  46.1 9.2 %copy-start.10 = (bf16[3,768,128]{2,1,0:T(8,128)(2,1)S(1)}, bf16[3,768,128]{2,1,0:T(8,128)(2,1)}, u32[]{:S(2)}) copy-start(bf16[3,768,128]{2,1,0:T(8,128)(2,1)} %copy-done.9) | copy-start | bytes 1769476
  46.1 30.9 %all-to-all-start.1 = ((bf16[32,96,128]{2,1,0:T(8,128)(2,1)}), bf16[32,96,128]{2,1,0:T(8,128)(2,1)S(1)}, u32[]{:S(2)}, u32[]{:S(2)}) async-start(bf16[32,96,128]{2,1,0:T(8,128)(2,1)} %get-tuple-element.36), calls=%async_computation.1 | async-start | bytes 1572864 | tf_op jit(solution)/shard_map/all_to_all | solution.py:540
  50.5 25.6 %collective-permute-start.2 = (bf16[3,768,128]{2,1,0:T(8,128)(2,1)}, bf16[3,768,128]{2,1,0:T(8,128)(2,1)S(1)}, u32[]{:S(2)}, u32[]{:S(2)}) collective-permute-start(bf16[3,768,128]{2,1,0:T(8,128)(2,1)} %get-tuple-element.71), channel_id=1, source_target_pairs={{0,24},{8,16},{16,8},{24,0},{1,25},{9,17},{17,9},{25,1},{2,26},{10... | collective-permute-start | bytes 1769480 | tf_op jit(solution)/shard_map/ppermute | solution.py:543
  77.0 0.9 copy-start
  103.0 11.5 %all-to-all-start.3 = ((bf16[32,24,128]{2,1,0:T(8,128)(2,1)}), bf16[32,24,128]{2,1,0:T(8,128)(2,1)S(1)}, u32[]{:S(2)}, u32[]{:S(2)}) async-start(bf16[32,24,128]{2,1,0:T(8,128)(2,1)} %bitcast.85), calls=%async_computation.3 | async-start | bytes 393216 | tf_op jit(solution)/shard_map/all_to_all | solution.py:540
  114.4 0.7 copy-start.5
  115.1 6.9 %copy-start.11 = (bf16[4,512,128]{2,1,0:T(8,128)(2,1)S(1)}, bf16[4,512,128]{2,1,0:T(8,128)(2,1)}, u32[]{:S(2)}) copy-start(bf16[4,512,128]{2,1,0:T(8,128)(2,1)} %get-tuple-element.45) | copy-start | bytes 1572868
  119.3 16.1 %all-to-all-start.4 = ((bf16[32,24,128]{2,1,0:T(8,128)(2,1)}), bf16[32,24,128]{2,1,0:T(8,128)(2,1)S(1)}, u32[]{:S(2)}, u32[]{:S(2)}) async-start(bf16[32,24,128]{2,1,0:T(8,128)(2,1)} %get-tuple-element.44), calls=%async_computation.4 | async-start | bytes 393216 | tf_op jit(solution)/shard_map/all_to_all | solution.py:540
  122.9 9.3 %collective-permute-start.5 = (bf16[5,128,128]{2,1,0:T(8,128)(2,1)S(1)}, bf16[5,128,128]{2,1,0:T(8,128)(2,1)S(1)}, u32[]{:S(2)}, u32[]{:S(2)}) collective-permute-start(bf16[5,128,128]{2,1,0:T(8,128)(2,1)S(1)} %get-tuple-element.75), channel_id=1, source_target_pairs={{0,24},{8,16},{16,8},{24,0},{1,25},{9,17},{17,9},{25,1},{2,26},{10... | collective-permute-start | bytes 491528 | tf_op jit(solution)/shard_map/ppermute | solution.py:543
  125.6 9.4 %collective-permute-start.3 = (bf16[5,128,128]{2,1,0:T(8,128)(2,1)S(1)}, bf16[5,128,128]{2,1,0:T(8,128)(2,1)S(1)}, u32[]{:S(2)}, u32[]{:S(2)}) collective-permute-start(bf16[5,128,128]{2,1,0:T(8,128)(2,1)S(1)} %get-tuple-element.77), channel_id=1, source_target_pairs={{0,8},{8,0},{16,24},{24,16},{1,9},{9,1},{17,25},{25,17},{2,10},{10... | collective-permute-start | bytes 491528 | tf_op jit(solution)/shard_map/ppermute | solution.py:543
  126.2 9.2 %collective-permute-start.4 = (bf16[5,128,128]{2,1,0:T(8,128)(2,1)S(1)}, bf16[5,128,128]{2,1,0:T(8,128)(2,1)S(1)}, u32[]{:S(2)}, u32[]{:S(2)}) collective-permute-start(bf16[5,128,128]{2,1,0:T(8,128)(2,1)S(1)} %get-tuple-element.78), channel_id=1, source_target_pairs={{0,16},{8,24},{16,0},{24,8},{1,17},{9,25},{17,1},{25,9},{2,18},{10... | collective-permute-start | bytes 491528 | tf_op jit(solution)/shard_map/ppermute | solution.py:543
  135.3 0.7 copy-start.8
  144.4 13.2 %all-to-all-start.5 = ((bf16[32,24,128]{2,1,0:T(8,128)(2,1)}), bf16[32,24,128]{2,1,0:T(8,128)(2,1)S(1)}, u32[]{:S(2)}, u32[]{:S(2)}) async-start(bf16[32,24,128]{2,1,0:T(8,128)(2,1)} %bitcast.86), calls=%async_computation.5 | async-start | bytes 393216 | tf_op jit(solution)/shard_map/all_to_all | solution.py:540
  157.5 0.7 copy-start.7
  182.7 11.4 %all-to-all-start.7 = ((bf16[32,24,128]{2,1,0:T(8,128)(2,1)}), bf16[32,24,128]{2,1,0:T(8,128)(2,1)S(1)}, u32[]{:S(2)}, u32[]{:S(2)}) async-start(bf16[32,24,128]{2,1,0:T(8,128)(2,1)} %bitcast.84), calls=%async_computation.7 | async-start | bytes 393216 | tf_op jit(solution)/shard_map/all_to_all | solution.py:540
  194.1 0.7 copy-start.6
  200.2 15.0 %all-to-all-start.8 = ((bf16[32,40,128]{2,1,0:T(8,128)(2,1)}), bf16[32,40,128]{2,1,0:T(8,128)(2,1)S(1)}, u32[]{:S(2)}, u32[]{:S(2)}) async-start(bf16[32,40,128]{2,1,0:T(8,128)(2,1)} %get-tuple-element.58), calls=%async_computation.8 | async-start | bytes 655360 | tf_op jit(solution)/shard_map/all_to_all | solution.py:540
  206.1 41.2 %collective-permute-start.8 = (bf16[3,768,128]{2,1,0:T(8,128)(2,1)}, bf16[3,768,128]{2,1,0:T(8,128)(2,1)}, u32[]{:S(2)}, u32[]{:S(2)}) collective-permute-start(bf16[3,768,128]{2,1,0:T(8,128)(2,1)} %get-tuple-element.67), channel_id=1, source_target_pairs={{0,24},{8,16},{16,8},{24,0},{1,25},{9,17},{17,9},{25,1},{2,26},{10... | collective-permute-start | bytes 1769480 | tf_op jit(solution)/shard_map/ppermute | solution.py:543
  208.7 49.1 %collective-permute-start.7 = (bf16[3,768,128]{2,1,0:T(8,128)(2,1)}, bf16[3,768,128]{2,1,0:T(8,128)(2,1)}, u32[]{:S(2)}, u32[]{:S(2)}) collective-permute-start(bf16[3,768,128]{2,1,0:T(8,128)(2,1)} %get-tuple-element.68), channel_id=1, source_target_pairs={{0,16},{8,24},{16,0},{24,8},{1,17},{9,25},{17,1},{25,9},{2,18},{10... | collective-permute-start | bytes 1769480 | tf_op jit(solution)/shard_map/ppermute | solution.py:543
  209.3 48.6 %collective-permute-start.6 = (bf16[3,768,128]{2,1,0:T(8,128)(2,1)}, bf16[3,768,128]{2,1,0:T(8,128)(2,1)}, u32[]{:S(2)}, u32[]{:S(2)}) collective-permute-start(bf16[3,768,128]{2,1,0:T(8,128)(2,1)} %get-tuple-element.69), channel_id=1, source_target_pairs={{0,8},{8,0},{16,24},{24,16},{1,9},{9,1},{17,25},{25,17},{2,10},{10... | collective-permute-start | bytes 1769480 | tf_op jit(solution)/shard_map/ppermute | solution.py:543
  215.2 0.7 copy-start.3
  224.4 20.3 %all-to-all-start.9 = ((bf16[8,112,128]{2,1,0:T(8,128)(2,1)}), bf16[8,112,128]{2,1,0:T(8,128)(2,1)S(1)}, u32[]{:S(2)}, u32[]{:S(2)}) async-start(bf16[8,112,128]{2,1,0:T(8,128)(2,1)} %get-tuple-element.59), calls=%async_computation.9 | async-start | bytes 458752 | tf_op jit(solution)/shard_map/all_to_all | solution.py:767
  228.9 10.3 %collective-permute-start.14 = (bf16[3,128,128]{2,1,0:T(8,128)(2,1)S(1)}, bf16[3,128,128]{2,1,0:T(8,128)(2,1)S(1)}, u32[]{:S(2)}, u32[]{:S(2)}) collective-permute-start(bf16[3,128,128]{2,1,0:T(8,128)(2,1)S(1)} %get-tuple-element.80), channel_id=1, source_target_pairs={{0,24},{8,16},{16,8},{24,0},{1,25},{9,17},{17,9},{25,1},{2,26},{10... | collective-permute-start | bytes 294920 | tf_op jit(solution)/shard_map/ppermute | solution.py:543
  229.4 12.1 %collective-permute-start.13 = (bf16[3,128,128]{2,1,0:T(8,128)(2,1)S(1)}, bf16[3,128,128]{2,1,0:T(8,128)(2,1)S(1)}, u32[]{:S(2)}, u32[]{:S(2)}) collective-permute-start(bf16[3,128,128]{2,1,0:T(8,128)(2,1)S(1)} %get-tuple-element.81), channel_id=1, source_target_pairs={{0,16},{8,24},{16,0},{24,8},{1,17},{9,25},{17,1},{25,9},{2,18},{10... | collective-permute-start | bytes 294920 | tf_op jit(solution)/shard_map/ppermute | solution.py:543
  239.2 4.6 %collective-permute-start.12 = (bf16[3,128,128]{2,1,0:T(8,128)(2,1)S(1)}, bf16[3,128,128]{2,1,0:T(8,128)(2,1)S(1)}, u32[]{:S(2)}, u32[]{:S(2)}) collective-permute-start(bf16[3,128,128]{2,1,0:T(8,128)(2,1)S(1)} %get-tuple-element.82), channel_id=1, source_target_pairs={{0,8},{8,0},{16,24},{24,16},{1,9},{9,1},{17,25},{25,17},{2,10},{10... | collective-permute-start | bytes 294920 | tf_op jit(solution)/shard_map/ppermute | solution.py:543
  244.7 12.6 %copy-start.4 = (bf16[8,112,128]{2,1,0:T(8,128)(2,1)}, bf16[8,112,128]{2,1,0:T(8,128)(2,1)S(1)}, u32[]{:S(2)}) copy-start(bf16[8,112,128]{2,1,0:T(8,128)(2,1)S(1)} %all-to-all-done.9.refs_4_) | copy-start | bytes 688132
  244.7 13.2 %collective-permute-start.11 = (bf16[8,112,128]{2,1,0:T(8,128)(2,1)S(1)}, bf16[8,112,128]{2,1,0:T(8,128)(2,1)S(1)}, u32[]{:S(2)}, u32[]{:S(2)}) collective-permute-start(bf16[8,112,128]{2,1,0:T(8,128)(2,1)S(1)} %all-to-all-done.9.refs_4_), channel_id=1, source_target_pairs={{24,0},{25,1},{26,2},{27,3},{28,4},{29,5},{30,6},{31,7}} | collective-permute-start | bytes 688136 | tf_op jit(solution)/shard_map/ppermute | solution.py:795
  245.9 12.4 %collective-permute-start.10 = (bf16[8,112,128]{2,1,0:T(8,128)(2,1)S(1)}, bf16[8,112,128]{2,1,0:T(8,128)(2,1)S(1)}, u32[]{:S(2)}, u32[]{:S(2)}) collective-permute-start(bf16[8,112,128]{2,1,0:T(8,128)(2,1)S(1)} %all-to-all-done.9.refs_4_), channel_id=1, source_target_pairs={{16,0},{17,1},{18,2},{19,3},{20,4},{21,5},{22,6},{23,7}} | collective-permute-start | bytes 688136 | tf_op jit(solution)/shard_map/ppermute | solution.py:795
  247.3 11.1 %collective-permute-start.9 = (bf16[8,112,128]{2,1,0:T(8,128)(2,1)S(1)}, bf16[8,112,128]{2,1,0:T(8,128)(2,1)}, u32[]{:S(2)}, u32[]{:S(2)}) collective-permute-start(bf16[8,112,128]{2,1,0:T(8,128)(2,1)S(1)} %all-to-all-done.9.refs_4_), channel_id=1, source_target_pairs={{8,0},{9,1},{10,2},{11,3},{12,4},{13,5},{14,6},{15,7}} | collective-permute-start | bytes 688136 | tf_op jit(solution)/shard_map/ppermute | solution.py:795
  257.9 0.7 copy-start.12
  258.4 0.7 copy-start.13

commit v6 on v5

--- a/solution.py
+++ b/solution.py
@@ -276,7 +276,8 @@
     r, w, tile, carried, slope_ref, state_ref, low_ref
 ):
     low = (carried.astype(F32) * slope_ref[r, w : w + tile, :]).astype(BF16)
-    low_ref[r, w : w + tile, :] = low
+    if low_ref is not None:
+        low_ref[r, w : w + tile, :] = low
     term = dot(state_ref[0, r, w : w + tile, :], low, ((0,), (0,)))
     return low, term
 
@@ -336,10 +337,10 @@
     mix_ref,
     acc_in_ref,
     grad_ref,
-    low_ref,
-    send_ref,
-    acc_ref,
+    *refs,
 ):
+    low_ref = None if last else refs[0]
+    send_ref, acc_ref = refs[-2:]
     rows, cells, channels = prev_ref.shape
     carried_ref = carried_ref.at[0]
     here = grad_ref.at[1 if last else 0]
@@ -705,9 +706,10 @@
         carried_at = 0 if first else s + 1
         span = 2 if last else 1
         grad_at = 0 if last else s
-        store, low, send, acc = call(
+        outs = turn_outs[1:] if last else turn_outs
+        store, *results = call(
             functools.partial(turn_kernel, packed, devices, row_devs, last),
-            [jax.ShapeDtypeStruct(store_shape, BF16)] + turn_outs,
+            [jax.ShapeDtypeStruct(store_shape, BF16)] + outs,
             [
                 whole(got.shape),
                 pl.BlockSpec(field_block, functools.partial(lambda n, *_: (n, 0, 0, 0), carried_at)),
@@ -725,12 +727,13 @@
                     (span,) + shape3, functools.partial(lambda n, *_: (n, 0, 0, 0), grad_at)
                 )
             ]
-            + [whole(o.shape) for o in turn_outs],
+            + [whole(o.shape) for o in outs],
             prefetch=sec,
             aliases={} if first else {2: 0},
             flops=4 * total * cells * rows * channels,
             moved=16 * rows * cells * channels,
         )
+        low, send, acc = results[0], *results[-2:]
 
     parts_of = [lax.dynamic_index_in_dim(store, section, 0, False)]
     for d in range(1, sections):

time: 265 us -> 265 us (level)
  no operation moved by 1% of the time
where the time goes in v6:
time: 265 us; the launch traced here: 264 us
  Pallas kernels  87.1 us (33%)
  waiting for transfers between devices  76.7 us (29%)
  starting transfers between devices  50 us (19%)
  blocking collectives  24.6 us (9%)
  local copies, waits for them, and re-layouts  17.5 us (7%)
  other arithmetic  7.05 us (3%)
    pallas_call x15, Pallas kernels, call(): pl.pallas_call(kernel, out_shape=outs, grid_spec=pltpu.PrefetchScalarGrid...  87.1 us
    ppermute x12, waiting for transfers between devices, share(): return lax.ppermute(piece, 'section', [(i, i ^ d) for i in range(sections)])  56.7 us
    all_to_all x7, starting transfers between devices, exchange(): return lax.all_to_all(values, ALL, 0, 0, tiled=True)  27.1 us
    all_to_all x2, blocking collectives, exchange(): return lax.all_to_all(values, ALL, 0, 0, tiled=True)  24.6 us
    all_to_all x7, waiting for transfers between devices, exchange(): return lax.all_to_all(values, ALL, 0, 0, tiled=True)  19.6 us
    ppermute x12, starting transfers between devices, share(): return lax.ppermute(piece, 'section', [(i, i ^ d) for i in range(sections)])  15.6 us
    unnamed x28, local copies, waits for them, and re-layouts  6.75 us
  transfers between devices with their start and end apart: 23, of which 12 were waited for; matrix products, arithmetic and copies ran while one was open for 7% of the time, Pallas kernels for 10%

profile of v6, /device:TPU:0, one launch (start us, length us, event | category | flops | bytes accessed | tf_op | source)
XLA Modules:
  0.0 263.8 jit_solution(13807985731335844159)
XLA Ops:
  0.6 3.4 %shard_map.148 = bf16[32,96,128]{2,1,0:T(8,128)(2,1)} custom-call(bf16[12,768,128]{2,1,0:T(8,128)(2,1)} %bitcast.73, bf16[256,768]{1,0:T(8,128)(2,1)} %constant.75.clone.basis_ref), custom_call_target="tpu_custom_call" | custom-call | flops 603979776 | bytes 4718592 | tf_op jit(solution)/shard_map/pallas_call | solution.py:482
  4.0 7.3 %all-to-all-start = ((bf16[32,96,128]{2,1,0:T(8,128)(2,1)}), bf16[32,96,128]{2,1,0:T(8,128)(2,1)S(1)}, u32[]{:S(2)}, u32[]{:S(2)}) async-start(bf16[32,96,128]{2,1,0:T(8,128)(2,1)} %shard_map.148), calls=%async_computation | async-start | bytes 1572864 | tf_op jit(solution)/shard_map/all_to_all | solution.py:541
  11.3 2.8 %dynamic-slice_bitcast_fusion.4 = (bf16[3,768,128]{2,1,0:T(8,128)(2,1)}, bf16[3,768,128]{2,1,0:T(8,128)(2,1)S(1)}, bf16[3,768,128]{2,1,0:T(8,128)(2,1)S(1)}, bf16[3,768,128]{2,1,0:T(8,128)(2,1)}) fusion(bf16[4,3,768,128]{3,2,1,0:T(8,128)(2,1)} %bitcast.74, s32[]{:T(128)S(6)} %select_n.34, s32[]{:T(128)S(6)} %select_n.32, s32[]{:T(128)S(6)} %select_n.31, ...), kind=kLoop, calls=%fused_computation.15 | loop fusion | bytes 4718608 | tf_op jit(solution)/shard_map/jit(dynamic_index_in_dim)/squeeze | solution.py:549
  14.1 1.8 collective-permute-start.1
  15.9 1.5 collective-permute-start
  17.4 18.3 %collective-permute-done.1 = bf16[3,768,128]{2,1,0:T(8,128)(2,1)S(1)} collective-permute-done((bf16[3,768,128]{2,1,0:T(8,128)(2,1)S(1)}, bf16[3,768,128]{2,1,0:T(8,128)(2,1)S(1)}, u32[]{:S(2)}, u32[]{:S(2)}) %collective-permute-start.1) | collective-permute-done | bytes 589856 | tf_op jit(solution)/shard_map/ppermute | solution.py:544
  35.6 0.8 copy-done.9
  36.5 0.9 copy-done.1
  37.3 8.7 %shard_map.149 = (bf16[4,512,128]{2,1,0:T(8,128)(2,1)}, bf16[32,96,128]{2,1,0:T(8,128)(2,1)}) custom-call(s32[1]{0:T(128)} %bitcast.sec_ref, bf16[3072,128]{1,0:T(8,128)(2,1)} %bitcast.75, bf16[512,768]{1,0:T(8,128)(2,1)} %constant.78.clone.lat_any, bf16[768,512]{1,0:T(8,128)(2,1)} %constant.80.clone.inv_any, bf16[64,16,2,128,128]{4,3,2,1,0:T(8,128)(2,1)} %all_ref.9), custom_call_target="tpu_custom_call" | custom-call | flops 67108864 | bytes 16777216 | tf_op jit(solution)/shard_map/pallas_call | solution.py:482
  46.1 4.4 %all-to-all-start.1 = ((bf16[32,96,128]{2,1,0:T(8,128)(2,1)}), bf16[32,96,128]{2,1,0:T(8,128)(2,1)S(1)}, u32[]{:S(2)}, u32[]{:S(2)}) async-start(bf16[32,96,128]{2,1,0:T(8,128)(2,1)} %get-tuple-element.36), calls=%async_computation.1 | async-start | bytes 1572864 | tf_op jit(solution)/shard_map/all_to_all | solution.py:541
  50.5 2.7 %collective-permute-start.2 = (bf16[3,768,128]{2,1,0:T(8,128)(2,1)}, bf16[3,768,128]{2,1,0:T(8,128)(2,1)S(1)}, u32[]{:S(2)}, u32[]{:S(2)}) collective-permute-start(bf16[3,768,128]{2,1,0:T(8,128)(2,1)} %get-tuple-element.71), channel_id=1, source_target_pairs={{0,24},{8,16},{16,8},{24,0},{1,25},{9,17},{17,9},{25,1},{2,26},{10... | collective-permute-start | bytes 1769480 | tf_op jit(solution)/shard_map/ppermute | solution.py:544
  53.3 1.9 constant_dynamic-slice_fusion.cot_ref
  55.2 2.7 %maximum_maximum_fusion = bf16[4,3,768,128]{3,2,1,0:T(8,128)(2,1)} fusion(bf16[1,3,768,128]{3,2,1,0:T(8,128)(2,1)S(1)} %bitcast.82, bf16[1,3,768,128]{3,2,1,0:T(8,128)(2,1)} %bitcast.8, bf16[1,3,768,128]{3,2,1,0:T(8,128)(2,1)S(1)} %bitcast.77, bf16[4]{0:T(256)(128)(2,1)S(1)} %pad.16.clone), kind=kLoop, calls=%fused_computation | loop fusion | flops 3538944 | bytes 4128776 | tf_op jit(solution)/shard_map/stack | solution.py:567
  58.0 18.1 %collective-permute-done.2 = bf16[3,768,128]{2,1,0:T(8,128)(2,1)S(1)} collective-permute-done((bf16[3,768,128]{2,1,0:T(8,128)(2,1)}, bf16[3,768,128]{2,1,0:T(8,128)(2,1)S(1)}, u32[]{:S(2)}, u32[]{:S(2)}) %collective-permute-start.2) | collective-permute-done | bytes 589856 | tf_op jit(solution)/shard_map/ppermute | solution.py:544
  76.1 0.9 bitcast_dynamic-update-slice_fusion.state_ref
  77.0 0.9 copy-done
  77.9 4.1 %shard_map.150 = (bf16[3,768,128]{2,1,0:T(8,128)(2,1)}, bf16[32,24,128]{2,1,0:T(8,128)(2,1)}, f32[128,128]{1,0:T(8,128)}) custom-call(s32[1]{0:T(128)} %bitcast.sec_ref, bf16[32,96,128]{2,1,0:T(8,128)(2,1)} %copy-done, bf16[3,768,128]{2,1,0:T(8,128)(2,1)} %constant_dynamic-slice_fusion.cot_ref, ...), custom_call_target="tpu_custom_call" | custom-call | flops 150994944 | bytes 2949120 | tf_op jit(solution)/shard_map/pallas_call | solution.py:482
  82.0 12.6 %all_to_all.50 = bf16[32,24,128]{2,1,0:T(8,128)(2,1)} all-to-all(bf16[32,24,128]{2,1,0:T(8,128)(2,1)} %get-tuple-element.40), channel_id=1, replica_groups=mesh['section'=4,'row'=8] {'section','row'}, dimensions={0} | all-to-all | bytes 393216 | tf_op jit(solution)/shard_map/all_to_all | solution.py:541
  94.6 8.3 %shard_map.151 = (bf16[512,128]{1,0:T(8,128)(2,1)}, bf16[768,128]{1,0:T(8,128)(2,1)}) custom-call(s32[1]{0:T(128)} %bitcast.sec_ref, bf16[768,128]{1,0:T(8,128)(2,1)} %bitcast.80, bf16[512,768]{1,0:T(8,128)(2,1)} %constant.79.clone.lat_any, bf16[768,512]{1,0:T(8,128)(2,1)} %constant.80.clone.inv_any, bf16[64,16,2,128,128]{4,3,2,1,0:T(8,128)(2,1)} %all_ref.9), custom_call_target="tpu_custom_call" | custom-call | flops 33554432 | bytes 16777216 | tf_op jit(solution)/shard_map/pallas_call | solution.py:482
  103.0 2.7 %all-to-all-start.3 = ((bf16[32,24,128]{2,1,0:T(8,128)(2,1)}), bf16[32,24,128]{2,1,0:T(8,128)(2,1)S(1)}, u32[]{:S(2)}, u32[]{:S(2)}) async-start(bf16[32,24,128]{2,1,0:T(8,128)(2,1)} %bitcast.85), calls=%async_computation.3 | async-start | bytes 393216 | tf_op jit(solution)/shard_map/all_to_all | solution.py:541
  105.7 1.9 fusion.8.carried_ref
  107.6 3.4 %shard_map.152.slope_ref = f32[3,768,128]{2,1,0:T(8,128)} custom-call(s32[1]{0:T(128)} %bitcast.sec_ref, bf16[32,96,128]{2,1,0:T(8,128)(2,1)} %copy-done, bf16[4,3,768,128]{3,2,1,0:T(8,128)(2,1)} %bitcast_dynamic-update-slice_fusion.state_ref, bf16[768,256]{1,0:T(8,128)(2,1)} %constant.77.clone.synth_t_ref.synth_ref, bf16[128,128]{1,0:T(8,128)(2,1)} %mix_ref.13, ...), custom_call_target="tpu_custom_call" | custom-call | flops 150994944 | bytes 2949120 | tf_op jit(solution)/shard_map/pallas_call | solution.py:482
  111.0 3.4 %all-to-all-done.3.recv_ref = bf16[32,24,128]{2,1,0:T(8,128)(2,1)S(1)} async-done(((bf16[32,24,128]{2,1,0:T(8,128)(2,1)}), bf16[32,24,128]{2,1,0:T(8,128)(2,1)S(1)}, u32[]{:S(2)}, u32[]{:S(2)}) %all-to-all-start.3) | async-done | bytes 196640 | tf_op jit(solution)/shard_map/all_to_all | solution.py:541
  114.4 0.7 copy-done.5
  115.1 4.1 %shard_map.153 = (bf16[4,3,768,128]{3,2,1,0:T(8,128)(2,1)}, bf16[3,768,128]{2,1,0:T(8,128)(2,1)}, bf16[32,24,128]{2,1,0:T(8,128)(2,1)}, f32[128,128]{1,0:T(8,128)}) custom-call(s32[1]{0:T(128)} %bitcast.sec_ref, bf16[32,24,128]{2,1,0:T(8,128)(2,1)} %copy-done.5, bf16[1,3,768,128]{3,2,1,0:T(8,128)(2,1)} %fusion.8.carried_ref, ...), custom_call_target="tpu_custom_call" | custom-call | flops 301989888 | bytes 4718592 | tf_op jit(solution)/shard_map/pallas_call | solution.py:482
  119.3 2.7 %all-to-all-start.4 = ((bf16[32,24,128]{2,1,0:T(8,128)(2,1)}), bf16[32,24,128]{2,1,0:T(8,128)(2,1)S(1)}, u32[]{:S(2)}, u32[]{:S(2)}) async-start(bf16[32,24,128]{2,1,0:T(8,128)(2,1)} %get-tuple-element.44), calls=%async_computation.4 | async-start | bytes 393216 | tf_op jit(solution)/shard_map/all_to_all | solution.py:541
  122.0 0.9 fusion.1
  122.9 2.7 %collective-permute-start.5 = (bf16[5,128,128]{2,1,0:T(8,128)(2,1)S(1)}, bf16[5,128,128]{2,1,0:T(8,128)(2,1)S(1)}, u32[]{:S(2)}, u32[]{:S(2)}) collective-permute-start(bf16[5,128,128]{2,1,0:T(8,128)(2,1)S(1)} %get-tuple-element.75), channel_id=1, source_target_pairs={{0,24},{8,16},{16,8},{24,0},{1,25},{9,17},{17,9},{25,1},{2,26},{10... | collective-permute-start | bytes 491528 | tf_op jit(solution)/shard_map/ppermute | solution.py:544
  126.4 5.7 %collective-permute-done.5 = bf16[5,128,128]{2,1,0:T(8,128)(2,1)S(1)} collective-permute-done((bf16[5,128,128]{2,1,0:T(8,128)(2,1)S(1)}, bf16[5,128,128]{2,1,0:T(8,128)(2,1)S(1)}, u32[]{:S(2)}, u32[]{:S(2)}) %collective-permute-start.5) | collective-permute-done | bytes 163872 | tf_op jit(solution)/shard_map/ppermute | solution.py:544
  132.1 2.9 %collective-permute-done.3 = bf16[5,128,128]{2,1,0:T(8,128)(2,1)S(1)} collective-permute-done((bf16[5,128,128]{2,1,0:T(8,128)(2,1)S(1)}, bf16[5,128,128]{2,1,0:T(8,128)(2,1)S(1)}, u32[]{:S(2)}, u32[]{:S(2)}) %collective-permute-start.3) | collective-permute-done | bytes 163872 | tf_op jit(solution)/shard_map/ppermute | solution.py:544
  135.3 0.7 copy-done.8
  136.0 8.3 %shard_map.154 = (bf16[512,128]{1,0:T(8,128)(2,1)}, bf16[768,128]{1,0:T(8,128)(2,1)}) custom-call(s32[1]{0:T(128)} %bitcast.sec_ref, bf16[768,128]{1,0:T(8,128)(2,1)} %bitcast.78, bf16[512,768]{1,0:T(8,128)(2,1)} %constant.79.clone.lat_any, bf16[768,512]{1,0:T(8,128)(2,1)} %constant.80.clone.inv_any, bf16[64,16,2,128,128]{4,3,2,1,0:T(8,128)(2,1)} %all_ref.9), custom_call_target="tpu_custom_call" | custom-call | flops 33554432 | bytes 16777216 | tf_op jit(solution)/shard_map/pallas_call | solution.py:482
  144.4 4.6 %all-to-all-start.5 = ((bf16[32,24,128]{2,1,0:T(8,128)(2,1)}), bf16[32,24,128]{2,1,0:T(8,128)(2,1)S(1)}, u32[]{:S(2)}, u32[]{:S(2)}) async-start(bf16[32,24,128]{2,1,0:T(8,128)(2,1)} %bitcast.86), calls=%async_computation.5 | async-start | bytes 393216 | tf_op jit(solution)/shard_map/all_to_all | solution.py:541
  149.0 3.4 %shard_map.155.slope_ref = f32[3,768,128]{2,1,0:T(8,128)} custom-call(s32[1]{0:T(128)} %bitcast.sec_ref, bf16[32,96,128]{2,1,0:T(8,128)(2,1)} %copy-done, bf16[4,3,768,128]{3,2,1,0:T(8,128)(2,1)} %bitcast_dynamic-update-slice_fusion.state_ref, bf16[768,256]{1,0:T(8,128)(2,1)} %constant.77.clone.synth_t_ref.synth_ref, bf16[128,128]{1,0:T(8,128)(2,1)} %mix_ref.13, ...), custom_call_target="tpu_custom_call" | custom-call | flops 150994944 | bytes 2949120 | tf_op jit(solution)/shard_map/pallas_call | solution.py:482
  152.4 5.1 %all-to-all-done.5.recv_ref = bf16[32,24,128]{2,1,0:T(8,128)(2,1)S(1)} async-done(((bf16[32,24,128]{2,1,0:T(8,128)(2,1)}), bf16[32,24,128]{2,1,0:T(8,128)(2,1)S(1)}, u32[]{:S(2)}, u32[]{:S(2)}) %all-to-all-start.5) | async-done | bytes 196640 | tf_op jit(solution)/shard_map/all_to_all | solution.py:541
  157.5 0.7 copy-done.7
  158.2 4.1 %shard_map.156 = (bf16[4,3,768,128]{3,2,1,0:T(8,128)(2,1)}, bf16[3,768,128]{2,1,0:T(8,128)(2,1)}, bf16[32,24,128]{2,1,0:T(8,128)(2,1)}, f32[128,128]{1,0:T(8,128)}) custom-call(s32[1]{0:T(128)} %bitcast.sec_ref, bf16[32,24,128]{2,1,0:T(8,128)(2,1)} %copy-done.7, ...), custom_call_target="tpu_custom_call", output_to_operand_aliasing={{0}: (2, {})} | custom-call | flops 301989888 | bytes 4718592 | tf_op jit(solution)/shard_map/pallas_call | solution.py:482
  162.3 12.0 %all_to_all.51 = bf16[32,24,128]{2,1,0:T(8,128)(2,1)} all-to-all(bf16[32,24,128]{2,1,0:T(8,128)(2,1)} %get-tuple-element.52), channel_id=1, replica_groups=mesh['section'=4,'row'=8] {'section','row'}, dimensions={0} | all-to-all | bytes 393216 | tf_op jit(solution)/shard_map/all_to_all | solution.py:541
  174.3 8.4 %shard_map.157 = (bf16[512,128]{1,0:T(8,128)(2,1)}, bf16[768,128]{1,0:T(8,128)(2,1)}) custom-call(s32[1]{0:T(128)} %bitcast.sec_ref, bf16[768,128]{1,0:T(8,128)(2,1)} %bitcast.79, bf16[512,768]{1,0:T(8,128)(2,1)} %constant.79.clone.lat_any, bf16[768,512]{1,0:T(8,128)(2,1)} %constant.80.clone.inv_any, bf16[64,16,2,128,128]{4,3,2,1,0:T(8,128)(2,1)} %all_ref.9), custom_call_target="tpu_custom_call" | custom-call | flops 33554432 | bytes 16777216 | tf_op jit(solution)/shard_map/pallas_call | solution.py:482
  182.7 2.6 all-to-all-start.7
  185.3 3.4 %shard_map.158.slope_ref = f32[3,768,128]{2,1,0:T(8,128)} custom-call(s32[1]{0:T(128)} %bitcast.sec_ref, bf16[32,96,128]{2,1,0:T(8,128)(2,1)} %copy-done, bf16[4,3,768,128]{3,2,1,0:T(8,128)(2,1)} %bitcast_dynamic-update-slice_fusion.state_ref, bf16[768,256]{1,0:T(8,128)(2,1)} %constant.77.clone.synth_t_ref.synth_ref, bf16[128,128]{1,0:T(8,128)(2,1)} %mix_ref.13, ...), custom_call_target="tpu_custom_call" | custom-call | flops 150994944 | bytes 2949120 | tf_op jit(solution)/shard_map/pallas_call | solution.py:482
  188.7 5.3 %all-to-all-done.7.recv_ref = bf16[32,24,128]{2,1,0:T(8,128)(2,1)S(1)} async-done(((bf16[32,24,128]{2,1,0:T(8,128)(2,1)}), bf16[32,24,128]{2,1,0:T(8,128)(2,1)S(1)}, u32[]{:S(2)}, u32[]{:S(2)}) %all-to-all-start.7) | async-done | bytes 196640 | tf_op jit(solution)/shard_map/all_to_all | solution.py:541
  194.1 0.7 copy-done.6
  194.7 5.4 %shard_map.159 = (bf16[4,3,768,128]{3,2,1,0:T(8,128)(2,1)}, bf16[32,40,128]{2,1,0:T(8,128)(2,1)}, f32[128,128]{1,0:T(8,128)}) custom-call(s32[1]{0:T(128)} %bitcast.sec_ref, bf16[32,24,128]{2,1,0:T(8,128)(2,1)} %copy-done.6, bf16[4,3,768,128]{3,2,1,0:T(8,128)(2,1)} %get-tuple-element.54.carried_ref, ...), custom_call_target="tpu_custom_call", output_to_operand_aliasing={{0}: (2, {})} | custom-call | flops 301989888 | bytes 4718592 | tf_op jit(solution)/shard_map/pallas_call | solution.py:482
  200.1 2.7 %all-to-all-start.8 = ((bf16[32,40,128]{2,1,0:T(8,128)(2,1)}), bf16[32,40,128]{2,1,0:T(8,128)(2,1)S(1)}, u32[]{:S(2)}, u32[]{:S(2)}) async-start(bf16[32,40,128]{2,1,0:T(8,128)(2,1)} %get-tuple-element.58), calls=%async_computation.8 | async-start | bytes 655360 | tf_op jit(solution)/shard_map/all_to_all | solution.py:541
  202.9 3.1 %dynamic-slice_bitcast_fusion = (bf16[3,768,128]{2,1,0:T(8,128)(2,1)}, bf16[3,768,128]{2,1,0:T(8,128)(2,1)}, bf16[3,768,128]{2,1,0:T(8,128)(2,1)}, bf16[3,768,128]{2,1,0:T(8,128)(2,1)}) fusion(bf16[4,3,768,128]{3,2,1,0:T(8,128)(2,1)} %get-tuple-element.57, s32[]{:T(128)S(6)} %select_n.34, s32[]{:T(128)S(6)} %select_n.32, s32[]{:T(128)S(6)} %select_n.31, ...), kind=kLoop, calls=%fused_computation.11 | loop fusion | bytes 4718608 | tf_op jit(solution)/shard_map/jit(dynamic_index_in_dim)/squeeze | solution.py:740
  206.0 2.7 %collective-permute-start.8 = (bf16[3,768,128]{2,1,0:T(8,128)(2,1)}, bf16[3,768,128]{2,1,0:T(8,128)(2,1)}, u32[]{:S(2)}, u32[]{:S(2)}) collective-permute-start(bf16[3,768,128]{2,1,0:T(8,128)(2,1)} %get-tuple-element.67), channel_id=1, source_target_pairs={{0,24},{8,16},{16,8},{24,0},{1,25},{9,17},{17,9},{25,1},{2,26},{10... | collective-permute-start | bytes 1769480 | tf_op jit(solution)/shard_map/ppermute | solution.py:544
  209.5 5.7 %all-to-all-done.8.x_any = bf16[32,40,128]{2,1,0:T(8,128)(2,1)S(1)} async-done(((bf16[32,40,128]{2,1,0:T(8,128)(2,1)}), bf16[32,40,128]{2,1,0:T(8,128)(2,1)S(1)}, u32[]{:S(2)}, u32[]{:S(2)}) %all-to-all-start.8) | async-done | bytes 327712 | tf_op jit(solution)/shard_map/all_to_all | solution.py:541
  215.1 0.7 copy-done.3
  215.9 8.4 %shard_map.160 = (bf16[512,128]{1,0:T(8,128)(2,1)}, bf16[8,112,128]{2,1,0:T(8,128)(2,1)}) custom-call(s32[1]{0:T(128)} %bitcast.sec_ref, bf16[32,40,128]{2,1,0:T(8,128)(2,1)} %copy-done.3, bf16[512,768]{1,0:T(8,128)(2,1)} %constant.79.clone.lat_any, bf16[768,512]{1,0:T(8,128)(2,1)} %constant.81.clone.inv_any, bf16[64,16,2,128,128]{4,3,2,1,0:T(8,128)(2,1)} %all_ref.9), custom_call_target="tpu_custom_call" | custom-call | flops 33554432 | bytes 16777216 | tf_op jit(solution)/shard_map/pallas_call | solution.py:482
  224.3 3.4 %all-to-all-start.9 = ((bf16[8,112,128]{2,1,0:T(8,128)(2,1)}), bf16[8,112,128]{2,1,0:T(8,128)(2,1)S(1)}, u32[]{:S(2)}, u32[]{:S(2)}) async-start(bf16[8,112,128]{2,1,0:T(8,128)(2,1)} %get-tuple-element.59), calls=%async_computation.9 | async-start | bytes 458752 | tf_op jit(solution)/shard_map/all_to_all | solution.py:770
  227.7 1.1 pad_maximum_fusion.1
  229.3 0.7 collective-permute-start.13
  230.0 9.1 %collective-permute-done.14 = bf16[3,128,128]{2,1,0:T(8,128)(2,1)S(1)} collective-permute-done((bf16[3,128,128]{2,1,0:T(8,128)(2,1)S(1)}, bf16[3,128,128]{2,1,0:T(8,128)(2,1)S(1)}, u32[]{:S(2)}, u32[]{:S(2)}) %collective-permute-start.14) | collective-permute-done | bytes 98336 | tf_op jit(solution)/shard_map/ppermute | solution.py:544
  239.1 1.4 collective-permute-start.12
  240.5 0.9 pad_maximum_fusion.first_ref
  241.5 2.3 collective-permute-done.12
  243.8 0.8 pad_maximum_fusion.2.late_ref
  244.6 1.3 collective-permute-start.11
  245.8 1.3 collective-permute-start.10
  247.2 1.3 collective-permute-start.9
  248.5 8.7 %shard_map.162 = bf16[16,16,2,128,128]{4,3,2,1,0:T(8,128)(2,1)} custom-call(s32[1]{0:T(128)} %bitcast.sec_ref, bf16[4,5,128,128]{3,2,1,0:T(8,128)(2,1)} %pad_maximum_fusion.first_ref, bf16[4,3,128,128]{3,2,1,0:T(8,128)(2,1)} %pad_maximum_fusion.2.late_ref), custom_call_target="tpu_custom_call" | custom-call | flops 134217728 | bytes 16777216 | tf_op jit(solution)/shard_map/pallas_call | solution.py:482
  257.1 0.6 convert_multiply_fusion
  259.0 4.8 %shard_map.161 = bf16[12,768,128]{2,1,0:T(8,128)(2,1)} custom-call(s32[1]{0:T(128)} %bitcast.sec_ref, bf16[3,768,128]{2,1,0:T(8,128)(2,1)} %get-tuple-element.70.refs_0_, bf16[3,768,128]{2,1,0:T(8,128)(2,1)} %collective-permute-done.6.refs_1_, bf16[3,768,128]{2,1,0:T(8,128)(2,1)} %collective-permute-done.7.refs_2_, ...), custom_call_target="tpu_custom_call" | custom-call | flops 603979776 | bytes 9437184 | tf_op jit(solution)/shard_map/pallas_call | solution.py:482
  (40 shorter events, 3.8 us)
Async XLA Ops:
  4.0 32.4 %all-to-all-start = ((bf16[32,96,128]{2,1,0:T(8,128)(2,1)}), bf16[32,96,128]{2,1,0:T(8,128)(2,1)S(1)}, u32[]{:S(2)}, u32[]{:S(2)}) async-start(bf16[32,96,128]{2,1,0:T(8,128)(2,1)} %shard_map.148), calls=%async_computation | async-start | bytes 1572864 | tf_op jit(solution)/shard_map/all_to_all | solution.py:541
  14.1 21.5 %collective-permute-start.1 = (bf16[3,768,128]{2,1,0:T(8,128)(2,1)S(1)}, bf16[3,768,128]{2,1,0:T(8,128)(2,1)S(1)}, u32[]{:S(2)}, u32[]{:S(2)}) collective-permute-start(bf16[3,768,128]{2,1,0:T(8,128)(2,1)S(1)} %get-tuple-element.72), channel_id=1, source_target_pairs={{0,16},{8,24},{16,0},{24,8},{1,17},{9,25},{17,1},{25,9},{2,18},{10... | collective-permute-start | bytes 1769480 | tf_op jit(solution)/shard_map/ppermute | solution.py:544
  15.9 20.6 %collective-permute-start = (bf16[3,768,128]{2,1,0:T(8,128)(2,1)S(1)}, bf16[3,768,128]{2,1,0:T(8,128)(2,1)}, u32[]{:S(2)}, u32[]{:S(2)}) collective-permute-start(bf16[3,768,128]{2,1,0:T(8,128)(2,1)S(1)} %get-tuple-element.73), channel_id=1, source_target_pairs={{0,8},{8,0},{16,24},{24,16},{1,9},{9,1},{17,25},{25,17},{2,10},{10... | collective-permute-start | bytes 1769480 | tf_op jit(solution)/shard_map/ppermute | solution.py:544
  35.6 0.8 copy-start.9
  36.4 0.9 copy-start.1
  46.0 9.2 %copy-start.2 = (bf16[3,768,128]{2,1,0:T(8,128)(2,1)S(1)}, bf16[3,768,128]{2,1,0:T(8,128)(2,1)}, u32[]{:S(2)}) copy-start(bf16[3,768,128]{2,1,0:T(8,128)(2,1)} %get-tuple-element.37) | copy-start | bytes 1769476
  46.1 9.2 %copy-start.10 = (bf16[3,768,128]{2,1,0:T(8,128)(2,1)S(1)}, bf16[3,768,128]{2,1,0:T(8,128)(2,1)}, u32[]{:S(2)}) copy-start(bf16[3,768,128]{2,1,0:T(8,128)(2,1)} %copy-done.9) | copy-start | bytes 1769476
  46.1 30.9 %all-to-all-start.1 = ((bf16[32,96,128]{2,1,0:T(8,128)(2,1)}), bf16[32,96,128]{2,1,0:T(8,128)(2,1)S(1)}, u32[]{:S(2)}, u32[]{:S(2)}) async-start(bf16[32,96,128]{2,1,0:T(8,128)(2,1)} %get-tuple-element.36), calls=%async_computation.1 | async-start | bytes 1572864 | tf_op jit(solution)/shard_map/all_to_all | solution.py:541
  50.5 25.6 %collective-permute-start.2 = (bf16[3,768,128]{2,1,0:T(8,128)(2,1)}, bf16[3,768,128]{2,1,0:T(8,128)(2,1)S(1)}, u32[]{:S(2)}, u32[]{:S(2)}) collective-permute-start(bf16[3,768,128]{2,1,0:T(8,128)(2,1)} %get-tuple-element.71), channel_id=1, source_target_pairs={{0,24},{8,16},{16,8},{24,0},{1,25},{9,17},{17,9},{25,1},{2,26},{10... | collective-permute-start | bytes 1769480 | tf_op jit(solution)/shard_map/ppermute | solution.py:544
  77.0 0.9 copy-start
  103.0 11.5 %all-to-all-start.3 = ((bf16[32,24,128]{2,1,0:T(8,128)(2,1)}), bf16[32,24,128]{2,1,0:T(8,128)(2,1)S(1)}, u32[]{:S(2)}, u32[]{:S(2)}) async-start(bf16[32,24,128]{2,1,0:T(8,128)(2,1)} %bitcast.85), calls=%async_computation.3 | async-start | bytes 393216 | tf_op jit(solution)/shard_map/all_to_all | solution.py:541
  114.4 0.7 copy-start.5
  115.1 6.9 %copy-start.11 = (bf16[4,512,128]{2,1,0:T(8,128)(2,1)S(1)}, bf16[4,512,128]{2,1,0:T(8,128)(2,1)}, u32[]{:S(2)}) copy-start(bf16[4,512,128]{2,1,0:T(8,128)(2,1)} %get-tuple-element.45) | copy-start | bytes 1572868
  119.3 16.1 %all-to-all-start.4 = ((bf16[32,24,128]{2,1,0:T(8,128)(2,1)}), bf16[32,24,128]{2,1,0:T(8,128)(2,1)S(1)}, u32[]{:S(2)}, u32[]{:S(2)}) async-start(bf16[32,24,128]{2,1,0:T(8,128)(2,1)} %get-tuple-element.44), calls=%async_computation.4 | async-start | bytes 393216 | tf_op jit(solution)/shard_map/all_to_all | solution.py:541
  122.9 9.3 %collective-permute-start.5 = (bf16[5,128,128]{2,1,0:T(8,128)(2,1)S(1)}, bf16[5,128,128]{2,1,0:T(8,128)(2,1)S(1)}, u32[]{:S(2)}, u32[]{:S(2)}) collective-permute-start(bf16[5,128,128]{2,1,0:T(8,128)(2,1)S(1)} %get-tuple-element.75), channel_id=1, source_target_pairs={{0,24},{8,16},{16,8},{24,0},{1,25},{9,17},{17,9},{25,1},{2,26},{10... | collective-permute-start | bytes 491528 | tf_op jit(solution)/shard_map/ppermute | solution.py:544
  125.6 9.4 %collective-permute-start.3 = (bf16[5,128,128]{2,1,0:T(8,128)(2,1)S(1)}, bf16[5,128,128]{2,1,0:T(8,128)(2,1)S(1)}, u32[]{:S(2)}, u32[]{:S(2)}) collective-permute-start(bf16[5,128,128]{2,1,0:T(8,128)(2,1)S(1)} %get-tuple-element.77), channel_id=1, source_target_pairs={{0,8},{8,0},{16,24},{24,16},{1,9},{9,1},{17,25},{25,17},{2,10},{10... | collective-permute-start | bytes 491528 | tf_op jit(solution)/shard_map/ppermute | solution.py:544
  126.2 9.2 %collective-permute-start.4 = (bf16[5,128,128]{2,1,0:T(8,128)(2,1)S(1)}, bf16[5,128,128]{2,1,0:T(8,128)(2,1)S(1)}, u32[]{:S(2)}, u32[]{:S(2)}) collective-permute-start(bf16[5,128,128]{2,1,0:T(8,128)(2,1)S(1)} %get-tuple-element.78), channel_id=1, source_target_pairs={{0,16},{8,24},{16,0},{24,8},{1,17},{9,25},{17,1},{25,9},{2,18},{10... | collective-permute-start | bytes 491528 | tf_op jit(solution)/shard_map/ppermute | solution.py:544
  135.3 0.7 copy-start.8
  144.4 13.2 %all-to-all-start.5 = ((bf16[32,24,128]{2,1,0:T(8,128)(2,1)}), bf16[32,24,128]{2,1,0:T(8,128)(2,1)S(1)}, u32[]{:S(2)}, u32[]{:S(2)}) async-start(bf16[32,24,128]{2,1,0:T(8,128)(2,1)} %bitcast.86), calls=%async_computation.5 | async-start | bytes 393216 | tf_op jit(solution)/shard_map/all_to_all | solution.py:541
  157.5 0.7 copy-start.7
  182.7 11.4 %all-to-all-start.7 = ((bf16[32,24,128]{2,1,0:T(8,128)(2,1)}), bf16[32,24,128]{2,1,0:T(8,128)(2,1)S(1)}, u32[]{:S(2)}, u32[]{:S(2)}) async-start(bf16[32,24,128]{2,1,0:T(8,128)(2,1)} %bitcast.84), calls=%async_computation.7 | async-start | bytes 393216 | tf_op jit(solution)/shard_map/all_to_all | solution.py:541
  194.1 0.7 copy-start.6
  200.1 15.0 %all-to-all-start.8 = ((bf16[32,40,128]{2,1,0:T(8,128)(2,1)}), bf16[32,40,128]{2,1,0:T(8,128)(2,1)S(1)}, u32[]{:S(2)}, u32[]{:S(2)}) async-start(bf16[32,40,128]{2,1,0:T(8,128)(2,1)} %get-tuple-element.58), calls=%async_computation.8 | async-start | bytes 655360 | tf_op jit(solution)/shard_map/all_to_all | solution.py:541
  206.0 41.2 %collective-permute-start.8 = (bf16[3,768,128]{2,1,0:T(8,128)(2,1)}, bf16[3,768,128]{2,1,0:T(8,128)(2,1)}, u32[]{:S(2)}, u32[]{:S(2)}) collective-permute-start(bf16[3,768,128]{2,1,0:T(8,128)(2,1)} %get-tuple-element.67), channel_id=1, source_target_pairs={{0,24},{8,16},{16,8},{24,0},{1,25},{9,17},{17,9},{25,1},{2,26},{10... | collective-permute-start | bytes 1769480 | tf_op jit(solution)/shard_map/ppermute | solution.py:544
  208.6 49.1 %collective-permute-start.7 = (bf16[3,768,128]{2,1,0:T(8,128)(2,1)}, bf16[3,768,128]{2,1,0:T(8,128)(2,1)}, u32[]{:S(2)}, u32[]{:S(2)}) collective-permute-start(bf16[3,768,128]{2,1,0:T(8,128)(2,1)} %get-tuple-element.68), channel_id=1, source_target_pairs={{0,16},{8,24},{16,0},{24,8},{1,17},{9,25},{17,1},{25,9},{2,18},{10... | collective-permute-start | bytes 1769480 | tf_op jit(solution)/shard_map/ppermute | solution.py:544
  209.2 48.6 %collective-permute-start.6 = (bf16[3,768,128]{2,1,0:T(8,128)(2,1)}, bf16[3,768,128]{2,1,0:T(8,128)(2,1)}, u32[]{:S(2)}, u32[]{:S(2)}) collective-permute-start(bf16[3,768,128]{2,1,0:T(8,128)(2,1)} %get-tuple-element.69), channel_id=1, source_target_pairs={{0,8},{8,0},{16,24},{24,16},{1,9},{9,1},{17,25},{25,17},{2,10},{10... | collective-permute-start | bytes 1769480 | tf_op jit(solution)/shard_map/ppermute | solution.py:544
  215.1 0.7 copy-start.3
  224.3 20.3 %all-to-all-start.9 = ((bf16[8,112,128]{2,1,0:T(8,128)(2,1)}), bf16[8,112,128]{2,1,0:T(8,128)(2,1)S(1)}, u32[]{:S(2)}, u32[]{:S(2)}) async-start(bf16[8,112,128]{2,1,0:T(8,128)(2,1)} %get-tuple-element.59), calls=%async_computation.9 | async-start | bytes 458752 | tf_op jit(solution)/shard_map/all_to_all | solution.py:770
  228.9 10.3 %collective-permute-start.14 = (bf16[3,128,128]{2,1,0:T(8,128)(2,1)S(1)}, bf16[3,128,128]{2,1,0:T(8,128)(2,1)S(1)}, u32[]{:S(2)}, u32[]{:S(2)}) collective-permute-start(bf16[3,128,128]{2,1,0:T(8,128)(2,1)S(1)} %get-tuple-element.80), channel_id=1, source_target_pairs={{0,24},{8,16},{16,8},{24,0},{1,25},{9,17},{17,9},{25,1},{2,26},{10... | collective-permute-start | bytes 294920 | tf_op jit(solution)/shard_map/ppermute | solution.py:544
  229.3 12.1 %collective-permute-start.13 = (bf16[3,128,128]{2,1,0:T(8,128)(2,1)S(1)}, bf16[3,128,128]{2,1,0:T(8,128)(2,1)S(1)}, u32[]{:S(2)}, u32[]{:S(2)}) collective-permute-start(bf16[3,128,128]{2,1,0:T(8,128)(2,1)S(1)} %get-tuple-element.81), channel_id=1, source_target_pairs={{0,16},{8,24},{16,0},{24,8},{1,17},{9,25},{17,1},{25,9},{2,18},{10... | collective-permute-start | bytes 294920 | tf_op jit(solution)/shard_map/ppermute | solution.py:544
  239.1 4.6 %collective-permute-start.12 = (bf16[3,128,128]{2,1,0:T(8,128)(2,1)S(1)}, bf16[3,128,128]{2,1,0:T(8,128)(2,1)S(1)}, u32[]{:S(2)}, u32[]{:S(2)}) collective-permute-start(bf16[3,128,128]{2,1,0:T(8,128)(2,1)S(1)} %get-tuple-element.82), channel_id=1, source_target_pairs={{0,8},{8,0},{16,24},{24,16},{1,9},{9,1},{17,25},{25,17},{2,10},{10... | collective-permute-start | bytes 294920 | tf_op jit(solution)/shard_map/ppermute | solution.py:544
  244.6 12.6 %copy-start.4 = (bf16[8,112,128]{2,1,0:T(8,128)(2,1)}, bf16[8,112,128]{2,1,0:T(8,128)(2,1)S(1)}, u32[]{:S(2)}) copy-start(bf16[8,112,128]{2,1,0:T(8,128)(2,1)S(1)} %all-to-all-done.9.refs_4_) | copy-start | bytes 688132
  244.6 13.2 %collective-permute-start.11 = (bf16[8,112,128]{2,1,0:T(8,128)(2,1)S(1)}, bf16[8,112,128]{2,1,0:T(8,128)(2,1)S(1)}, u32[]{:S(2)}, u32[]{:S(2)}) collective-permute-start(bf16[8,112,128]{2,1,0:T(8,128)(2,1)S(1)} %all-to-all-done.9.refs_4_), channel_id=1, source_target_pairs={{24,0},{25,1},{26,2},{27,3},{28,4},{29,5},{30,6},{31,7}} | collective-permute-start | bytes 688136 | tf_op jit(solution)/shard_map/ppermute | solution.py:798
  245.8 12.4 %collective-permute-start.10 = (bf16[8,112,128]{2,1,0:T(8,128)(2,1)S(1)}, bf16[8,112,128]{2,1,0:T(8,128)(2,1)S(1)}, u32[]{:S(2)}, u32[]{:S(2)}) collective-permute-start(bf16[8,112,128]{2,1,0:T(8,128)(2,1)S(1)} %all-to-all-done.9.refs_4_), channel_id=1, source_target_pairs={{16,0},{17,1},{18,2},{19,3},{20,4},{21,5},{22,6},{23,7}} | collective-permute-start | bytes 688136 | tf_op jit(solution)/shard_map/ppermute | solution.py:798
  247.2 11.1 %collective-permute-start.9 = (bf16[8,112,128]{2,1,0:T(8,128)(2,1)S(1)}, bf16[8,112,128]{2,1,0:T(8,128)(2,1)}, u32[]{:S(2)}, u32[]{:S(2)}) collective-permute-start(bf16[8,112,128]{2,1,0:T(8,128)(2,1)S(1)} %all-to-all-done.9.refs_4_), channel_id=1, source_target_pairs={{8,0},{9,1},{10,2},{11,3},{12,4},{13,5},{14,6},{15,7}} | collective-permute-start | bytes 688136 | tf_op jit(solution)/shard_map/ppermute | solution.py:798
  257.8 0.7 copy-start.12
  258.3 0.7 copy-start.13
